TPU v7x, 32 devices: a whole 2x2x4 slice. The times are simulated.
32 devices in a mesh: dp: 8 (over z, y), mp: 4 (over x, core).
Axes of the slice: x: 2, y: 2, z: 4, core: 2. Of those that a mesh axis runs over, the one named last changes fastest.
Arguments:
- inputs: bfloat16 [4, 512, 1024], P(None, 'dp'), may hold values from -8 to 8
- depth_counts: int32 [512], P('dp'), may hold values from 2 to 4, as said below
- out_grad: bfloat16 [4, 512, 1024], P(None, 'dp'), may hold values from -8 to 8
- attn_weight: float32 [1024, 4, 4, 1024], P('dp', None, None, 'mp'), may hold values from -0.26516504 to 0.26516504
- attn_first: float32 [1024, 4, 4, 1024], P('dp', None, None, 'mp'), may hold values from -0.0007324219 to 0.0007324219
- attn_second: float32 [1024, 4, 4, 1024], P('dp', None, None, 'mp'), may hold values from 1.4901161e-08 to 5.9604645e-08
- ffn_weight: float32 [1024, 3, 4, 4096], P('dp', None, None, 'mp'), may hold values from -0.125 to 0.125
- ffn_first: float32 [1024, 3, 4, 4096], P('dp', None, None, 'mp'), may hold values from -0.0007324219 to 0.0007324219
- ffn_second: float32 [1024, 3, 4, 4096], P('dp', None, None, 'mp'), may hold values from 1.4901161e-08 to 5.9604645e-08
- norm_gains: float32 [2, 1024], replicated, may hold values from 0.25 to 1.75
- gain_first: float32 [2, 1024], replicated, may hold values from -0.00390625 to 0.00390625
- gain_second: float32 [2, 1024], replicated, may hold values from 3.7252903e-07 to 1.4901161e-06
Outputs:
- output: bfloat16 [4, 512, 1024], P(None, 'dp')
- input_grad: bfloat16 [4, 512, 1024], P(None, 'dp')
- grad_norm: float32 [], replicated
- attn_weight_new: float32 [1024, 4, 4, 1024], P('dp', None, None, 'mp')
- attn_first_new: float32 [1024, 4, 4, 1024], P('dp', None, None, 'mp')
- attn_second_new: float32 [1024, 4, 4, 1024], P('dp', None, None, 'mp')
- ffn_weight_new: float32 [1024, 3, 4, 4096], P('dp', None, None, 'mp')
- ffn_first_new: float32 [1024, 3, 4, 4096], P('dp', None, None, 'mp')
- ffn_second_new: float32 [1024, 3, 4, 4096], P('dp', None, None, 'mp')
- gains_new: float32 [2, 1024], replicated
- gain_first_new: float32 [2, 1024], replicated
- gain_second_new: float32 [2, 1024], replicated
Inputs may be any that keep to these rules, and one draw needn't show every extreme that they name: `depth_counts`: every count is 2 or 4; among the 64 frames of one device at most 48 have count 4, and in every draw some device has exactly 48.
All inputs are finite; a program needn't handle non-finite values.
Results may differ from a plain program's by a relative error of at most 0.012.
Values may be sent and summed in bfloat16 or wider, within the bound.
No kernel may reach another device: no remote copies, remote signals or barrier semaphores. Data moves between devices by JAX's collectives and lax.ppermute only.
A program may use at most 384 MiB of HBM per device.

v0:
```python
import functools
import math

import jax
import jax.numpy as jnp
from jax import lax
from jax.experimental import pallas as pl
from jax.experimental.pallas import tpu as pltpu
from jax.sharding import Mesh, PartitionSpec as P

HD = 64
STEP = 5
NORM_EPS = 1e-05
BETA_ONE = 0.5
BETA_TWO = 0.5
LEARN_RATE = 0.02
GAIN_RATE = 0.4
WEIGHT_DECAY = 0.1
ADAM_EPS = 1e-08
CLIP_NORM = 1.0

VMEM_LIMIT = 16 << 20

BF = jnp.bfloat16
F32 = jnp.float32


def axis_total(axes):
    return math.prod(lax.axis_size(a) for a in axes)


def linear_index(axes):
    index = 0
    for a in axes:
        index = index * lax.axis_size(a) + lax.axis_index(a)
    return index


def hop(value, axes, step):
    n = axis_total(axes)
    return lax.ppermute(value, axes, [(i, i ^ step) for i in range(n)])


def take(stack, index):
    return lax.dynamic_index_in_dim(stack, index, 0, keepdims=False)


def put(stack, value, index):
    return lax.dynamic_update_index_in_dim(stack, value, index, 0)


def gather_parts(parts, me):
    full = jnp.zeros((len(parts),) + parts[0].shape, parts[0].dtype)
    for s, part in enumerate(parts):
        full = put(full, part, me ^ s)
    return full


def all_to_all(stack, axes):
    n = axis_total(axes)
    me = linear_index(axes)
    parts = [take(stack, me)]
    for s in range(1, n):
        parts.append(hop(take(stack, me ^ s), axes, s))
    return gather_parts(parts, me)


def all_gather(value, axes):
    n = axis_total(axes)
    me = linear_index(axes)
    return gather_parts([value] + [hop(value, axes, s) for s in range(1, n)], me)


def tree_sum(parts):
    while len(parts) > 1:
        parts = [a + b for a, b in zip(parts[::2], parts[1::2])]
    return parts[0]


def all_sum(value, axes):
    n = axis_total(axes)
    return tree_sum([value] + [hop(value, axes, s) for s in range(1, n)])


CHIPS = ("rs", "mx")
CORES = ("mc",)


def rms_forward(values, gain):
    inv_rms = lax.rsqrt(jnp.mean(values * values, axis=-1, keepdims=True) + NORM_EPS)
    unit_rows = values * inv_rms
    return unit_rows, inv_rms, (unit_rows * gain).astype(BF)


def rms_backward(grad_normed, unit_rows, inv_rms, gain):
    scaled = grad_normed * gain
    return inv_rms * (scaled - unit_rows * jnp.mean(scaled * unit_rows, axis=-1, keepdims=True))


def mm(a, b):
    return jnp.dot(a, b, preferred_element_type=F32)


def mm_nt(a, b):
    return lax.dot_general(a, b, (((1,), (1,)), ((), ())), preferred_element_type=F32)


def mm_tn(a, b):
    return lax.dot_general(a, b, (((0,), (0,)), ((), ())), preferred_element_type=F32)


def head_sums(products):
    width = products.shape[-1]
    head_in = lax.broadcasted_iota(jnp.int32, (width, width), 0) // HD
    head_out = lax.broadcasted_iota(jnp.int32, (width, width), 1) // HD
    ones = jnp.where(head_in == head_out, 1.0, 0.0).astype(BF)
    high = products.astype(BF)
    low = (products - high.astype(F32)).astype(BF)
    return mm(high, ones) + mm(low, ones)


def attend(query, key, value):
    depth = len(query)
    q32, k32, v32 = ([v.astype(F32) for v in rows] for rows in (query, key, value))
    pairs = [(p, q) for p in range(depth) for q in range(p + 1)]
    rows = query[0].shape[0]
    sums = head_sums(jnp.concatenate([q32[p] * k32[q] for p, q in pairs], 0)) * HD ** (-0.5)
    scores = {pq: sums[i * rows : (i + 1) * rows] for i, pq in enumerate(pairs)}
    probs = {}
    context = []
    for p in range(depth):
        top = scores[p, 0]
        for q in range(1, p + 1):
            top = jnp.maximum(top, scores[p, q])
        terms = [jnp.exp(scores[p, q] - top) for q in range(p + 1)]
        scale = 1.0 / sum(terms[1:], terms[0])
        acc = 0.0
        for q in range(p + 1):
            probs[p, q] = terms[q] * scale
            acc = acc + probs[p, q].astype(BF).astype(F32) * v32[q]
        context.append(acc.astype(BF))
    return context, probs


def attend_back(query, key, value, probs, grad_context):
    depth = len(query)
    q32, k32, v32, g32 = ([v.astype(F32) for v in r] for r in (query, key, value, grad_context))
    pairs = [(p, q) for p in range(depth) for q in range(p + 1)]
    rows = query[0].shape[0]
    sums = head_sums(jnp.concatenate([g32[p] * v32[q] for p, q in pairs], 0))
    grad_probs = {pq: sums[i * rows : (i + 1) * rows] for i, pq in enumerate(pairs)}
    grad_scores = {}
    for p in range(depth):
        inner = sum(probs[p, q] * grad_probs[p, q] for q in range(p + 1))
        for q in range(p + 1):
            low = (probs[p, q] * (grad_probs[p, q] - inner)).astype(BF)
            grad_scores[p, q] = low.astype(F32)
    scale = HD ** (-0.5)
    grad_query, grad_key, grad_value = [], [], []
    for p in range(depth):
        later = range(p, depth)
        grad_query.append(
            (scale * sum(grad_scores[p, q] * k32[q] for q in range(p + 1))).astype(BF)
        )
        grad_key.append((scale * sum(grad_scores[o, p] * q32[o] for o in later)).astype(BF))
        grad_value.append(
            sum(probs[o, p].astype(BF).astype(F32) * g32[o] for o in later).astype(BF)
        )
    return grad_query, grad_key, grad_value


def vmem_call(kernel, outs, *args, index=None, scratch=(), flops=0, wait_for=()):
    size = sum(v.size * v.dtype.itemsize for v in args)
    size += sum(math.prod(v.shape) * v.dtype.itemsize for v in outs)
    first = () if index is None else (jnp.reshape(index, (-1,)).astype(jnp.int32),)
    specs = [pl.BlockSpec(memory_space=pltpu.SMEM)] * len(first)
    specs += [pl.BlockSpec(memory_space=pltpu.VMEM)] * len(args)
    specs += [pl.BlockSpec(memory_space=pl.ANY)] * len(wait_for)
    read = len(first) + len(args)

    def run(*refs):
        kernel(*refs[:read], *refs[read + len(wait_for) :])

    return pl.pallas_call(
        run,
        out_shape=list(outs),
        in_specs=specs,
        out_specs=[pl.BlockSpec(memory_space=pltpu.VMEM)] * len(outs),
        scratch_shapes=list(scratch),
        compiler_params=pltpu.CompilerParams(vmem_limit_bytes=VMEM_LIMIT),
        cost_estimate=pl.CostEstimate(flops=flops, bytes_accessed=size, transcendentals=0),
        name=getattr(kernel, "func", kernel).__name__,
    )(*first, *args, *wait_for)


def sds(shape, dtype):
    return jax.ShapeDtypeStruct(shape, dtype)


def pass_kernel(*refs):
    pass


def after(value, *others):
    anywhere = pl.BlockSpec(memory_space=pl.ANY)
    return pl.pallas_call(
        pass_kernel,
        out_shape=sds(value.shape, value.dtype),
        in_specs=[anywhere] * (1 + len(others)),
        out_specs=anywhere,
        input_output_aliases={0: 0},
        name="after",
    )(value, *others)


def swap_parts(parts, axes):
    return [parts[0]] + [hop(part, axes, t) for t, part in enumerate(parts) if t]


def stack_kernel(*refs):
    at = 0
    for ref in refs[:-1]:
        rows = ref.shape[0]
        refs[-1][at : at + rows, :] = ref[...]
        at += rows


def stack_rows(parts):
    shape = (sum(p.shape[0] for p in parts), parts[0].shape[1])
    return vmem_call(stack_kernel, [sds(shape, parts[0].dtype)], *parts)[0]


def gather_pieces(rows):
    near = [rows] + [hop(rows, CHIPS, t) for t in range(1, axis_total(CHIPS))]
    return near + [hop(stack_rows(near), CORES, 1)]


def pair_kernel(near_ref, far_ref, *out_refs):
    rows = out_refs[0].shape[0]
    for t, ref in enumerate(out_refs):
        at = slice(t * rows, (t + 1) * rows)
        ref[...] = (near_ref[at, :].astype(F32) + far_ref[at, :].astype(F32)).astype(BF)


def scatter_pieces(near, far):
    chips = axis_total(CHIPS)
    got = hop(far, CORES, 1)
    rows = near.shape[0] // chips
    pair = vmem_call(pair_kernel, [sds((rows, near.shape[1]), BF)] * chips, near, got)
    return swap_parts(pair, CHIPS)


def sum_refs(refs):
    return tree_sum([ref[...].astype(F32) for ref in refs])


def pack_rows(inputs, out_grad, depth_counts, me, mine, share):
    depth = inputs.shape[0]
    counts = lax.dynamic_slice_in_dim(depth_counts, mine * share, share, 0)
    live = (jnp.arange(depth)[:, None] < counts[None, :]).astype(BF)
    live = jnp.broadcast_to(live[:, None, :, None], (depth, 2, share, 128))
    rows = [lax.dynamic_slice_in_dim(v, mine * share, share, 1) for v in (inputs, out_grad)]
    sent = jnp.concatenate([jnp.stack(rows, 1), live], -1)
    return [take(sent, me ^ t) for t in range(depth)]


def unpack_kernel(depth, me_ref, *refs):
    got = refs[:depth]
    gain_ref, rows_ref, grad_ref, mask_ref, normed_ref, masked_ref = refs[depth:]
    share, wide = got[0].shape[1:]
    model = rows_ref.shape[1]
    for t in range(depth):
        at = pl.ds(pl.multiple_of((me_ref[0] ^ t) * share, share), share)
        rows_ref[at, :] = got[t][0, :, :model].astype(F32)
        grad_ref[at, :] = got[t][1, :, :model].astype(F32)
        mask_ref[at, :] = got[t][0, :, model:].astype(F32)
    normed_ref[...] = rms_forward(rows_ref[...], gain_ref[...])[2]
    masked_ref[...] = (mask_ref[:, :1] * grad_ref[...]).astype(BF)


def unpack_rows(got, gain, me):
    depth = len(got)
    share, wide = got[0].shape[1:]
    shape = (depth * share, wide - 128)
    return vmem_call(
        functools.partial(unpack_kernel, depth),
        [sds(shape, F32), sds(shape, F32), sds((shape[0], 128), F32), sds(shape, BF), sds(shape, BF)],
        *got,
        gain[None],
        index=me,
    )


def project_kernel(width, parts, *refs):
    me_ref = refs[0]
    pieces = refs[1 : 1 + parts]
    w_ref = refs[1 + parts]
    normed_ref = refs[2 + parts]
    out_refs = refs[3 + parts : -1]
    all_ref = refs[-1]
    stack_kernel(*pieces, normed_ref)
    depth, rows, _ = all_ref.shape
    weights = w_ref[:, : 3 * width]
    for c in range(depth):
        all_ref[c] = mm(normed_ref[c * rows : (c + 1) * rows, :], weights).astype(BF)
    for t, ref in enumerate(out_refs):
        ref[...] = all_ref[me_ref[0] ^ t]


def project(pieces, attn_w, width, me, depth):
    tokens = sum(p.shape[0] for p in pieces)
    rows = tokens // depth
    out = vmem_call(
        functools.partial(project_kernel, width, len(pieces)),
        [sds((tokens, attn_w.shape[0]), BF)] + [sds((rows, 3 * width), BF)] * depth,
        *pieces,
        attn_w,
        index=me,
        scratch=[pltpu.VMEM((depth, rows, 3 * width), BF)],
        flops=6 * tokens * width * attn_w.shape[0],
    )
    return out[0], out[1:]


def attend_kernel(depth, me_ref, *refs):
    got = refs[:depth]
    outs = refs[depth : 2 * depth]
    qkv, ctx = refs[2 * depth :]
    width = ctx.shape[-1]
    for t in range(depth):
        qkv[me_ref[0] ^ t] = got[t][...]
    q, k, v = ([qkv[p, :, j * width : (j + 1) * width] for p in range(depth)] for j in range(3))
    context, _ = attend(q, k, v)
    for p in range(depth):
        ctx[p] = context[p]
    for t in range(depth):
        outs[t][...] = ctx[me_ref[0] ^ t]


def attend_pieces(got, me):
    depth = len(got)
    rows, wide = got[0].shape
    return vmem_call(
        functools.partial(attend_kernel, depth),
        [sds((rows, wide // 3), BF)] * depth,
        *got,
        index=me,
        scratch=[pltpu.VMEM((depth, rows, wide), BF), pltpu.VMEM((depth, rows, wide // 3), BF)],
        flops=depth * rows * wide * 60,
    )


def attend_back_kernel(depth, me_ref, *refs):
    got = refs[:depth]
    got_context = refs[depth : 2 * depth]
    outs = refs[2 * depth : 3 * depth]
    qkv, ctx = refs[3 * depth :]
    width = ctx.shape[-1]
    for t in range(depth):
        qkv[me_ref[0] ^ t] = got[t][...]
        ctx[me_ref[0] ^ t] = got_context[t][...]
    q, k, v = ([qkv[p, :, j * width : (j + 1) * width] for p in range(depth)] for j in range(3))
    _, probs = attend(q, k, v)
    grads = attend_back(q, k, v, probs, [ctx[p] for p in range(depth)])
    for p in range(depth):
        for j in range(3):
            qkv[p, :, j * width : (j + 1) * width] = grads[j][p]
    for t in range(depth):
        outs[t][...] = qkv[me_ref[0] ^ t]


def attend_back_pieces(got, got_context, me):
    depth = len(got)
    rows, wide = got[0].shape
    return vmem_call(
        functools.partial(attend_back_kernel, depth),
        [sds((rows, wide), BF)] * depth,
        *got,
        *got_context,
        index=me,
        scratch=[pltpu.VMEM((depth, rows, wide), BF), pltpu.VMEM((depth, rows, wide // 3), BF)],
        flops=depth * rows * wide * 100,
    )


def attn_out_kernel(depth, width, me_ref, *refs):
    got = refs[:depth]
    w_ref = refs[depth]
    ctx_ref, near_ref, far_ref = refs[depth + 1 : depth + 4]
    by_chunk = refs[depth + 4]
    for t in range(depth):
        by_chunk[me_ref[0] ^ t] = got[t][...]
    rows = by_chunk.shape[1]
    half = depth // 2
    for c in range(depth):
        ctx_ref[c * rows : (c + 1) * rows, :] = by_chunk[c]
        out = near_ref if c < half else far_ref
        at = (c % half) * rows
        out[at : at + rows, :] = mm_nt(by_chunk[c], w_ref[:, 3 * width :]).astype(BF)


def attn_out_terms(got, attn_w, me):
    depth = len(got)
    rows, width = got[0].shape
    model = attn_w.shape[0]
    tokens = depth * rows
    return vmem_call(
        functools.partial(attn_out_kernel, depth, width),
        [sds((tokens, width), BF)] + [sds((tokens // 2, model), BF)] * 2,
        *got,
        attn_w,
        index=me,
        scratch=[pltpu.VMEM((depth, rows, width), BF)],
        flops=2 * tokens * width * model,
    )


def join_kernel(chips, *refs):
    terms = refs[:chips]
    rows_ref, mask_ref, gain_ref = refs[chips : chips + 3]
    hidden_ref, normed_ref = refs[chips + 3 :]
    hidden = rows_ref[...] + mask_ref[:, :1] * sum_refs(terms)
    hidden_ref[...] = hidden
    normed_ref[...] = rms_forward(hidden, gain_ref[...])[2]


def join_rows(terms, rows_in, mask, gain):
    shape = rows_in.shape
    return vmem_call(
        functools.partial(join_kernel, len(terms)),
        [sds(shape, F32), sds(shape, BF)],
        *terms,
        rows_in,
        mask,
        gain[None],
    )


def norm_back_kernel(chips, _, *refs):
    terms = refs[:chips]
    rows_ref, grad_ref, mask_ref, gain_ref = refs[chips : chips + 4]
    out_ref, masked_ref, gain_out_ref = refs[chips + 4 :]
    grad_normed = sum_refs(terms)
    unit_rows, inv_rms, _ = rms_forward(rows_ref[...], gain_ref[...])
    grad = grad_ref[...] + rms_backward(grad_normed, unit_rows, inv_rms, gain_ref[...])
    out_ref[...] = grad
    masked_ref[...] = (mask_ref[:, :1] * grad).astype(BF)
    gain_out_ref[...] = jnp.sum(grad_normed * unit_rows, axis=0, keepdims=True)


def norm_back(terms, rows, grad_rows, mask, gain, index):
    shape = rows.shape
    return vmem_call(
        functools.partial(norm_back_kernel, len(terms)),
        [sds(shape, F32), sds(shape, BF), sds((1, shape[1]), F32)],
        *terms,
        rows,
        grad_rows,
        mask,
        gain[None],
        index=index,
    )


def finish_kernel(depth, chips, me_ref, *refs):
    terms, ffn_terms = refs[:chips], refs[chips : 2 * chips]
    rows_ref, grad_ref, hidden_ref, mask_ref, gain_ref = refs[2 * chips : 2 * chips + 5]
    outs = refs[2 * chips + 5 : -2]
    output, input_grad = refs[-2:]
    unit_rows, inv_rms, _ = rms_forward(rows_ref[...], gain_ref[...])
    grad = rms_backward(sum_refs(terms), unit_rows, inv_rms, gain_ref[...])
    output[...] = (hidden_ref[...] + mask_ref[:, :1] * sum_refs(ffn_terms)).astype(BF)
    input_grad[...] = (grad_ref[...] + grad).astype(BF)
    share = outs[0].shape[1]
    for t, ref in enumerate(outs):
        at = pl.ds(pl.multiple_of((me_ref[0] ^ t) * share, share), share)
        ref[0] = output[at, :]
        ref[1] = input_grad[at, :]


def finish_rows(terms, ffn_terms, rows, grad_rows, hidden, mask, gain, me, depth):
    tokens, model = rows.shape
    return vmem_call(
        functools.partial(finish_kernel, depth, len(terms)),
        [sds((2, tokens // depth, model), BF)] * depth,
        *terms,
        *ffn_terms,
        rows,
        grad_rows,
        hidden,
        mask,
        gain[None],
        index=me,
        scratch=[pltpu.VMEM((tokens, model), BF)] * 2,
    )


def by_position_kernel(depth, me_ref, *refs):
    for t in range(depth):
        refs[depth][me_ref[0] ^ t] = refs[t][...]


def by_position(got, me):
    return vmem_call(
        functools.partial(by_position_kernel, len(got)),
        [sds((len(got),) + got[0].shape, got[0].dtype)],
        *got,
        index=me,
    )[0]


def whole_frames_kernel(parts, me_ref, *refs):
    share = refs[0].shape[2]
    for t in range(parts):
        at = pl.ds(pl.multiple_of((me_ref[0] ^ t) * share, share), share)
        for p in range(refs[0].shape[0]):
            for j in range(2):
                refs[parts + j][p, at, :] = refs[t][p, j]


def whole_frames(got, me):
    depth, _, share, model = got[0].shape
    return vmem_call(
        functools.partial(whole_frames_kernel, len(got)),
        [sds((depth, len(got) * share, model), BF)] * 2,
        *got,
        index=me,
    )


def ffn_tile(x, g, w_ref, hidden):
    gate_up = mm(x, w_ref[:, : 2 * hidden])
    gate_pre = gate_up[:, :hidden]
    up_proj = gate_up[:, hidden:]
    sig = jax.nn.sigmoid(gate_pre)
    acts = (gate_pre * sig * up_proj).astype(BF)
    grad_act = mm(g, w_ref[:, 2 * hidden :])
    grad_gate = (grad_act * up_proj * sig * (1.0 + gate_pre * (1.0 - sig))).astype(BF)
    grad_up = (grad_act * gate_pre * sig).astype(BF)
    return acts, grad_gate, grad_up


def ffn_kernel(x_ref, g_ref, w_ref, acts_ref, grads_ref, near_ref, far_ref):
    hidden = w_ref.shape[1] // 3
    half = near_ref.shape[0]
    for j, out_ref in enumerate((near_ref, far_ref)):
        at = slice(j * half, (j + 1) * half)
        acts, grad_gate, grad_up = ffn_tile(x_ref[at, :], g_ref[at, :], w_ref, hidden)
        acts_ref[at, :] = acts
        grads_ref[at, :hidden] = grad_gate
        grads_ref[at, hidden:] = grad_up
        out_ref[...] = mm_nt(grads_ref[at, :], w_ref[:, : 2 * hidden]).astype(BF)


def ffn_block(normed, grad_ffn, ffn_w):
    tokens, model = normed.shape
    hidden = ffn_w.shape[1] // 3
    return vmem_call(
        ffn_kernel,
        [sds((tokens, hidden), BF), sds((tokens, 2 * hidden), BF)]
        + [sds((tokens // 2, model), BF)] * 2,
        normed,
        grad_ffn,
        ffn_w,
        flops=10 * tokens * hidden * model,
    )


def weight_grad_kernel(count, *refs):
    out_ref, square_ref = refs[2 * count :]
    total = jnp.zeros((1, 128), F32)
    lane = 0
    for i in range(count):
        left, right = refs[2 * i], refs[2 * i + 1]
        width = right.shape[1]
        grads = mm_tn(left[...], right[...])
        out_ref[:, lane : lane + width] = grads.astype(BF)
        squares = jnp.sum(grads * grads, axis=0, keepdims=True)
        for j in range(0, width, 128):
            total = total + squares[:, j : j + 128]
        lane += width

    @pl.when(pl.program_id(0) == 0)
    def _():
        square_ref[...] = total

    @pl.when(pl.program_id(0) > 0)
    def _():
        square_ref[...] += total


def weight_grads(*pairs):
    owners = axis_total(OWNERS)
    tokens, model = pairs[0][0].shape
    widths = [last - first for _, _, first, last in pairs]
    width = sum(widths)
    if lax.axis_size("rf") > 1 or any(w % 128 for w in widths):
        grads = [mm_tn(left, right[:, first:last]) for left, right, first, last in pairs]
        grads = jnp.concatenate(grads, 1)
        if lax.axis_size("rf") > 1:
            grads = grads.reshape(lax.axis_size("pz"), lax.axis_size("rf"), -1, width)
            grads = lax.psum_scatter(grads, "rf", scatter_dimension=1)
        squares = jnp.sum((grads * grads).reshape(-1, 128), axis=0, keepdims=True)
        return grads.astype(BF).reshape(owners, -1, width), squares
    step = 512
    in_specs = []
    for (_, _, first, _), w in zip(pairs, widths):
        in_specs.append(pl.BlockSpec((tokens, step), lambda i: (0, i)))
        in_specs.append(pl.BlockSpec((tokens, w), lambda i, at=first // w: (0, at)))
    out, squares = pl.pallas_call(
        functools.partial(weight_grad_kernel, len(pairs)),
        out_shape=[sds((model, width), BF), sds((1, 128), F32)],
        grid=(model // step,),
        in_specs=in_specs,
        out_specs=[
            pl.BlockSpec((step, width), lambda i: (i, 0)),
            pl.BlockSpec((1, 128), lambda i: (0, 0)),
        ],
        compiler_params=pltpu.CompilerParams(vmem_limit_bytes=VMEM_LIMIT),
        cost_estimate=pl.CostEstimate(
            flops=2 * tokens * model * width,
            bytes_accessed=2 * (tokens * (2 * model + width) + model * width),
            transcendentals=0,
        ),
        name="weight_grads",
    )(*[v for left, right, _, _ in pairs for v in (left, right)])
    return out.reshape(owners, -1, width), squares


def context_kernel(depth, width, *refs):
    me_ref = refs[0]
    parts = len(refs) - 4 - depth
    pieces = refs[1 : 1 + parts]
    w_ref = refs[1 + parts]
    rows_ref = refs[2 + parts]
    outs = refs[3 + parts : 3 + parts + depth]
    by_chunk = refs[-1]
    stack_kernel(*pieces, rows_ref)
    rows = by_chunk.shape[1]
    for c in range(depth):
        by_chunk[c] = mm(rows_ref[c * rows : (c + 1) * rows, :], w_ref[:, 3 * width :]).astype(BF)
    for t in range(depth):
        outs[t][...] = by_chunk[me_ref[0] ^ t]


def context_grads(pieces, attn_w, width, me, depth):
    tokens = sum(p.shape[0] for p in pieces)
    rows = tokens // depth
    out = vmem_call(
        functools.partial(context_kernel, depth, width),
        [sds((tokens, attn_w.shape[0]), BF)] + [sds((rows, width), BF)] * depth,
        *pieces,
        attn_w,
        index=me,
        scratch=[pltpu.VMEM((depth, rows, width), BF)],
        flops=2 * tokens * width * attn_w.shape[0],
    )
    return out[0], out[1:]


def qkv_back_kernel(depth, width, me_ref, *refs):
    got = refs[:depth]
    w_ref, normed_ref, gain_ref, rows_ref, near_ref, far_ref, gain_out_ref, by_chunk = refs[depth:]
    for t in range(depth):
        by_chunk[me_ref[0] ^ t] = got[t][...]
    rows = by_chunk.shape[1]
    half = depth // 2
    total = jnp.zeros(gain_out_ref.shape, F32)
    for c in range(depth):
        here = slice(c * rows, (c + 1) * rows)
        rows_ref[here, :] = by_chunk[c]
        out = near_ref if c < half else far_ref
        at = (c % half) * rows
        terms = mm_nt(by_chunk[c], w_ref[:, : 3 * width])
        out[at : at + rows, :] = terms.astype(BF)
        total = total + jnp.sum(terms * normed_ref[here, :].astype(F32), axis=0, keepdims=True)
    gain_out_ref[...] = total / gain_ref[...]


def qkv_back(got, attn_w, normed, gain, width, me):
    depth = len(got)
    rows = got[0].shape[0]
    tokens = depth * rows
    model = attn_w.shape[0]
    return vmem_call(
        functools.partial(qkv_back_kernel, depth, width),
        [sds((tokens, 3 * width), BF)]
        + [sds((tokens // 2, model), BF)] * 2
        + [sds((1, model), F32)],
        *got,
        attn_w,
        normed,
        gain[None],
        index=me,
        scratch=[pltpu.VMEM((depth, rows, 3 * width), BF)],
        flops=6 * tokens * width * model,
    )


OWNERS = ("pz", "rs")


def lanes_view(array):
    rows, kinds, depth, cols = array.shape
    split = array.reshape(rows, kinds, depth, cols // 128, 128)
    return split.transpose(0, 1, 3, 2, 4).reshape(-1, 128)


def lanes_back(view, shape):
    rows, kinds, depth, cols = shape
    split = view.reshape(rows, kinds, cols // 128, depth, 128)
    return split.transpose(0, 1, 3, 2, 4).reshape(shape)


def tiles_of(dims, pieces):
    kinds, tiles, depth, parts = dims
    per = tiles // parts
    for number, piece in enumerate(pieces):
        lane = 0
        for k, first, count in piece:
            for t in range(first, first + count):
                for part in range(parts):
                    for p in range(depth):
                        at = (k * tiles + part * per + t) * depth + p
                        yield at, p * parts + part, number, lane
                lane += 128


def widths_of(pieces):
    return [128 * sum(count for _, _, count in piece) for piece in pieces]


def whole_message(kinds, cols):
    return [[(k, 0, cols // 128) for k in range(kinds)]]


def split_kernel(dims, pieces, w_ref, *out_refs):
    kinds, tiles, depth, _ = dims
    rows = out_refs[0].shape[1]
    for at, chunk, number, lane in tiles_of(dims, pieces):
        values = w_ref[pl.ds(at, rows, stride=kinds * tiles * depth), :]
        out_refs[number][chunk, :, lane : lane + 128] = values.astype(BF)


def in_blocks(kernel, grid, in_specs, out_shape, out_specs, args, vmem, scalars=(), scratch=(), **more):
    n_in, n_out, n_scalar = len(in_specs), len(out_specs), len(scalars)

    def run(*refs):
        fixed = refs[:n_scalar]
        arrays = refs[n_scalar : n_scalar + n_in + n_out]
        held = refs[n_scalar + n_in + n_out :]
        pltpu.emit_pipeline(
            lambda *blocks: kernel(*fixed, *blocks, *held),
            grid=grid,
            in_specs=in_specs,
            out_specs=out_specs,
        )(*arrays)

    return pl.pallas_call(
        run,
        out_shape=out_shape,
        in_specs=[pl.BlockSpec(memory_space=pltpu.SMEM)] * n_scalar
        + [pl.BlockSpec(memory_space=pltpu.HBM)] * n_in,
        out_specs=[pl.BlockSpec(memory_space=pltpu.HBM)] * n_out,
        scratch_shapes=list(scratch),
        compiler_params=pltpu.CompilerParams(vmem_limit_bytes=vmem << 20),
        **more,
    )(*scalars, *args)


def split_weights(weights, vmem, pieces=None):
    rows, kinds, depth, cols = weights.shape
    parts = lax.axis_size("rs")
    if (cols // parts) % 128 or rows % 16:
        low = weights.astype(BF).reshape(rows, kinds, depth, parts, cols // parts)
        return [low.transpose(2, 3, 0, 1, 4).reshape(depth * parts, rows, -1)]
    pieces = pieces or whole_message(kinds, cols // parts)
    tiles = cols // 128
    step = math.gcd(rows, 32)
    chunks = depth * parts
    return in_blocks(
        functools.partial(split_kernel, (kinds, tiles, depth, parts), pieces),
        (rows // step,),
        [pl.BlockSpec((step * kinds * tiles * depth, 128), lambda i: (i, 0))],
        [sds((chunks, rows, w), BF) for w in widths_of(pieces)],
        [pl.BlockSpec((chunks, step, w), lambda i: (0, i, 0)) for w in widths_of(pieces)],
        [lanes_view(weights)],
        vmem=vmem,
        cost_estimate=pl.CostEstimate(
            flops=weights.size, bytes_accessed=6 * weights.size, transcendentals=0
        ),
        name="split_weights",
    )


def to_planes(low):
    full = lax.all_to_all(low, OWNERS, 0, 0, tiled=True)
    if lax.axis_size("rf") > 1:
        full = full.reshape((lax.axis_size("pz"), lax.axis_size("rs")) + full.shape[1:])
        full = lax.all_gather(full, "rf", axis=1)
    return full.reshape(-1, full.shape[-1])


def to_owners(chunks):
    return lax.all_to_all(chunks, OWNERS, 0, 0, tiled=True)


def adamw_update(weights, first, second, grads, clip_factor, decay_rate, step_rate):
    clipped = clip_factor * grads
    first_new = BETA_ONE * first + (1.0 - BETA_ONE) * clipped
    second_new = BETA_TWO * second + (1.0 - BETA_TWO) * clipped * clipped
    first_hat = first_new * (1.0 / (1.0 - BETA_ONE**STEP))
    second_hat = second_new * (1.0 / (1.0 - BETA_TWO**STEP))
    new_weights = weights - step_rate * (
        first_hat / (jnp.sqrt(second_hat) + ADAM_EPS) + decay_rate * weights
    )
    return (new_weights, first_new, second_new)


def adamw_kernel(dims, pieces, clip_ref, *refs):
    kinds, tiles, depth, _ = dims
    g_refs = refs[: len(pieces)]
    w_ref, m_ref, v_ref, wn_ref, mn_ref, vn_ref, grads = refs[len(pieces) :]
    rows, units, _ = grads.shape
    places = {at: (number, chunk, lane) for at, chunk, number, lane in tiles_of(dims, pieces)}
    for first in range(0, units, 8):
        tile = [
            g_refs[number][chunk, :, lane : lane + 128].astype(F32)
            for number, chunk, lane in (places[at] for at in range(first, first + 8))
        ]
        grads[:, first : first + 8, :] = jnp.swapaxes(jnp.stack(tile), 0, 1)
    clip = clip_ref[0, 0]

    @pl.loop(0, rows)
    def _(row):
        at = pl.ds(pl.multiple_of(row * units, units), units)
        wn_ref[at, :], mn_ref[at, :], vn_ref[at, :] = adamw_update(
            w_ref[at, :], m_ref[at, :], v_ref[at, :], grads[row], clip, WEIGHT_DECAY, LEARN_RATE
        )


def adamw_owned(weights, first, second, chunks, clip_factor, step, vmem, pieces=None):
    rows, kinds, depth, cols = weights.shape
    parts = lax.axis_size("rs")
    units = kinds * cols // 128 * depth
    if (cols // parts) % 128 or rows % 16 or units % 8:
        grads = chunks[0].reshape(depth, parts, rows, kinds, -1).transpose(2, 3, 0, 1, 4)
        grads = grads.reshape(weights.shape).astype(F32)
        new = adamw_update(weights, first, second, grads, clip_factor, WEIGHT_DECAY, LEARN_RATE)
        return new, new[0]
    pieces = pieces or whole_message(kinds, cols // parts)
    step = math.gcd(rows, step)
    block = pl.BlockSpec((step * units, 128), lambda i: (i, 0))
    new = in_blocks(
        functools.partial(adamw_kernel, (kinds, cols // 128, depth, parts), pieces),
        (rows // step,),
        [pl.BlockSpec((depth * parts, step, w), lambda i: (0, i, 0)) for w in widths_of(pieces)]
        + [block] * 3,
        [sds((weights.size // 128, 128), F32)] * 3,
        [block] * 3,
        [*chunks, lanes_view(weights), lanes_view(first), lanes_view(second)],
        scalars=[clip_factor.reshape(1, 1)],
        vmem=vmem,
        scratch=[pltpu.VMEM((step, units, 128), F32)],
        cost_estimate=pl.CostEstimate(
            flops=20 * weights.size, bytes_accessed=26 * weights.size, transcendentals=0
        ),
        name="adamw",
    )
    return tuple(lanes_back(v, weights.shape) for v in new), new[0]


def body(
    inputs,
    depth_counts,
    out_grad,
    attn_weight,
    attn_first,
    attn_second,
    ffn_weight,
    ffn_first,
    ffn_second,
    norm_gains,
    gain_first,
    gain_second,
):
    depth, frames, model = inputs.shape
    mp_axes = ("mx", "mc")
    share = frames // axis_total(mp_axes)
    gain_attn = norm_gains[0]
    gain_ffn = norm_gains[1]

    me = lax.axis_index("pz")
    positions = ("pz",)
    per = ffn_weight.shape[3] // lax.axis_size("rs") // 128
    packed = pack_rows(inputs, out_grad, depth_counts, me, linear_index(mp_axes), share)
    packed = swap_parts(packed, positions)
    attn_low = split_weights(attn_weight, 48)[0]
    rows_in, rows_grad, mask, normed1_rows, masked = unpack_rows(packed, gain_attn, me)
    attn_w = to_planes(after(attn_low, normed1_rows))
    ffn_low = split_weights(ffn_weight, 48)[0]
    width = attn_w.shape[1] // 4
    normed1_pieces = gather_pieces(normed1_rows)
    grad_ffn = stack_rows(gather_pieces(masked))

    normed1, qkv = project(normed1_pieces, attn_w, width, after(me.reshape(1), ffn_low), depth)
    qkv = swap_parts(qkv, positions)
    context = swap_parts(attend_pieces(qkv, me), positions)
    ffn_w = to_planes(after(ffn_low, *context))
    context, near, far = attn_out_terms(context, attn_w, me)
    hidden_in, normed2_rows = join_rows(scatter_pieces(near, far), rows_in, mask, gain_ffn)
    normed2 = stack_rows(gather_pieces(normed2_rows))

    acts, gate_up_grads, near, far = ffn_block(normed2, grad_ffn, ffn_w)
    terms = scatter_pieces(near, far)
    hidden = acts.shape[1]
    pieces = [[(0, 0, per), (1, 0, per)], [(2, 0, per)]]
    chunks_a, squares_a = weight_grads((normed2, gate_up_grads, 0, 2 * hidden))
    owned_a = to_owners(chunks_a)
    chunks_b, squares_b = weight_grads((grad_ffn, acts, 0, hidden))

    ffn_terms = mm_nt(acts, ffn_w[:, 2 * hidden :]).astype(BF)

    grad_hidden, masked, gain_part2 = norm_back(
        terms, hidden_in, rows_grad, mask, gain_ffn, after(me.reshape(1), chunks_b, ffn_terms)
    )
    grad_attn, grad_context = context_grads(gather_pieces(masked), attn_w, width, me, depth)
    grad_context = swap_parts(grad_context, positions)
    grad_qkv = swap_parts(attend_back_pieces(qkv, grad_context, me), positions)
    half = ffn_terms.shape[0] // 2
    ffn_terms = scatter_pieces(ffn_terms[:half], ffn_terms[half:])
    owned_b = to_owners(after(chunks_b, *grad_qkv, *ffn_terms))
    grad_qkv, near, far, gain_part1 = qkv_back(
        grad_qkv, attn_w, normed1, gain_attn, width, after(me.reshape(1), owned_a)
    )
    attn_chunks, squares_attn = weight_grads(
        (normed1, grad_qkv, 0, 3 * width), (grad_attn, context, 0, width)
    )

    squares = squares_a + squares_b + squares_attn
    squares = jnp.pad(squares, ((0, 0), (0, model - 128)))
    total = jnp.concatenate([gain_part1, gain_part2, squares], 0)
    if lax.axis_size("rf") > 1:
        total = lax.psum(total, "rf")
    for axis in ("mc", "mx", "rs"):
        total = all_sum(total, (axis,))
    back = finish_rows(
        scatter_pieces(near, far),
        ffn_terms,
        rows_in,
        grad_hidden,
        hidden_in,
        mask,
        gain_attn,
        me,
        depth,
    )
    total = all_sum(after(total, back[0]), positions)
    attn_owned = to_owners(after(attn_chunks, total, owned_b))
    back = by_position(swap_parts(back, positions), me)

    gain_grad = total[:2]
    grad_norm = jnp.sqrt(jnp.sum(total[2]) + jnp.sum(gain_grad * gain_grad))
    clip_factor = CLIP_NORM / jnp.maximum(grad_norm, CLIP_NORM)

    ffn_new, ffn_done = adamw_owned(
        ffn_weight, ffn_first, ffn_second, [owned_a, owned_b], clip_factor, 16, 48, pieces
    )
    attn_new, _ = adamw_owned(attn_weight, attn_first, attn_second, [attn_owned], clip_factor, 64, 48)

    back = after(back, attn_owned, ffn_done)
    back = swap_parts([back] * axis_total(mp_axes), mp_axes)
    output, input_grad = whole_frames(back, linear_index(mp_axes))
    gain_new = adamw_update(
        norm_gains, gain_first, gain_second, gain_grad, clip_factor, 0.0, GAIN_RATE
    )
    return (output, input_grad, grad_norm) + attn_new + ffn_new + gain_new


def solution(mesh):
    dp = mesh.shape["dp"]
    mp = mesh.shape["mp"]

    def run(*args):
        depth, _, model = args[0].shape
        heads = args[3].shape[3] // mp // HD
        parts = math.gcd(dp // depth, heads)
        fine = Mesh(
            mesh.devices.reshape(depth, dp // depth // parts, parts, mp // 2, 2),
            ("pz", "rf", "rs", "mx", "mc"),
        )
        rows = ("pz", "rf", "rs")
        cols = ("mx", "mc")
        acts = P(None, rows, None)
        weight = P(rows, None, None, cols)
        return jax.shard_map(
            body,
            mesh=fine,
            in_specs=(acts, P(rows), acts) + (weight,) * 6 + (P(),) * 3,
            out_specs=(acts, acts, P()) + (weight,) * 6 + (P(),) * 3,
            check_vma=False,
        )(*args)

    return run
```

profile of v0, /device:TPU:0, one launch (start us, length us, event | category | flops | bytes accessed | tf_op | source)
XLA Modules:
  0.0 327.3 jit_solution(3207105728132844426)
XLA Ops:
  16.1 4.8 %all-to-all-start = ((bf16[8,128,512]{2,1,0:T(8,128)(2,1)}), bf16[8,128,512]{2,1,0:T(8,128)(2,1)S(1)}, u32[]{:S(2)}, u32[]{:S(2)}) async-start(bf16[8,128,512]{2,1,0:T(8,128)(2,1)} %after.10), calls=%async_computation | async-start | bytes 2097152 | tf_op jit(solution)/shard_map/all_to_all | solution.py:797
  27.1 10.7 %collective-permute-done.4.refs_2_.refs_3_ = bf16[64,1024]{1,0:T(8,128)(2,1)S(1)} collective-permute-done((bf16[64,1024]{1,0:T(8,128)(2,1)S(1)}, bf16[64,1024]{1,0:T(8,128)(2,1)S(1)}, u32[]{:S(2)}, u32[]{:S(2)}) %collective-permute-start.4) | collective-permute-done | bytes 131104 | tf_op jit(solution)/shard_map/ppermute | solution.py:41
  37.9 6.0 %split_weights.2.refs_1_.refs_0_ = bf16[8,128,1536]{2,1,0:T(8,128)(2,1)S(1)} custom-call(f32[12288,128]{1,0:T(8,128)} %bitcast.92), custom_call_target="tpu_custom_call" | custom-call | flops 1572864 | bytes 9437184 | tf_op jit(solution)/shard_map/split_weights/pallas_call | solution.py:759
  50.3 5.2 %collective-permute-start.8 = (bf16[128,384]{1,0:T(8,128)(2,1)S(1)}, bf16[128,384]{1,0:T(8,128)(2,1)S(1)}, u32[]{:S(2)}, u32[]{:S(2)}) collective-permute-start(bf16[128,384]{1,0:T(8,128)(2,1)S(1)} %get-tuple-element.88), channel_id=1, source_target_pairs={{0,16},{8,24},{16,0},{24,8},{1,17},{9,25},{17,1},{25,9},{2,18},{10... | collective-permute-start | bytes 294920 | tf_op jit(solution)/shard_map/ppermute | solution.py:41
  55.5 7.8 %collective-permute-done.8.refs_3_ = bf16[128,384]{1,0:T(8,128)(2,1)S(1)} collective-permute-done((bf16[128,384]{1,0:T(8,128)(2,1)S(1)}, bf16[128,384]{1,0:T(8,128)(2,1)S(1)}, u32[]{:S(2)}, u32[]{:S(2)}) %collective-permute-start.8) | collective-permute-done | bytes 98336 | tf_op jit(solution)/shard_map/ppermute | solution.py:41
  74.7 4.6 %all-to-all-start.1 = ((bf16[8,128,1536]{2,1,0:T(8,128)(2,1)}), bf16[8,128,1536]{2,1,0:T(8,128)(2,1)}, u32[]{:S(2)}, u32[]{:S(2)}) async-start(bf16[8,128,1536]{2,1,0:T(8,128)(2,1)} %after.11), calls=%async_computation.1 | async-start | bytes 6291456 | tf_op jit(solution)/shard_map/all_to_all | solution.py:797
  91.7 23.8 %collective-permute-done.15.refs_2_ = bf16[64,1024]{1,0:T(8,128)(2,1)S(1)} collective-permute-done((bf16[64,1024]{1,0:T(8,128)(2,1)S(1)}, bf16[64,1024]{1,0:T(8,128)(2,1)S(1)}, u32[]{:S(2)}, u32[]{:S(2)}) %collective-permute-start.15) | collective-permute-done | bytes 131104 | tf_op jit(solution)/shard_map/ppermute | solution.py:41
  123.3 8.7 %collective-permute-done.18.refs_2_ = bf16[64,1024]{1,0:T(8,128)(2,1)S(1)} collective-permute-done((bf16[64,1024]{1,0:T(8,128)(2,1)S(1)}, bf16[64,1024]{1,0:T(8,128)(2,1)S(1)}, u32[]{:S(2)}, u32[]{:S(2)}) %collective-permute-start.18) | collective-permute-done | bytes 131104 | tf_op jit(solution)/shard_map/ppermute | solution.py:41
  134.0 14.7 %all-to-all-done.1 = bf16[8,128,1536]{2,1,0:T(8,128)(2,1)} async-done(((bf16[8,128,1536]{2,1,0:T(8,128)(2,1)}), bf16[8,128,1536]{2,1,0:T(8,128)(2,1)}, u32[]{:S(2)}, u32[]{:S(2)}) %all-to-all-start.1) | async-done | bytes 3145760 | tf_op jit(solution)/shard_map/all_to_all | solution.py:797
  149.9 5.1 %ffn_kernel.1 = (bf16[512,512]{1,0:T(8,128)(2,1)S(1)}, bf16[512,1024]{1,0:T(8,128)(2,1)S(1)}, bf16[256,1024]{1,0:T(8,128)(2,1)S(1)}, bf16[256,1024]{1,0:T(8,128)(2,1)S(1)}) custom-call(bf16[512,1024]{1,0:T(8,128)(2,1)S(1)} %stack_kernel.8.refs_0_, bf16[512,1024]{1,0:T(8,128)(2,1)S(1)} %copy-done.20, bf16[1024,1536]{1,0:T(8,128)(2,1)} %bitcast.15.refs_2_), custom_call_target="tpu_custom_call" | custom-call | flops 2684354560 | bytes 7864320 | tf_op jit(solution)/shard_map/ffn_kernel/pallas_call | solution.py:184
  159.9 7.2 %all-to-all-start.2 = ((bf16[8,128,1024]{2,1,0:T(8,128)(2,1)}), bf16[8,128,1024]{2,1,0:T(8,128)(2,1)S(1)}, u32[]{:S(2)}, u32[]{:S(2)}) async-start(bf16[8,128,1024]{2,1,0:T(8,128)(2,1)} %bitcast.90), calls=%async_computation.2 | async-start | bytes 4194304 | tf_op jit(solution)/shard_map/all_to_all | solution.py:805
  181.4 10.1 %collective-permute-done.27.refs_3_ = bf16[64,1024]{1,0:T(8,128)(2,1)} collective-permute-done((bf16[64,1024]{1,0:T(8,128)(2,1)}, bf16[64,1024]{1,0:T(8,128)(2,1)}, u32[]{:S(2)}, u32[]{:S(2)}) %collective-permute-start.27) | collective-permute-done | bytes 131104 | tf_op jit(solution)/shard_map/ppermute | solution.py:41
  201.8 4.5 %collective-permute-done.30.refs_2_.refs_3_ = bf16[64,1024]{1,0:T(8,128)(2,1)S(1)} collective-permute-done((bf16[64,1024]{1,0:T(8,128)(2,1)S(1)}, bf16[64,1024]{1,0:T(8,128)(2,1)S(1)}, u32[]{:S(2)}, u32[]{:S(2)}) %collective-permute-start.30) | collective-permute-done | bytes 131104 | tf_op jit(solution)/shard_map/ppermute | solution.py:41
  209.8 7.0 %collective-permute-start.34 = (bf16[128,128]{1,0:T(8,128)(2,1)S(1)}, bf16[128,128]{1,0:T(8,128)(2,1)S(1)}, u32[]{:S(2)}, u32[]{:S(2)}) collective-permute-start(bf16[128,128]{1,0:T(8,128)(2,1)S(1)} %get-tuple-element.119), channel_id=1, source_target_pairs={{0,16},{8,24},{16,0},{24,8},{1,17},{9,25},{17,1},{25,9},{2,18},{10... | collective-permute-start | bytes 98312 | tf_op jit(solution)/shard_map/ppermute | solution.py:41
  219.3 3.2 collective-permute-done.35.refs_8_
  230.2 3.4 %collective-permute-done.37.refs_3_ = bf16[128,384]{1,0:T(8,128)(2,1)} collective-permute-done((bf16[128,384]{1,0:T(8,128)(2,1)S(1)}, bf16[128,384]{1,0:T(8,128)(2,1)}, u32[]{:S(2)}, u32[]{:S(2)}) %collective-permute-start.37) | collective-permute-done | bytes 98336 | tf_op jit(solution)/shard_map/ppermute | solution.py:41
  233.6 4.9 %all-to-all-start.3 = ((bf16[8,128,512]{2,1,0:T(8,128)(2,1)}), bf16[8,128,512]{2,1,0:T(8,128)(2,1)}, u32[]{:S(2)}, u32[]{:S(2)}) async-start(bf16[8,128,512]{2,1,0:T(8,128)(2,1)} %after.15), calls=%async_computation.3 | async-start | bytes 2097152 | tf_op jit(solution)/shard_map/all_to_all | solution.py:805
  256.9 5.9 %collective-permute-done.52 = f32[3,1024]{1,0:T(4,128)S(1)} collective-permute-done((f32[3,1024]{1,0:T(4,128)S(1)}, f32[3,1024]{1,0:T(4,128)S(1)}, u32[]{:S(2)}, u32[]{:S(2)}) %collective-permute-start.52) | collective-permute-done | bytes 12320 | tf_op jit(solution)/shard_map/ppermute | solution.py:41
  266.1 3.8 %collective-permute-start.54 = (f32[3,1024]{1,0:T(4,128)}, f32[3,1024]{1,0:T(4,128)S(1)}, u32[]{:S(2)}, u32[]{:S(2)}) collective-permute-start(f32[3,1024]{1,0:T(4,128)} %after.14), channel_id=1, source_target_pairs={{0,16},{8,24},{16,0},{24,8},{1,17},{9,25},{17,1},{25,9},{2,18},{10... | collective-permute-start | bytes 36872 | tf_op jit(solution)/shard_map/ppermute | solution.py:41
  271.8 3.8 %collective-permute-done.55 = f32[3,1024]{1,0:T(4,128)S(1)} collective-permute-done((f32[3,1024]{1,0:T(4,128)}, f32[3,1024]{1,0:T(4,128)S(1)}, u32[]{:S(2)}, u32[]{:S(2)}) %collective-permute-start.55) | collective-permute-done | bytes 12320 | tf_op jit(solution)/shard_map/ppermute | solution.py:41
  277.0 4.4 %all-to-all-start.4 = ((bf16[8,128,512]{2,1,0:T(8,128)(2,1)}), bf16[8,128,512]{2,1,0:T(8,128)(2,1)}, u32[]{:S(2)}, u32[]{:S(2)}) async-start(bf16[8,128,512]{2,1,0:T(8,128)(2,1)} %after.16), calls=%async_computation.4 | async-start | bytes 2097152 | tf_op jit(solution)/shard_map/all_to_all | solution.py:805
  288.4 18.3 %adamw.2 = (f32[12288,128]{1,0:T(8,128)}, f32[12288,128]{1,0:T(8,128)}, f32[12288,128]{1,0:T(8,128)}) custom-call(f32[1,1]{1,0:T(1,128)} %bitcast.19.refs_0_, bf16[8,128,1024]{2,1,0:T(8,128)(2,1)S(1)} %copy-done.2, bf16[8,128,512]{2,1,0:T(8,128)(2,1)} %all-to-all-done.3.refs_2_, f32[12288,128]{1,0:T(8,128)} %bitcast.93, f32[12288,128]{1,0:T(8,128)} %bitcast.94, ...), custom_call_target="tpu_custom_call" | custom-call | flops 31457280 | bytes 40894464 | tf_op jit(solution)/shard_map/adamw/pallas_call | solution.py:759
  306.7 3.5 %collective-permute-done.48.refs_3_ = bf16[2,16,1024]{2,1,0:T(8,128)(2,1)S(1)} collective-permute-done((bf16[2,16,1024]{2,1,0:T(8,128)(2,1)}, bf16[2,16,1024]{2,1,0:T(8,128)(2,1)S(1)}, u32[]{:S(2)}, u32[]{:S(2)}) %collective-permute-start.48) | collective-permute-done | bytes 65568 | tf_op jit(solution)/shard_map/ppermute | solution.py:41
  315.1 7.3 %adamw.3 = (f32[4096,128]{1,0:T(8,128)}, f32[4096,128]{1,0:T(8,128)}, f32[4096,128]{1,0:T(8,128)}) custom-call(f32[1,1]{1,0:T(1,128)} %bitcast.19.refs_0_, bf16[8,128,512]{2,1,0:T(8,128)(2,1)} %all-to-all-done.4.refs_1_, f32[4096,128]{1,0:T(8,128)S(1)} %bitcast.88, f32[4096,128]{1,0:T(8,128)S(1)} %bitcast.91, f32[4096,128]{1,0:T(8,128)} %bitcast.97), custom_call_target="tpu_custom_call" | custom-call | flops 10485760 | bytes 13631488 | tf_op jit(solution)/shard_map/adamw/pallas_call | solution.py:759
  (317 shorter events, 144.5 us)
Async XLA Ops:
  16.1 30.8 %all-to-all-start = ((bf16[8,128,512]{2,1,0:T(8,128)(2,1)}), bf16[8,128,512]{2,1,0:T(8,128)(2,1)S(1)}, u32[]{:S(2)}, u32[]{:S(2)}) async-start(bf16[8,128,512]{2,1,0:T(8,128)(2,1)} %after.10), calls=%async_computation | async-start | bytes 2097152 | tf_op jit(solution)/shard_map/all_to_all | solution.py:797
  22.4 15.4 %collective-permute-start.4 = (bf16[64,1024]{1,0:T(8,128)(2,1)S(1)}, bf16[64,1024]{1,0:T(8,128)(2,1)S(1)}, u32[]{:S(2)}, u32[]{:S(2)}) collective-permute-start(bf16[64,1024]{1,0:T(8,128)(2,1)S(1)} %copy-done.16), channel_id=1, source_target_pairs={{0,4},{2,6},{4,0},{6,2},{1,5},{3,7},{5,1},{7,3},{8,12},{10,14},{12... | collective-permute-start | bytes 393224 | tf_op jit(solution)/shard_map/ppermute | solution.py:41
  24.3 13.4 %collective-permute-start.5 = (bf16[64,1024]{1,0:T(8,128)(2,1)S(1)}, bf16[64,1024]{1,0:T(8,128)(2,1)S(1)}, u32[]{:S(2)}, u32[]{:S(2)}) collective-permute-start(bf16[64,1024]{1,0:T(8,128)(2,1)S(1)} %copy-done.16), channel_id=1, source_target_pairs={{0,6},{2,4},{4,2},{6,0},{1,7},{3,5},{5,3},{7,1},{8,14},{10,12},{12... | collective-permute-start | bytes 393224 | tf_op jit(solution)/shard_map/ppermute | solution.py:41
  50.3 13.0 %collective-permute-start.8 = (bf16[128,384]{1,0:T(8,128)(2,1)S(1)}, bf16[128,384]{1,0:T(8,128)(2,1)S(1)}, u32[]{:S(2)}, u32[]{:S(2)}) collective-permute-start(bf16[128,384]{1,0:T(8,128)(2,1)S(1)} %get-tuple-element.88), channel_id=1, source_target_pairs={{0,16},{8,24},{16,0},{24,8},{1,17},{9,25},{17,1},{25,9},{2,18},{10... | collective-permute-start | bytes 294920 | tf_op jit(solution)/shard_map/ppermute | solution.py:41
  74.7 74.0 %all-to-all-start.1 = ((bf16[8,128,1536]{2,1,0:T(8,128)(2,1)}), bf16[8,128,1536]{2,1,0:T(8,128)(2,1)}, u32[]{:S(2)}, u32[]{:S(2)}) async-start(bf16[8,128,1536]{2,1,0:T(8,128)(2,1)} %after.11), calls=%async_computation.1 | async-start | bytes 6291456 | tf_op jit(solution)/shard_map/all_to_all | solution.py:797
  84.0 31.5 %collective-permute-start.15 = (bf16[64,1024]{1,0:T(8,128)(2,1)S(1)}, bf16[64,1024]{1,0:T(8,128)(2,1)S(1)}, u32[]{:S(2)}, u32[]{:S(2)}) collective-permute-start(bf16[64,1024]{1,0:T(8,128)(2,1)S(1)} %get-tuple-element.98), channel_id=1, source_target_pairs={{0,4},{2,6},{4,0},{6,2},{1,5},{3,7},{5,1},{7,3},{8,12},{10,14},{12... | collective-permute-start | bytes 393224 | tf_op jit(solution)/shard_map/ppermute | solution.py:41
  85.9 29.6 %collective-permute-start.16 = (bf16[64,1024]{1,0:T(8,128)(2,1)S(1)}, bf16[64,1024]{1,0:T(8,128)(2,1)S(1)}, u32[]{:S(2)}, u32[]{:S(2)}) collective-permute-start(bf16[64,1024]{1,0:T(8,128)(2,1)S(1)} %get-tuple-element.99), channel_id=1, source_target_pairs={{0,6},{2,4},{4,2},{6,0},{1,7},{3,5},{5,3},{7,1},{8,14},{10,12},{12... | collective-permute-start | bytes 393224 | tf_op jit(solution)/shard_map/ppermute | solution.py:41
  86.0 35.0 %collective-permute-start.21 = (bf16[64,1024]{1,0:T(8,128)(2,1)S(1)}, bf16[64,1024]{1,0:T(8,128)(2,1)S(1)}, u32[]{:S(2)}, u32[]{:S(2)}) collective-permute-start(bf16[64,1024]{1,0:T(8,128)(2,1)S(1)} %copy-done.36), channel_id=1, source_target_pairs={{0,2},{2,0},{4,6},{6,4},{1,3},{3,1},{5,7},{7,5},{8,10},{10,8},{12,... | collective-permute-start | bytes 393224 | tf_op jit(solution)/shard_map/ppermute | solution.py:41
  87.5 33.6 %collective-permute-start.22 = (bf16[64,1024]{1,0:T(8,128)(2,1)S(1)}, bf16[64,1024]{1,0:T(8,128)(2,1)S(1)}, u32[]{:S(2)}, u32[]{:S(2)}) collective-permute-start(bf16[64,1024]{1,0:T(8,128)(2,1)S(1)} %copy-done.36), channel_id=1, source_target_pairs={{0,4},{2,6},{4,0},{6,2},{1,5},{3,7},{5,1},{7,3},{8,12},{10,14},{12... | collective-permute-start | bytes 393224 | tf_op jit(solution)/shard_map/ppermute | solution.py:41
  89.4 31.7 %collective-permute-start.23 = (bf16[64,1024]{1,0:T(8,128)(2,1)S(1)}, bf16[64,1024]{1,0:T(8,128)(2,1)S(1)}, u32[]{:S(2)}, u32[]{:S(2)}) collective-permute-start(bf16[64,1024]{1,0:T(8,128)(2,1)S(1)} %copy-done.36), channel_id=1, source_target_pairs={{0,6},{2,4},{4,2},{6,0},{1,7},{3,5},{5,3},{7,1},{8,14},{10,12},{12... | collective-permute-start | bytes 393224 | tf_op jit(solution)/shard_map/ppermute | solution.py:41
  118.6 13.4 %collective-permute-start.18 = (bf16[64,1024]{1,0:T(8,128)(2,1)S(1)}, bf16[64,1024]{1,0:T(8,128)(2,1)S(1)}, u32[]{:S(2)}, u32[]{:S(2)}) collective-permute-start(bf16[64,1024]{1,0:T(8,128)(2,1)S(1)} %get-tuple-element.102.refs_0_), channel_id=1, source_target_pairs={{0,4},{2,6},{4,0},{6,2},{1,5},{3,7},{5,1},{7,3},{8,12},{10,14},{12... | collective-permute-start | bytes 393224 | tf_op jit(solution)/shard_map/ppermute | solution.py:41
  159.9 73.7 %all-to-all-start.2 = ((bf16[8,128,1024]{2,1,0:T(8,128)(2,1)}), bf16[8,128,1024]{2,1,0:T(8,128)(2,1)S(1)}, u32[]{:S(2)}, u32[]{:S(2)}) async-start(bf16[8,128,1024]{2,1,0:T(8,128)(2,1)} %bitcast.90), calls=%async_computation.2 | async-start | bytes 4194304 | tf_op jit(solution)/shard_map/all_to_all | solution.py:805
  173.0 18.5 %collective-permute-start.27 = (bf16[64,1024]{1,0:T(8,128)(2,1)}, bf16[64,1024]{1,0:T(8,128)(2,1)}, u32[]{:S(2)}, u32[]{:S(2)}) collective-permute-start(bf16[64,1024]{1,0:T(8,128)(2,1)} %get-tuple-element.112), channel_id=1, source_target_pairs={{0,4},{2,6},{4,0},{6,2},{1,5},{3,7},{5,1},{7,3},{8,12},{10,14},{12... | collective-permute-start | bytes 393224 | tf_op jit(solution)/shard_map/ppermute | solution.py:41
  174.9 16.6 %collective-permute-start.28 = (bf16[64,1024]{1,0:T(8,128)(2,1)}, bf16[64,1024]{1,0:T(8,128)(2,1)}, u32[]{:S(2)}, u32[]{:S(2)}) collective-permute-start(bf16[64,1024]{1,0:T(8,128)(2,1)} %get-tuple-element.113), channel_id=1, source_target_pairs={{0,6},{2,4},{4,2},{6,0},{1,7},{3,5},{5,3},{7,1},{8,14},{10,12},{12... | collective-permute-start | bytes 393224 | tf_op jit(solution)/shard_map/ppermute | solution.py:41
  206.6 18.7 %collective-permute-start.44 = (bf16[64,1024]{1,0:T(8,128)(2,1)S(1)}, bf16[64,1024]{1,0:T(8,128)(2,1)S(1)}, u32[]{:S(2)}, u32[]{:S(2)}) collective-permute-start(bf16[64,1024]{1,0:T(8,128)(2,1)S(1)} %get-tuple-element.133), channel_id=1, source_target_pairs={{0,2},{2,0},{4,6},{6,4},{1,3},{3,1},{5,7},{7,5},{8,10},{10,8},{12,... | collective-permute-start | bytes 393224 | tf_op jit(solution)/shard_map/ppermute | solution.py:41
  216.9 11.7 %collective-permute-start.45 = (bf16[64,1024]{1,0:T(8,128)(2,1)S(1)}, bf16[64,1024]{1,0:T(8,128)(2,1)}, u32[]{:S(2)}, u32[]{:S(2)}) collective-permute-start(bf16[64,1024]{1,0:T(8,128)(2,1)S(1)} %get-tuple-element.134), channel_id=1, source_target_pairs={{0,4},{2,6},{4,0},{6,2},{1,5},{3,7},{5,1},{7,3},{8,12},{10,14},{12... | collective-permute-start | bytes 393224 | tf_op jit(solution)/shard_map/ppermute | solution.py:41
  233.6 43.3 %all-to-all-start.3 = ((bf16[8,128,512]{2,1,0:T(8,128)(2,1)}), bf16[8,128,512]{2,1,0:T(8,128)(2,1)}, u32[]{:S(2)}, u32[]{:S(2)}) async-start(bf16[8,128,512]{2,1,0:T(8,128)(2,1)} %after.15), calls=%async_computation.3 | async-start | bytes 2097152 | tf_op jit(solution)/shard_map/all_to_all | solution.py:805
  251.2 12.2 %collective-permute-start.40 = (bf16[64,1024]{1,0:T(8,128)(2,1)S(1)}, bf16[64,1024]{1,0:T(8,128)(2,1)S(1)}, u32[]{:S(2)}, u32[]{:S(2)}) collective-permute-start(bf16[64,1024]{1,0:T(8,128)(2,1)S(1)} %get-tuple-element.129), channel_id=1, source_target_pairs={{0,2},{2,0},{4,6},{6,4},{1,3},{3,1},{5,7},{7,5},{8,10},{10,8},{12,... | collective-permute-start | bytes 393224 | tf_op jit(solution)/shard_map/ppermute | solution.py:41
  277.0 33.9 %all-to-all-start.4 = ((bf16[8,128,512]{2,1,0:T(8,128)(2,1)}), bf16[8,128,512]{2,1,0:T(8,128)(2,1)}, u32[]{:S(2)}, u32[]{:S(2)}) async-start(bf16[8,128,512]{2,1,0:T(8,128)(2,1)} %after.16), calls=%async_computation.4 | async-start | bytes 2097152 | tf_op jit(solution)/shard_map/all_to_all | solution.py:805
  281.3 25.4 %collective-permute-start.47 = (bf16[2,16,1024]{2,1,0:T(8,128)(2,1)}, bf16[2,16,1024]{2,1,0:T(8,128)(2,1)S(1)}, u32[]{:S(2)}, u32[]{:S(2)}) collective-permute-start(bf16[2,16,1024]{2,1,0:T(8,128)(2,1)} %get-tuple-element.138), channel_id=1, source_target_pairs={{0,8},{8,0},{16,24},{24,16},{1,9},{9,1},{17,25},{25,17},{2,10},{10... | collective-permute-start | bytes 196616 | tf_op jit(solution)/shard_map/ppermute | solution.py:41
  283.2 26.9 %collective-permute-start.48 = (bf16[2,16,1024]{2,1,0:T(8,128)(2,1)}, bf16[2,16,1024]{2,1,0:T(8,128)(2,1)S(1)}, u32[]{:S(2)}, u32[]{:S(2)}) collective-permute-start(bf16[2,16,1024]{2,1,0:T(8,128)(2,1)} %get-tuple-element.139), channel_id=1, source_target_pairs={{0,16},{8,24},{16,0},{24,8},{1,17},{9,25},{17,1},{25,9},{2,18},{10... | collective-permute-start | bytes 196616 | tf_op jit(solution)/shard_map/ppermute | solution.py:41
  285.6 24.5 %collective-permute-start.49 = (bf16[2,16,1024]{2,1,0:T(8,128)(2,1)}, bf16[2,16,1024]{2,1,0:T(8,128)(2,1)S(1)}, u32[]{:S(2)}, u32[]{:S(2)}) collective-permute-start(bf16[2,16,1024]{2,1,0:T(8,128)(2,1)} %get-tuple-element.140), channel_id=1, source_target_pairs={{0,24},{8,16},{16,8},{24,0},{1,25},{9,17},{17,9},{25,1},{2,26},{10... | collective-permute-start | bytes 196616 | tf_op jit(solution)/shard_map/ppermute | solution.py:41
  310.9 11.5 %collective-permute-start.56 = (bf16[4,2,16,1024]{3,2,1,0:T(8,128)(2,1)}, bf16[4,2,16,1024]{3,2,1,0:T(8,128)(2,1)S(1)}, u32[]{:S(2)}, u32[]{:S(2)}) collective-permute-start(bf16[4,2,16,1024]{3,2,1,0:T(8,128)(2,1)} %after.17.refs_1_), channel_id=1, source_target_pairs={{0,1},{1,0},{2,3},{3,2},{4,5},{5,4},{6,7},{7,6},{8,9},{9,8},{10,11... | collective-permute-start | bytes 786440 | tf_op jit(solution)/shard_map/ppermute | solution.py:41
  311.9 13.2 %collective-permute-start.58 = (bf16[4,2,16,1024]{3,2,1,0:T(8,128)(2,1)}, bf16[4,2,16,1024]{3,2,1,0:T(8,128)(2,1)S(1)}, u32[]{:S(2)}, u32[]{:S(2)}) collective-permute-start(bf16[4,2,16,1024]{3,2,1,0:T(8,128)(2,1)} %after.17.refs_1_), channel_id=1, source_target_pairs={{0,3},{1,2},{2,1},{3,0},{4,7},{5,6},{6,5},{7,4},{8,11},{9,10},{10,... | collective-permute-start | bytes 786440 | tf_op jit(solution)/shard_map/ppermute | solution.py:41
  (118 other events, 817.3 us)
where the time goes:
time: 329 us; the launch traced here: 327 us
  waiting for transfers between devices  123 us (37%)
  starting transfers between devices  98.7 us (30%)
  Pallas kernels  57.2 us (17%)
  local copies, waits for them, and re-layouts  37.7 us (11%)
  between operations  4.11 us (1%)
  other arithmetic  3.88 us (1%)
    ppermute x59, waiting for transfers between devices, hop(): return lax.ppermute(value, axes, [(i, i ^ step) for i in range(n)])  108 us
    ppermute x59, starting transfers between devices, hop(): return lax.ppermute(value, axes, [(i, i ^ step) for i in range(n)])  72.9 us
    unnamed x156, local copies, waits for them, and re-layouts  33.8 us
    pallas_call x4, Pallas kernels, in_blocks(): pl.pallas_call(run, out_shape=out_shape, in_specs=[pl.BlockSpec(memory_sp...  33.2 us
    pallas_call x23, Pallas kernels, vmem_call(): pl.pallas_call(run, out_shape=list(outs), in_specs=specs, out_specs=[pl.B...  18.4 us
    all_to_all x3, starting transfers between devices, to_owners(): return lax.all_to_all(chunks, OWNERS, 0, 0, tiled=True)  16.5 us
    all_to_all x2, waiting for transfers between devices, to_planes(): full = lax.all_to_all(low, OWNERS, 0, 0, tiled=True)  14.7 us
    all_to_all x2, starting transfers between devices, to_planes(): full = lax.all_to_all(low, OWNERS, 0, 0, tiled=True)  9.38 us
  transfers between devices with their start and end apart: 64, of which 27 were waited for; matrix products, arithmetic and copies ran while one was open for 3% of the time, Pallas kernels for 14%

commit v1 on v0

--- a/solution.py
+++ b/solution.py
@@ -169,28 +169,23 @@
     return grad_query, grad_key, grad_value
 
 
-def vmem_call(kernel, outs, *args, index=None, scratch=(), flops=0, wait_for=()):
+def vmem_call(kernel, outs, *args, index=None, scratch=(), flops=0, vmem=None):
     size = sum(v.size * v.dtype.itemsize for v in args)
     size += sum(math.prod(v.shape) * v.dtype.itemsize for v in outs)
     first = () if index is None else (jnp.reshape(index, (-1,)).astype(jnp.int32),)
-    specs = [pl.BlockSpec(memory_space=pltpu.SMEM)] * len(first)
-    specs += [pl.BlockSpec(memory_space=pltpu.VMEM)] * len(args)
-    specs += [pl.BlockSpec(memory_space=pl.ANY)] * len(wait_for)
-    read = len(first) + len(args)
-
-    def run(*refs):
-        kernel(*refs[:read], *refs[read + len(wait_for) :])
-
+    array = pl.BlockSpec() if vmem else pl.BlockSpec(memory_space=pltpu.VMEM)
     return pl.pallas_call(
-        run,
+        kernel,
         out_shape=list(outs),
-        in_specs=specs,
-        out_specs=[pl.BlockSpec(memory_space=pltpu.VMEM)] * len(outs),
+        in_specs=[pl.BlockSpec(memory_space=pltpu.SMEM)] * len(first) + [array] * len(args),
+        out_specs=[array] * len(outs),
         scratch_shapes=list(scratch),
-        compiler_params=pltpu.CompilerParams(vmem_limit_bytes=VMEM_LIMIT),
+        compiler_params=pltpu.CompilerParams(
+            vmem_limit_bytes=vmem << 20 if vmem else VMEM_LIMIT
+        ),
         cost_estimate=pl.CostEstimate(flops=flops, bytes_accessed=size, transcendentals=0),
         name=getattr(kernel, "func", kernel).__name__,
-    )(*first, *args, *wait_for)
+    )(*first, *args)
 
 
 def sds(shape, dtype):
@@ -491,6 +486,7 @@
         mask,
         gain[None],
         index=me,
+        vmem=56,
         scratch=[pltpu.VMEM((tokens, model), BF)] * 2,
     )
 
@@ -697,6 +693,67 @@
     )
 
 
+def attn_grads_kernel(depth, width, me_ref, *refs):
+    got = refs[:depth]
+    w_ref, normed_ref, grad_ref, context_ref, gain_ref, gain2_ref, square_ref = refs[depth : depth + 7]
+    near_ref, far_ref, chunk_ref, total_ref, by_chunk, grads = refs[depth + 7 :]
+    for t in range(depth):
+        by_chunk[me_ref[0] ^ t] = got[t][...]
+    rows = by_chunk.shape[1]
+    half = depth // 2
+    total = jnp.zeros(gain_ref.shape, F32)
+    for c in range(depth):
+        here = slice(c * rows, (c + 1) * rows)
+        grads[here, :] = by_chunk[c]
+        out = near_ref if c < half else far_ref
+        at = (c % half) * rows
+        terms = mm_nt(by_chunk[c], w_ref[:, : 3 * width])
+        out[at : at + rows, :] = terms.astype(BF)
+        total = total + jnp.sum(terms * normed_ref[here, :].astype(F32), axis=0, keepdims=True)
+    total_ref[0:1, :] = total / gain_ref[...]
+    total_ref[1:2, :] = gain2_ref[...]
+    squares = square_ref[...]
+    for first, left, right in ((0, normed_ref, grads), (3 * width, grad_ref, context_ref)):
+        chunk = mm_tn(left[...], right[...])
+        last = first + chunk.shape[1]
+        chunk_ref[:, first:last] = chunk.astype(BF)
+        column = jnp.sum(chunk * chunk, axis=0, keepdims=True)
+        for j in range(0, last - first, 128):
+            squares = squares + column[:, j : j + 128]
+    total_ref[2:3, :] = jnp.zeros(gain_ref.shape, F32)
+    total_ref[2:3, :128] = squares
+
+
+def attn_grads(got, attn_w, normed, grad_attn, context, gain, gain_part2, squares, me):
+    depth = len(got)
+    rows, wide = got[0].shape
+    width = wide // 3
+    tokens = depth * rows
+    model = attn_w.shape[0]
+    if lax.axis_size("rf") > 1 or width % 128:
+        grads, near, far, gain_part1 = qkv_back(got, attn_w, normed, gain, width, me)
+        chunks, more = weight_grads((normed, grads, 0, wide), (grad_attn, context, 0, width))
+        squares = jnp.pad(squares + more, ((0, 0), (0, model - 128)))
+        return near, far, chunks, jnp.concatenate([gain_part1, gain_part2, squares], 0)
+    near, far, chunks, total = vmem_call(
+        functools.partial(attn_grads_kernel, depth, width),
+        [sds((tokens // 2, model), BF)] * 2 + [sds((model, 4 * width), BF), sds((3, model), F32)],
+        *got,
+        attn_w,
+        normed,
+        grad_attn,
+        context,
+        gain[None],
+        gain_part2,
+        squares,
+        index=me,
+        scratch=[pltpu.VMEM((depth, rows, wide), BF), pltpu.VMEM((tokens, wide), BF)],
+        flops=14 * tokens * width * model,
+        vmem=56,
+    )
+    return near, far, chunks.reshape(axis_total(OWNERS), -1, 4 * width), total
+
+
 OWNERS = ("pz", "rs")
 
 
@@ -817,57 +874,117 @@
     return (new_weights, first_new, second_new)
 
 
-def adamw_kernel(dims, pieces, clip_ref, *refs):
+def norm_of(total):
+    sums = jnp.sum(total[:2] * total[:2], axis=0, keepdims=True) + total[2:3]
+    return jnp.sqrt(jnp.sum(sums, axis=1, keepdims=True))
+
+
+def adamw_kernel(dims, pieces, steps, stages, total_ref, *refs):
     kinds, tiles, depth, _ = dims
-    g_refs = refs[: len(pieces)]
-    w_ref, m_ref, v_ref, wn_ref, mn_ref, vn_ref, grads = refs[len(pieces) :]
+    n = len(pieces)
+    g_refs, state, refs = refs[:n], refs[n : n + 3], refs[n + 3 :]
+    stage_refs, new_refs, staged_refs = refs[:stages], refs[stages : stages + 3], refs[stages + 3 :]
+    staged_refs, refs = staged_refs[:stages], staged_refs[stages:]
+    g_held, refs = refs[:n], refs[n:]
+    here = len(refs) == 6
+    state_held, refs = (state, refs) if here else (refs[:3], refs[3:])
+    new_held, grads, in_sems, out_sems = refs[:3], refs[3], refs[4], refs[5]
     rows, units, _ = grads.shape
+    count = rows * units
     places = {at: (number, chunk, lane) for at, chunk, number, lane in tiles_of(dims, pieces)}
-    for first in range(0, units, 8):
-        tile = [
-            g_refs[number][chunk, :, lane : lane + 128].astype(F32)
-            for number, chunk, lane in (places[at] for at in range(first, first + 8))
-        ]
-        grads[:, first : first + 8, :] = jnp.swapaxes(jnp.stack(tile), 0, 1)
-    clip = clip_ref[0, 0]
-
-    @pl.loop(0, rows)
-    def _(row):
-        at = pl.ds(pl.multiple_of(row * units, units), units)
-        wn_ref[at, :], mn_ref[at, :], vn_ref[at, :] = adamw_update(
-            w_ref[at, :], m_ref[at, :], v_ref[at, :], grads[row], clip, WEIGHT_DECAY, LEARN_RATE
-        )
-
-
-def adamw_owned(weights, first, second, chunks, clip_factor, step, vmem, pieces=None):
-    rows, kinds, depth, cols = weights.shape
+
+    def fetches(i):
+        some = pl.ds(pl.multiple_of(i * rows, rows), rows)
+        pairs = [(g.at[:, some, :], held.at[:, some, :]) for g, held in zip(g_refs, g_held)]
+        if not here:
+            some = pl.ds(pl.multiple_of(i * count, count), count)
+            pairs += [(v.at[some, :], held.at[some, :]) for v, held in zip(state, state_held)]
+        return [pltpu.make_async_copy(*pair, in_sems.at[i, j]) for j, pair in enumerate(pairs)]
+
+    def stores(i):
+        some = pl.ds(pl.multiple_of(i * count, count), count)
+        pairs = [(held.at[some, :], new.at[some, :]) for held, new in zip(new_held, new_refs)]
+        return [pltpu.make_async_copy(*pair, out_sems.at[i, j]) for j, pair in enumerate(pairs)]
+
+    staging = [
+        pltpu.make_async_copy(source, to, out_sems.at[steps, j])
+        for j, (source, to) in enumerate(zip(stage_refs, staged_refs))
+    ]
+
+    @pl.loop(0, steps)
+    def _(i):
+        for copy in fetches(i):
+            copy.start()
+
+    for copy in staging:
+        copy.start()
+    clip = CLIP_NORM / jnp.maximum(norm_of(total_ref[...]), CLIP_NORM)
+
+    @pl.loop(0, steps)
+    def _(i):
+        for copy in fetches(i):
+            copy.wait()
+        some = pl.ds(pl.multiple_of(i * rows, rows), rows)
+        for first in range(0, units, 8):
+            tile = [
+                g_held[number][chunk, some, lane : lane + 128].astype(F32)
+                for number, chunk, lane in (places[at] for at in range(first, first + 8))
+            ]
+            grads[:, first : first + 8, :] = jnp.swapaxes(jnp.stack(tile), 0, 1)
+
+        @pl.loop(0, rows)
+        def _(row):
+            at = pl.ds(pl.multiple_of(i * count + row * units, units), units)
+            new = adamw_update(
+                *(held[at, :] for held in state_held), grads[row], clip, WEIGHT_DECAY, LEARN_RATE
+            )
+            for held, values in zip(new_held, new):
+                held[at, :] = values
+
+        for copy in stores(i):
+            copy.start()
+
+    @pl.loop(0, steps)
+    def _(i):
+        for copy in stores(i):
+            copy.wait()
+
+    for copy in staging:
+        copy.wait()
+
+
+def adamw_owned(state, chunks, total, shape, pieces=None, stage=(), here=False):
+    rows, kinds, depth, cols = shape
     parts = lax.axis_size("rs")
+    pieces = pieces or whole_message(kinds, cols // parts)
     units = kinds * cols // 128 * depth
-    if (cols // parts) % 128 or rows % 16 or units % 8:
-        grads = chunks[0].reshape(depth, parts, rows, kinds, -1).transpose(2, 3, 0, 1, 4)
-        grads = grads.reshape(weights.shape).astype(F32)
-        new = adamw_update(weights, first, second, grads, clip_factor, WEIGHT_DECAY, LEARN_RATE)
-        return new, new[0]
-    pieces = pieces or whole_message(kinds, cols // parts)
-    step = math.gcd(rows, step)
-    block = pl.BlockSpec((step * units, 128), lambda i: (i, 0))
-    new = in_blocks(
-        functools.partial(adamw_kernel, (kinds, cols // 128, depth, parts), pieces),
-        (rows // step,),
-        [pl.BlockSpec((depth * parts, step, w), lambda i: (0, i, 0)) for w in widths_of(pieces)]
-        + [block] * 3,
-        [sds((weights.size // 128, 128), F32)] * 3,
-        [block] * 3,
-        [*chunks, lanes_view(weights), lanes_view(first), lanes_view(second)],
-        scalars=[clip_factor.reshape(1, 1)],
-        vmem=vmem,
-        scratch=[pltpu.VMEM((step, units, 128), F32)],
+    step = math.gcd(rows, 16)
+    steps = rows // step
+    anywhere = pl.BlockSpec(memory_space=pl.ANY)
+    inside = pl.BlockSpec(memory_space=pltpu.VMEM)
+    view = state[0].shape
+    out = pl.pallas_call(
+        functools.partial(
+            adamw_kernel, (kinds, cols // 128, depth, parts), pieces, steps, len(stage)
+        ),
+        out_shape=[sds(view, F32)] * 3 + [sds(v.shape, F32) for v in stage],
+        in_specs=[inside]
+        + [anywhere] * len(chunks)
+        + [inside if here else anywhere] * 3
+        + [anywhere] * len(stage),
+        out_specs=[anywhere] * 3 + [inside] * len(stage),
+        scratch_shapes=[pltpu.VMEM(v.shape, BF) for v in chunks]
+        + [pltpu.VMEM(view, F32)] * (3 if here else 6)
+        + [pltpu.VMEM((step, units, 128), F32)]
+        + [pltpu.SemaphoreType.DMA((steps, len(chunks) + 3))]
+        + [pltpu.SemaphoreType.DMA((steps + 1, 3))],
+        compiler_params=pltpu.CompilerParams(vmem_limit_bytes=(20 if here else 52) << 20),
         cost_estimate=pl.CostEstimate(
-            flops=20 * weights.size, bytes_accessed=26 * weights.size, transcendentals=0
+            flops=20 * math.prod(shape), bytes_accessed=26 * math.prod(shape), transcendentals=0
         ),
         name="adamw",
-    )
-    return tuple(lanes_back(v, weights.shape) for v in new), new[0]
+    )(total, *chunks, *state, *stage)
+    return out[:3], out[3:]
 
 
 def body(
@@ -929,48 +1046,54 @@
     grad_qkv = swap_parts(attend_back_pieces(qkv, grad_context, me), positions)
     half = ffn_terms.shape[0] // 2
     ffn_terms = scatter_pieces(ffn_terms[:half], ffn_terms[half:])
-    owned_b = to_owners(after(chunks_b, *grad_qkv, *ffn_terms))
-    grad_qkv, near, far, gain_part1 = qkv_back(
-        grad_qkv, attn_w, normed1, gain_attn, width, after(me.reshape(1), owned_a)
-    )
-    attn_chunks, squares_attn = weight_grads(
-        (normed1, grad_qkv, 0, 3 * width), (grad_attn, context, 0, width)
-    )
-
-    squares = squares_a + squares_b + squares_attn
-    squares = jnp.pad(squares, ((0, 0), (0, model - 128)))
-    total = jnp.concatenate([gain_part1, gain_part2, squares], 0)
+    owned_b = to_owners(after(chunks_b, *grad_qkv, *ffn_terms[1:]))
+    near, far, attn_chunks, total = attn_grads(
+        grad_qkv,
+        attn_w,
+        normed1,
+        grad_attn,
+        context,
+        gain_attn,
+        gain_part2,
+        squares_a + squares_b,
+        after(me.reshape(1), owned_a),
+    )
+    terms = scatter_pieces(near, far)
+
     if lax.axis_size("rf") > 1:
         total = lax.psum(total, "rf")
-    for axis in ("mc", "mx", "rs"):
-        total = all_sum(total, (axis,))
+    total = all_sum(all_sum(total, mp_axes), ("rs",))
+    total = all_sum(after(total, *terms[1:]), positions)
     back = finish_rows(
-        scatter_pieces(near, far),
-        ffn_terms,
-        rows_in,
-        grad_hidden,
-        hidden_in,
-        mask,
-        gain_attn,
-        me,
-        depth,
-    )
-    total = all_sum(after(total, back[0]), positions)
-    attn_owned = to_owners(after(attn_chunks, total, owned_b))
-    back = by_position(swap_parts(back, positions), me)
-
-    gain_grad = total[:2]
-    grad_norm = jnp.sqrt(jnp.sum(total[2]) + jnp.sum(gain_grad * gain_grad))
-    clip_factor = CLIP_NORM / jnp.maximum(grad_norm, CLIP_NORM)
-
-    ffn_new, ffn_done = adamw_owned(
-        ffn_weight, ffn_first, ffn_second, [owned_a, owned_b], clip_factor, 16, 48, pieces
-    )
-    attn_new, _ = adamw_owned(attn_weight, attn_first, attn_second, [attn_owned], clip_factor, 64, 48)
-
-    back = after(back, attn_owned, ffn_done)
+        terms, ffn_terms, rows_in, grad_hidden, hidden_in, mask, gain_attn, me, depth
+    )
+    back = swap_parts(back, positions)
+    attn_owned = to_owners(after(attn_chunks, total, owned_b, *back[1:]))
+
+    back = by_position(back, me)
     back = swap_parts([back] * axis_total(mp_axes), mp_axes)
     output, input_grad = whole_frames(back, linear_index(mp_axes))
+
+    gain_grad = total[:2]
+    grad_norm = norm_of(total)[0, 0]
+    clip_factor = CLIP_NORM / jnp.maximum(grad_norm, CLIP_NORM)
+
+    ffn_state = [lanes_view(v) for v in (ffn_weight, ffn_first, ffn_second)]
+    attn_state = [lanes_view(v) for v in (attn_weight, attn_first, attn_second)]
+    ffn_new, _ = adamw_owned(ffn_state, [owned_a, owned_b], total, ffn_weight.shape, pieces)
+    if width % 128:
+        grads = attn_owned.reshape(depth, lax.axis_size("rs"), -1, 4, width)
+        grads = grads.transpose(2, 3, 0, 1, 4).reshape(attn_weight.shape).astype(F32)
+        attn_new = adamw_update(
+            attn_weight, attn_first, attn_second, grads, clip_factor, WEIGHT_DECAY, LEARN_RATE
+        )
+    else:
+        attn_new, _ = adamw_owned(
+            attn_state, [attn_owned], after(total, ffn_new[0], output), attn_weight.shape
+        )
+        attn_new = tuple(lanes_back(v, attn_weight.shape) for v in attn_new)
+    ffn_new = tuple(lanes_back(v, ffn_weight.shape) for v in ffn_new)
+
     gain_new = adamw_update(
         norm_gains, gain_first, gain_second, gain_grad, clip_factor, 0.0, GAIN_RATE
     )

time: 329 us -> 315 us (0.957)
  local copies, waits for them, and re-layouts: 37.7 us -> 25.4 us
    pallas_call x4 -> x2, Pallas kernels: 33.2 us -> 7.58 us  [in_blocks(): pl.pallas_call(run, out_shape=out_shape, in_specs=[pl.BlockSpec(memory_sp...]
    pallas_call x23 -> x25, Pallas kernels: 18.4 us -> 42.5 us  [the longest x2 21.8 us: adamw_owned(): pl.pallas_call(functools.partial(adamw_kernel, (kinds, cols // 128, depth...]
    unnamed x156 -> x132, local copies, waits for them, and re-layouts: 33.8 us -> 21.5 us
    ppermute x59 -> x60, starting transfers between devices: 72.9 us -> 70 us  [hop(): return lax.ppermute(value, axes, [(i, i ^ step) for i in range(n)])]
    ppermute x59 -> x60, waiting for transfers between devices: 108 us -> 109 us  [hop(): return lax.ppermute(value, axes, [(i, i ^ step) for i in range(n)])]
  transfers between devices with their start and end apart: 64 -> 65, of which waited for: 27 -> 24; matrix products, arithmetic and copies ran while one was open for 3% -> 3% of each run, Pallas kernels for 14% -> 12%
where the time goes in v1:
time: 315 us; the launch traced here: 313 us
  waiting for transfers between devices  125 us (40%)
  starting transfers between devices  96.8 us (31%)
  Pallas kernels  55.3 us (18%)
  local copies, waits for them, and re-layouts  25.4 us (8%)
  other arithmetic  4.52 us (1%)
  between operations  3.33 us (1%)
  matrix products  3.15 us (1%)
    ppermute x60, waiting for transfers between devices, hop(): return lax.ppermute(value, axes, [(i, i ^ step) for i in range(n)])  109 us
    ppermute x60, starting transfers between devices, hop(): return lax.ppermute(value, axes, [(i, i ^ step) for i in range(n)])  70 us
    pallas_call x2, Pallas kernels, adamw_owned(): pl.pallas_call(functools.partial(adamw_kernel, (kinds, cols // 128, depth...  21.8 us
    unnamed x132, local copies, waits for them, and re-layouts  21.5 us
    pallas_call x23, Pallas kernels, vmem_call(): pl.pallas_call(kernel, out_shape=list(outs), in_specs=[pl.BlockSpec(memor...  20.7 us
    all_to_all x3, starting transfers between devices, to_owners(): return lax.all_to_all(chunks, OWNERS, 0, 0, tiled=True)  16.7 us
    all_to_all x2, waiting for transfers between devices, to_planes(): full = lax.all_to_all(low, OWNERS, 0, 0, tiled=True)  14.5 us
    all_to_all x2, starting transfers between devices, to_planes(): full = lax.all_to_all(low, OWNERS, 0, 0, tiled=True)  10.1 us
  transfers between devices with their start and end apart: 65, of which 24 were waited for; matrix products, arithmetic and copies ran while one was open for 3% of the time, Pallas kernels for 12%

profile of v1, /device:TPU:0, one launch (start us, length us, event | category | flops | bytes accessed | tf_op | source)
XLA Modules:
  0.0 313.4 jit_solution(12893048163654570107)
XLA Ops:
  2.5 5.1 %collective-permute-start.2 = (bf16[2,16,1152]{2,1,0:T(8,128)(2,1)S(1)}, bf16[2,16,1152]{2,1,0:T(8,128)(2,1)S(1)}, u32[]{:S(2)}, u32[]{:S(2)}) collective-permute-start(bf16[2,16,1152]{2,1,0:T(8,128)(2,1)S(1)} %get-tuple-element.159), channel_id=1, source_target_pairs={{0,24},{8,16},{16,8},{24,0},{1,25},{9,17},{17,9},{25,1},{2,26},{10... | collective-permute-start | bytes 221192 | tf_op jit(solution)/shard_map/ppermute | solution.py:41
  15.5 5.5 %all-to-all-start = ((bf16[8,128,512]{2,1,0:T(8,128)(2,1)}), bf16[8,128,512]{2,1,0:T(8,128)(2,1)S(1)}, u32[]{:S(2)}, u32[]{:S(2)}) async-start(bf16[8,128,512]{2,1,0:T(8,128)(2,1)} %after.10), calls=%async_computation | async-start | bytes 2097152 | tf_op jit(solution)/shard_map/all_to_all | solution.py:854
  24.6 4.1 %collective-permute-done.5.refs_3_.refs_4_ = bf16[64,1024]{1,0:T(8,128)(2,1)S(1)} collective-permute-done((bf16[64,1024]{1,0:T(8,128)(2,1)S(1)}, bf16[64,1024]{1,0:T(8,128)(2,1)S(1)}, u32[]{:S(2)}, u32[]{:S(2)}) %collective-permute-start.5) | collective-permute-done | bytes 131104 | tf_op jit(solution)/shard_map/ppermute | solution.py:41
  28.7 9.3 %collective-permute-done.4.refs_2_.refs_3_ = bf16[64,1024]{1,0:T(8,128)(2,1)S(1)} collective-permute-done((bf16[64,1024]{1,0:T(8,128)(2,1)S(1)}, bf16[64,1024]{1,0:T(8,128)(2,1)S(1)}, u32[]{:S(2)}, u32[]{:S(2)}) %collective-permute-start.4) | collective-permute-done | bytes 131104 | tf_op jit(solution)/shard_map/ppermute | solution.py:41
  38.1 6.0 %split_weights.2.refs_1_.refs_0_ = bf16[8,128,1536]{2,1,0:T(8,128)(2,1)S(1)} custom-call(f32[12288,128]{1,0:T(8,128)} %bitcast.89), custom_call_target="tpu_custom_call" | custom-call | flops 1572864 | bytes 9437184 | tf_op jit(solution)/shard_map/split_weights/pallas_call | solution.py:816
  48.7 5.2 %collective-permute-start.8 = (bf16[128,384]{1,0:T(8,128)(2,1)S(1)}, bf16[128,384]{1,0:T(8,128)(2,1)S(1)}, u32[]{:S(2)}, u32[]{:S(2)}) collective-permute-start(bf16[128,384]{1,0:T(8,128)(2,1)S(1)} %get-tuple-element.86), channel_id=1, source_target_pairs={{0,16},{8,24},{16,0},{24,8},{1,17},{9,25},{17,1},{25,9},{2,18},{10... | collective-permute-start | bytes 294920 | tf_op jit(solution)/shard_map/ppermute | solution.py:41
  53.9 7.8 %collective-permute-done.8.refs_2_ = bf16[128,384]{1,0:T(8,128)(2,1)S(1)} collective-permute-done((bf16[128,384]{1,0:T(8,128)(2,1)S(1)}, bf16[128,384]{1,0:T(8,128)(2,1)S(1)}, u32[]{:S(2)}, u32[]{:S(2)}) %collective-permute-start.8) | collective-permute-done | bytes 98336 | tf_op jit(solution)/shard_map/ppermute | solution.py:41
  73.0 4.6 %all-to-all-start.1 = ((bf16[8,128,1536]{2,1,0:T(8,128)(2,1)}), bf16[8,128,1536]{2,1,0:T(8,128)(2,1)}, u32[]{:S(2)}, u32[]{:S(2)}) async-start(bf16[8,128,1536]{2,1,0:T(8,128)(2,1)} %after.11), calls=%async_computation.1 | async-start | bytes 6291456 | tf_op jit(solution)/shard_map/all_to_all | solution.py:854
  88.7 25.3 %collective-permute-done.15.refs_2_ = bf16[64,1024]{1,0:T(8,128)(2,1)S(1)} collective-permute-done((bf16[64,1024]{1,0:T(8,128)(2,1)S(1)}, bf16[64,1024]{1,0:T(8,128)(2,1)S(1)}, u32[]{:S(2)}, u32[]{:S(2)}) %collective-permute-start.15) | collective-permute-done | bytes 131104 | tf_op jit(solution)/shard_map/ppermute | solution.py:41
  119.0 4.9 %collective-permute-done.19.refs_3_ = bf16[64,1024]{1,0:T(8,128)(2,1)S(1)} collective-permute-done((bf16[64,1024]{1,0:T(8,128)(2,1)S(1)}, bf16[64,1024]{1,0:T(8,128)(2,1)S(1)}, u32[]{:S(2)}, u32[]{:S(2)}) %collective-permute-start.19) | collective-permute-done | bytes 131104 | tf_op jit(solution)/shard_map/ppermute | solution.py:41
  123.9 6.5 %collective-permute-done.18.refs_2_ = bf16[64,1024]{1,0:T(8,128)(2,1)S(1)} collective-permute-done((bf16[64,1024]{1,0:T(8,128)(2,1)S(1)}, bf16[64,1024]{1,0:T(8,128)(2,1)S(1)}, u32[]{:S(2)}, u32[]{:S(2)}) %collective-permute-start.18) | collective-permute-done | bytes 131104 | tf_op jit(solution)/shard_map/ppermute | solution.py:41
  132.6 14.5 %all-to-all-done.1 = bf16[8,128,1536]{2,1,0:T(8,128)(2,1)} async-done(((bf16[8,128,1536]{2,1,0:T(8,128)(2,1)}), bf16[8,128,1536]{2,1,0:T(8,128)(2,1)}, u32[]{:S(2)}, u32[]{:S(2)}) %all-to-all-start.1) | async-done | bytes 3145760 | tf_op jit(solution)/shard_map/all_to_all | solution.py:854
  147.0 5.1 %ffn_kernel.1 = (bf16[512,512]{1,0:T(8,128)(2,1)S(1)}, bf16[512,1024]{1,0:T(8,128)(2,1)S(1)}, bf16[256,1024]{1,0:T(8,128)(2,1)S(1)}, bf16[256,1024]{1,0:T(8,128)(2,1)S(1)}) custom-call(bf16[512,1024]{1,0:T(8,128)(2,1)S(1)} %stack_kernel.8.x_ref.refs_0_, bf16[512,1024]{1,0:T(8,128)(2,1)S(1)} %stack_kernel.10.g_ref.refs_0_, bf16[1024,1536]{1,0:T(8,128)(2,1)} %bitcast.15.w_ref), custom_call_target="tpu_custom_call" | custom-call | flops 2684354560 | bytes 7864320 | tf_op jit(solution)/shard_map/ffn_kernel/pallas_call | solution.py:177
  155.6 7.6 %all-to-all-start.2 = ((bf16[8,128,1024]{2,1,0:T(8,128)(2,1)}), bf16[8,128,1024]{2,1,0:T(8,128)(2,1)}, u32[]{:S(2)}, u32[]{:S(2)}) async-start(bf16[8,128,1024]{2,1,0:T(8,128)(2,1)} %bitcast.16), calls=%async_computation.2 | async-start | bytes 4194304 | tf_op jit(solution)/shard_map/all_to_all | solution.py:862
  175.2 12.7 %collective-permute-done.27.refs_2_ = bf16[64,1024]{1,0:T(8,128)(2,1)S(1)} collective-permute-done((bf16[64,1024]{1,0:T(8,128)(2,1)S(1)}, bf16[64,1024]{1,0:T(8,128)(2,1)S(1)}, u32[]{:S(2)}, u32[]{:S(2)}) %collective-permute-start.27) | collective-permute-done | bytes 131104 | tf_op jit(solution)/shard_map/ppermute | solution.py:41
  188.9 3.5 %collective-permute-start.31 = (bf16[64,1024]{1,0:T(8,128)(2,1)S(1)}, bf16[64,1024]{1,0:T(8,128)(2,1)S(1)}, u32[]{:S(2)}, u32[]{:S(2)}) collective-permute-start(bf16[64,1024]{1,0:T(8,128)(2,1)S(1)} %get-tuple-element.114.refs_0_.refs_1_), channel_id=1, source_target_pairs={{0,6},{2,4},{4,2},{6,0},{1,7},{3,5},{5,3},{7,1},{8,14},{10,12},{12... | collective-permute-start | bytes 393224 | tf_op jit(solution)/shard_map/ppermute | solution.py:41
  194.5 4.4 %collective-permute-done.31.refs_3_.refs_4_ = bf16[64,1024]{1,0:T(8,128)(2,1)S(1)} collective-permute-done((bf16[64,1024]{1,0:T(8,128)(2,1)S(1)}, bf16[64,1024]{1,0:T(8,128)(2,1)S(1)}, u32[]{:S(2)}, u32[]{:S(2)}) %collective-permute-start.31) | collective-permute-done | bytes 131104 | tf_op jit(solution)/shard_map/ppermute | solution.py:41
  224.1 4.0 %collective-permute-done.38.refs_3_.refs_4_ = bf16[128,384]{1,0:T(8,128)(2,1)S(1)} collective-permute-done((bf16[128,384]{1,0:T(8,128)(2,1)S(1)}, bf16[128,384]{1,0:T(8,128)(2,1)S(1)}, u32[]{:S(2)}, u32[]{:S(2)}) %collective-permute-start.38) | collective-permute-done | bytes 98336 | tf_op jit(solution)/shard_map/ppermute | solution.py:41
  228.7 5.0 %all-to-all-start.3 = ((bf16[8,128,512]{2,1,0:T(8,128)(2,1)}), bf16[8,128,512]{2,1,0:T(8,128)(2,1)S(1)}, u32[]{:S(2)}, u32[]{:S(2)}) async-start(bf16[8,128,512]{2,1,0:T(8,128)(2,1)} %after.15), calls=%async_computation.3 | async-start | bytes 2097152 | tf_op jit(solution)/shard_map/all_to_all | solution.py:862
  234.8 5.7 %attn_grads_kernel.1 = (bf16[256,1024]{1,0:T(8,128)(2,1)}, bf16[256,1024]{1,0:T(8,128)(2,1)}, bf16[1024,512]{1,0:T(8,128)(2,1)}, f32[3,1024]{1,0:T(4,128)}) custom-call(s32[1]{0:T(128)} %after.12.me_ref, bf16[128,384]{1,0:T(8,128)(2,1)} %copy-done.19, bf16[128,384]{1,0:T(8,128)(2,1)} %copy-done.60, bf16[128,384]{1,0:T(8,128)(2,1)} %copy-done.61, ...), custom_call_target="tpu_custom_call" | custom-call | flops 939524096 | bytes 5788160 | tf_op jit(solution)/shard_map/attn_grads_kernel/pallas_call | solution.py:177
  250.8 7.0 %collective-permute-done.56 = f32[3,1024]{1,0:T(4,128)S(1)} collective-permute-done((f32[3,1024]{1,0:T(4,128)S(1)}, f32[3,1024]{1,0:T(4,128)S(1)}, u32[]{:S(2)}, u32[]{:S(2)}) %collective-permute-start.56) | collective-permute-done | bytes 12320 | tf_op jit(solution)/shard_map/ppermute | solution.py:41
  277.0 4.1 %all-to-all-start.4 = ((bf16[8,128,512]{2,1,0:T(8,128)(2,1)}), bf16[8,128,512]{2,1,0:T(8,128)(2,1)S(1)}, u32[]{:S(2)}, u32[]{:S(2)}) async-start(bf16[8,128,512]{2,1,0:T(8,128)(2,1)} %after.17), calls=%async_computation.4 | async-start | bytes 2097152 | tf_op jit(solution)/shard_map/all_to_all | solution.py:862
  287.1 15.1 %adamw.2 = (f32[12288,128]{1,0:T(8,128)}, f32[12288,128]{1,0:T(8,128)}, f32[12288,128]{1,0:T(8,128)}) custom-call(f32[3,1024]{1,0:T(4,128)S(1)} %copy-done.14, bf16[8,128,1024]{2,1,0:T(8,128)(2,1)} %all-to-all-done.2.refs_1_.refs_0_, bf16[8,128,512]{2,1,0:T(8,128)(2,1)S(1)} %copy-done.3, f32[12288,128]{1,0:T(8,128)} %bitcast.90, f32[12288,128]{1,0:T(8,128)} %bitcast.92, ...), custom_call_target="tpu_custom_call" | custom-call | flops 31457280 | bytes 40894464 | tf_op jit(solution)/shard_map/adamw/pallas_call | solution.py:966
  305.6 6.7 %adamw.3 = (f32[4096,128]{1,0:T(8,128)}, f32[4096,128]{1,0:T(8,128)}, f32[4096,128]{1,0:T(8,128)}) custom-call(f32[3,1024]{1,0:T(4,128)S(1)} %copy-done.15, bf16[8,128,512]{2,1,0:T(8,128)(2,1)S(1)} %all-to-all-done.4.refs_0_, f32[4096,128]{1,0:T(8,128)} %bitcast.87, f32[4096,128]{1,0:T(8,128)} %bitcast.95, f32[4096,128]{1,0:T(8,128)} %bitcast.96), custom_call_target="tpu_custom_call" | custom-call | flops 10485760 | bytes 13631488 | tf_op jit(solution)/shard_map/adamw/pallas_call | solution.py:966
  (292 shorter events, 130.3 us)
Async XLA Ops:
  15.5 30.8 %all-to-all-start = ((bf16[8,128,512]{2,1,0:T(8,128)(2,1)}), bf16[8,128,512]{2,1,0:T(8,128)(2,1)S(1)}, u32[]{:S(2)}, u32[]{:S(2)}) async-start(bf16[8,128,512]{2,1,0:T(8,128)(2,1)} %after.10), calls=%async_computation | async-start | bytes 2097152 | tf_op jit(solution)/shard_map/all_to_all | solution.py:854
  23.9 14.0 %collective-permute-start.4 = (bf16[64,1024]{1,0:T(8,128)(2,1)S(1)}, bf16[64,1024]{1,0:T(8,128)(2,1)S(1)}, u32[]{:S(2)}, u32[]{:S(2)}) collective-permute-start(bf16[64,1024]{1,0:T(8,128)(2,1)S(1)} %copy-done.8), channel_id=1, source_target_pairs={{0,4},{2,6},{4,0},{6,2},{1,5},{3,7},{5,1},{7,3},{8,12},{10,14},{12... | collective-permute-start | bytes 393224 | tf_op jit(solution)/shard_map/ppermute | solution.py:41
  24.0 13.9 %collective-permute-start.3 = (bf16[64,1024]{1,0:T(8,128)(2,1)S(1)}, bf16[64,1024]{1,0:T(8,128)(2,1)S(1)}, u32[]{:S(2)}, u32[]{:S(2)}) collective-permute-start(bf16[64,1024]{1,0:T(8,128)(2,1)S(1)} %copy-done.8), channel_id=1, source_target_pairs={{0,2},{2,0},{4,6},{6,4},{1,3},{3,1},{5,7},{7,5},{8,10},{10,8},{12,... | collective-permute-start | bytes 393224 | tf_op jit(solution)/shard_map/ppermute | solution.py:41
  48.7 13.0 %collective-permute-start.8 = (bf16[128,384]{1,0:T(8,128)(2,1)S(1)}, bf16[128,384]{1,0:T(8,128)(2,1)S(1)}, u32[]{:S(2)}, u32[]{:S(2)}) collective-permute-start(bf16[128,384]{1,0:T(8,128)(2,1)S(1)} %get-tuple-element.86), channel_id=1, source_target_pairs={{0,16},{8,24},{16,0},{24,8},{1,17},{9,25},{17,1},{25,9},{2,18},{10... | collective-permute-start | bytes 294920 | tf_op jit(solution)/shard_map/ppermute | solution.py:41
  73.0 74.0 %all-to-all-start.1 = ((bf16[8,128,1536]{2,1,0:T(8,128)(2,1)}), bf16[8,128,1536]{2,1,0:T(8,128)(2,1)}, u32[]{:S(2)}, u32[]{:S(2)}) async-start(bf16[8,128,1536]{2,1,0:T(8,128)(2,1)} %after.11), calls=%async_computation.1 | async-start | bytes 6291456 | tf_op jit(solution)/shard_map/all_to_all | solution.py:854
  82.3 31.6 %collective-permute-start.15 = (bf16[64,1024]{1,0:T(8,128)(2,1)S(1)}, bf16[64,1024]{1,0:T(8,128)(2,1)S(1)}, u32[]{:S(2)}, u32[]{:S(2)}) collective-permute-start(bf16[64,1024]{1,0:T(8,128)(2,1)S(1)} %get-tuple-element.96), channel_id=1, source_target_pairs={{0,4},{2,6},{4,0},{6,2},{1,5},{3,7},{5,1},{7,3},{8,12},{10,14},{12... | collective-permute-start | bytes 393224 | tf_op jit(solution)/shard_map/ppermute | solution.py:41
  84.2 29.8 %collective-permute-start.16 = (bf16[64,1024]{1,0:T(8,128)(2,1)S(1)}, bf16[64,1024]{1,0:T(8,128)(2,1)S(1)}, u32[]{:S(2)}, u32[]{:S(2)}) collective-permute-start(bf16[64,1024]{1,0:T(8,128)(2,1)S(1)} %get-tuple-element.97), channel_id=1, source_target_pairs={{0,6},{2,4},{4,2},{6,0},{1,7},{3,5},{5,3},{7,1},{8,14},{10,12},{12... | collective-permute-start | bytes 393224 | tf_op jit(solution)/shard_map/ppermute | solution.py:41
  84.3 34.0 %collective-permute-start.23 = (bf16[64,1024]{1,0:T(8,128)(2,1)S(1)}, bf16[64,1024]{1,0:T(8,128)(2,1)S(1)}, u32[]{:S(2)}, u32[]{:S(2)}) collective-permute-start(bf16[64,1024]{1,0:T(8,128)(2,1)S(1)} %get-tuple-element.101.refs_0_), channel_id=1, source_target_pairs={{0,6},{2,4},{4,2},{6,0},{1,7},{3,5},{5,3},{7,1},{8,14},{10,12},{12... | collective-permute-start | bytes 393224 | tf_op jit(solution)/shard_map/ppermute | solution.py:41
  87.1 31.8 %collective-permute-start.22 = (bf16[64,1024]{1,0:T(8,128)(2,1)S(1)}, bf16[64,1024]{1,0:T(8,128)(2,1)S(1)}, u32[]{:S(2)}, u32[]{:S(2)}) collective-permute-start(bf16[64,1024]{1,0:T(8,128)(2,1)S(1)} %get-tuple-element.101.refs_0_), channel_id=1, source_target_pairs={{0,4},{2,6},{4,0},{6,2},{1,5},{3,7},{5,1},{7,3},{8,12},{10,14},{12... | collective-permute-start | bytes 393224 | tf_op jit(solution)/shard_map/ppermute | solution.py:41
  87.3 31.6 %collective-permute-start.21 = (bf16[64,1024]{1,0:T(8,128)(2,1)S(1)}, bf16[64,1024]{1,0:T(8,128)(2,1)S(1)}, u32[]{:S(2)}, u32[]{:S(2)}) collective-permute-start(bf16[64,1024]{1,0:T(8,128)(2,1)S(1)} %get-tuple-element.101.refs_0_), channel_id=1, source_target_pairs={{0,2},{2,0},{4,6},{6,4},{1,3},{3,1},{5,7},{7,5},{8,10},{10,8},{12,... | collective-permute-start | bytes 393224 | tf_op jit(solution)/shard_map/ppermute | solution.py:41
  118.3 12.1 %collective-permute-start.18 = (bf16[64,1024]{1,0:T(8,128)(2,1)S(1)}, bf16[64,1024]{1,0:T(8,128)(2,1)S(1)}, u32[]{:S(2)}, u32[]{:S(2)}) collective-permute-start(bf16[64,1024]{1,0:T(8,128)(2,1)S(1)} %get-tuple-element.100.refs_0_), channel_id=1, source_target_pairs={{0,4},{2,6},{4,0},{6,2},{1,5},{3,7},{5,1},{7,3},{8,12},{10,14},{12... | collective-permute-start | bytes 393224 | tf_op jit(solution)/shard_map/ppermute | solution.py:41
  118.3 12.1 %collective-permute-start.17 = (bf16[64,1024]{1,0:T(8,128)(2,1)S(1)}, bf16[64,1024]{1,0:T(8,128)(2,1)S(1)}, u32[]{:S(2)}, u32[]{:S(2)}) collective-permute-start(bf16[64,1024]{1,0:T(8,128)(2,1)S(1)} %get-tuple-element.100.refs_0_), channel_id=1, source_target_pairs={{0,2},{2,0},{4,6},{6,4},{1,3},{3,1},{5,7},{7,5},{8,10},{10,8},{12,... | collective-permute-start | bytes 393224 | tf_op jit(solution)/shard_map/ppermute | solution.py:41
  118.9 11.7 %collective-permute-start.24 = (bf16[256,1024]{1,0:T(8,128)(2,1)S(1)}, bf16[256,1024]{1,0:T(8,128)(2,1)S(1)}, u32[]{:S(2)}, u32[]{:S(2)}) collective-permute-start(bf16[256,1024]{1,0:T(8,128)(2,1)S(1)} %stack_kernel.9), channel_id=1, source_target_pairs={{0,1},{1,0},{2,3},{3,2},{4,5},{5,4},{6,7},{7,6},{8,9},{9,8},{10,11... | collective-permute-start | bytes 1572872 | tf_op jit(solution)/shard_map/ppermute | solution.py:41
  155.6 73.2 %all-to-all-start.2 = ((bf16[8,128,1024]{2,1,0:T(8,128)(2,1)}), bf16[8,128,1024]{2,1,0:T(8,128)(2,1)}, u32[]{:S(2)}, u32[]{:S(2)}) async-start(bf16[8,128,1024]{2,1,0:T(8,128)(2,1)} %bitcast.16), calls=%async_computation.2 | async-start | bytes 4194304 | tf_op jit(solution)/shard_map/all_to_all | solution.py:862
  167.5 20.5 %collective-permute-start.27 = (bf16[64,1024]{1,0:T(8,128)(2,1)S(1)}, bf16[64,1024]{1,0:T(8,128)(2,1)S(1)}, u32[]{:S(2)}, u32[]{:S(2)}) collective-permute-start(bf16[64,1024]{1,0:T(8,128)(2,1)S(1)} %get-tuple-element.110), channel_id=1, source_target_pairs={{0,4},{2,6},{4,0},{6,2},{1,5},{3,7},{5,1},{7,3},{8,12},{10,14},{12... | collective-permute-start | bytes 393224 | tf_op jit(solution)/shard_map/ppermute | solution.py:41
  169.5 18.5 %collective-permute-start.28 = (bf16[64,1024]{1,0:T(8,128)(2,1)S(1)}, bf16[64,1024]{1,0:T(8,128)(2,1)S(1)}, u32[]{:S(2)}, u32[]{:S(2)}) collective-permute-start(bf16[64,1024]{1,0:T(8,128)(2,1)S(1)} %get-tuple-element.111), channel_id=1, source_target_pairs={{0,6},{2,4},{4,2},{6,0},{1,7},{3,5},{5,3},{7,1},{8,14},{10,12},{12... | collective-permute-start | bytes 393224 | tf_op jit(solution)/shard_map/ppermute | solution.py:41
  203.3 17.2 %collective-permute-start.44 = (bf16[64,1024]{1,0:T(8,128)(2,1)S(1)}, bf16[64,1024]{1,0:T(8,128)(2,1)S(1)}, u32[]{:S(2)}, u32[]{:S(2)}) collective-permute-start(bf16[64,1024]{1,0:T(8,128)(2,1)S(1)} %get-tuple-element.136), channel_id=1, source_target_pairs={{0,2},{2,0},{4,6},{6,4},{1,3},{3,1},{5,7},{7,5},{8,10},{10,8},{12,... | collective-permute-start | bytes 393224 | tf_op jit(solution)/shard_map/ppermute | solution.py:41
  228.7 43.7 %all-to-all-start.3 = ((bf16[8,128,512]{2,1,0:T(8,128)(2,1)}), bf16[8,128,512]{2,1,0:T(8,128)(2,1)S(1)}, u32[]{:S(2)}, u32[]{:S(2)}) async-start(bf16[8,128,512]{2,1,0:T(8,128)(2,1)} %after.15), calls=%async_computation.3 | async-start | bytes 2097152 | tf_op jit(solution)/shard_map/all_to_all | solution.py:862
  244.5 13.9 %collective-permute-start.40 = (bf16[64,1024]{1,0:T(8,128)(2,1)S(1)}, bf16[64,1024]{1,0:T(8,128)(2,1)S(1)}, u32[]{:S(2)}, u32[]{:S(2)}) collective-permute-start(bf16[64,1024]{1,0:T(8,128)(2,1)S(1)} %get-tuple-element.132), channel_id=1, source_target_pairs={{0,2},{2,0},{4,6},{6,4},{1,3},{3,1},{5,7},{7,5},{8,10},{10,8},{12,... | collective-permute-start | bytes 393224 | tf_op jit(solution)/shard_map/ppermute | solution.py:41
  246.3 12.1 %collective-permute-start.41 = (bf16[64,1024]{1,0:T(8,128)(2,1)S(1)}, bf16[64,1024]{1,0:T(8,128)(2,1)S(1)}, u32[]{:S(2)}, u32[]{:S(2)}) collective-permute-start(bf16[64,1024]{1,0:T(8,128)(2,1)S(1)} %get-tuple-element.133), channel_id=1, source_target_pairs={{0,4},{2,6},{4,0},{6,2},{1,5},{3,7},{5,1},{7,3},{8,12},{10,14},{12... | collective-permute-start | bytes 393224 | tf_op jit(solution)/shard_map/ppermute | solution.py:41
  277.0 27.8 %all-to-all-start.4 = ((bf16[8,128,512]{2,1,0:T(8,128)(2,1)}), bf16[8,128,512]{2,1,0:T(8,128)(2,1)S(1)}, u32[]{:S(2)}, u32[]{:S(2)}) async-start(bf16[8,128,512]{2,1,0:T(8,128)(2,1)} %after.17), calls=%async_computation.4 | async-start | bytes 2097152 | tf_op jit(solution)/shard_map/all_to_all | solution.py:862
  283.7 19.1 %collective-permute-start.52 = (bf16[4,2,16,1024]{3,2,1,0:T(8,128)(2,1)S(1)}, bf16[4,2,16,1024]{3,2,1,0:T(8,128)(2,1)S(1)}, u32[]{:S(2)}, u32[]{:S(2)}) collective-permute-start(bf16[4,2,16,1024]{3,2,1,0:T(8,128)(2,1)S(1)} %by_position_kernel.1.refs_0_), channel_id=1, source_target_pairs={{0,3},{1,2},{2,1},{3,0},{4,7},{5,6},{6,5},{7,4},{8,11},{9,10},{10,... | collective-permute-start | bytes 786440 | tf_op jit(solution)/shard_map/ppermute | solution.py:41
  283.8 19.0 %collective-permute-start.51 = (bf16[4,2,16,1024]{3,2,1,0:T(8,128)(2,1)S(1)}, bf16[4,2,16,1024]{3,2,1,0:T(8,128)(2,1)S(1)}, u32[]{:S(2)}, u32[]{:S(2)}) collective-permute-start(bf16[4,2,16,1024]{3,2,1,0:T(8,128)(2,1)S(1)} %by_position_kernel.1.refs_0_), channel_id=1, source_target_pairs={{0,2},{1,3},{2,0},{3,1},{4,6},{5,7},{6,4},{7,5},{8,10},{9,11},{10,... | collective-permute-start | bytes 786440 | tf_op jit(solution)/shard_map/ppermute | solution.py:41
  284.4 18.4 %collective-permute-start.50 = (bf16[4,2,16,1024]{3,2,1,0:T(8,128)(2,1)S(1)}, bf16[4,2,16,1024]{3,2,1,0:T(8,128)(2,1)S(1)}, u32[]{:S(2)}, u32[]{:S(2)}) collective-permute-start(bf16[4,2,16,1024]{3,2,1,0:T(8,128)(2,1)S(1)} %by_position_kernel.1.refs_0_), channel_id=1, source_target_pairs={{0,1},{1,0},{2,3},{3,2},{4,5},{5,4},{6,7},{7,6},{8,9},{9,8},{10,11... | collective-permute-start | bytes 786440 | tf_op jit(solution)/shard_map/ppermute | solution.py:41
  (107 other events, 1068.5 us)

commit v2 on v1

--- a/solution.py
+++ b/solution.py
@@ -459,50 +459,66 @@
 
 def finish_kernel(depth, chips, me_ref, *refs):
     terms, ffn_terms = refs[:chips], refs[chips : 2 * chips]
-    rows_ref, grad_ref, hidden_ref, mask_ref, gain_ref = refs[2 * chips : 2 * chips + 5]
-    outs = refs[2 * chips + 5 : -2]
-    output, input_grad = refs[-2:]
+    totals, refs = refs[2 * chips : 2 * chips + 2], refs[2 * chips + 2 :]
+    rows_ref, grad_ref, hidden_ref, mask_ref, gain_ref = refs[:5]
+    outs, (output, input_grad) = refs[5:-2], refs[-2:]
     unit_rows, inv_rms, _ = rms_forward(rows_ref[...], gain_ref[...])
     grad = rms_backward(sum_refs(terms), unit_rows, inv_rms, gain_ref[...])
     output[...] = (hidden_ref[...] + mask_ref[:, :1] * sum_refs(ffn_terms)).astype(BF)
     input_grad[...] = (grad_ref[...] + grad).astype(BF)
-    share = outs[0].shape[1]
+    total = totals[0][...] + totals[1][...]
+    high = total.astype(BF)
+    low = (total - high.astype(F32)).astype(BF)
+    share, model = outs[0].shape[1:]
+    count = total.shape[0]
     for t, ref in enumerate(outs):
         at = pl.ds(pl.multiple_of((me_ref[0] ^ t) * share, share), share)
         ref[0] = output[at, :]
         ref[1] = input_grad[at, :]
-
-
-def finish_rows(terms, ffn_terms, rows, grad_rows, hidden, mask, gain, me, depth):
+        ref[2] = jnp.zeros((share, model), BF)
+        ref[2, :count, :] = high
+        ref[2, 8 : 8 + count, :] = low
+
+
+def finish_rows(terms, ffn_terms, totals, rows, grad_rows, hidden, mask, gain, me, depth):
     tokens, model = rows.shape
     return vmem_call(
         functools.partial(finish_kernel, depth, len(terms)),
-        [sds((2, tokens // depth, model), BF)] * depth,
+        [sds((3, tokens // depth, model), BF)] * depth,
         *terms,
         *ffn_terms,
+        *totals,
         rows,
         grad_rows,
         hidden,
         mask,
         gain[None],
         index=me,
+        scratch=[pltpu.VMEM((tokens, model), BF)] * 2,
         vmem=56,
-        scratch=[pltpu.VMEM((tokens, model), BF)] * 2,
     )
 
 
 def by_position_kernel(depth, me_ref, *refs):
+    rows_ref, total_ref = refs[depth:]
+    count = total_ref.shape[0]
+    parts = []
     for t in range(depth):
-        refs[depth][me_ref[0] ^ t] = refs[t][...]
-
-
-def by_position(got, me):
+        rows_ref[me_ref[0] ^ t] = refs[t][:2]
+        high, low = refs[t][2, :count, :], refs[t][2, 8 : 8 + count, :]
+        parts.append(high.astype(F32) + low.astype(F32))
+    total_ref[...] = tree_sum(parts)
+
+
+def by_position(got, me, count):
+    depth = len(got)
+    _, share, model = got[0].shape
     return vmem_call(
-        functools.partial(by_position_kernel, len(got)),
-        [sds((len(got),) + got[0].shape, got[0].dtype)],
+        functools.partial(by_position_kernel, depth),
+        [sds((depth, 2, share, model), BF), sds((count, model), F32)],
         *got,
         index=me,
-    )[0]
+    )
 
 
 def whole_frames_kernel(parts, me_ref, *refs):
@@ -695,8 +711,8 @@
 
 def attn_grads_kernel(depth, width, me_ref, *refs):
     got = refs[:depth]
-    w_ref, normed_ref, grad_ref, context_ref, gain_ref, gain2_ref, square_ref = refs[depth : depth + 7]
-    near_ref, far_ref, chunk_ref, total_ref, by_chunk, grads = refs[depth + 7 :]
+    w_ref, normed_ref, gain_ref, gain2_ref, square_ref = refs[depth : depth + 5]
+    near_ref, far_ref, chunk_ref, total_ref, by_chunk, grads = refs[depth + 5 :]
     for t in range(depth):
         by_chunk[me_ref[0] ^ t] = got[t][...]
     rows = by_chunk.shape[1]
@@ -712,19 +728,17 @@
         total = total + jnp.sum(terms * normed_ref[here, :].astype(F32), axis=0, keepdims=True)
     total_ref[0:1, :] = total / gain_ref[...]
     total_ref[1:2, :] = gain2_ref[...]
+    chunk = mm_tn(normed_ref[...], grads[...])
+    chunk_ref[...] = chunk.astype(BF)
+    column = jnp.sum(chunk * chunk, axis=0, keepdims=True)
     squares = square_ref[...]
-    for first, left, right in ((0, normed_ref, grads), (3 * width, grad_ref, context_ref)):
-        chunk = mm_tn(left[...], right[...])
-        last = first + chunk.shape[1]
-        chunk_ref[:, first:last] = chunk.astype(BF)
-        column = jnp.sum(chunk * chunk, axis=0, keepdims=True)
-        for j in range(0, last - first, 128):
-            squares = squares + column[:, j : j + 128]
+    for j in range(0, 3 * width, 128):
+        squares = squares + column[:, j : j + 128]
     total_ref[2:3, :] = jnp.zeros(gain_ref.shape, F32)
     total_ref[2:3, :128] = squares
 
 
-def attn_grads(got, attn_w, normed, grad_attn, context, gain, gain_part2, squares, me):
+def attn_grads(got, attn_w, normed, gain, gain_part2, squares, me):
     depth = len(got)
     rows, wide = got[0].shape
     width = wide // 3
@@ -732,26 +746,24 @@
     model = attn_w.shape[0]
     if lax.axis_size("rf") > 1 or width % 128:
         grads, near, far, gain_part1 = qkv_back(got, attn_w, normed, gain, width, me)
-        chunks, more = weight_grads((normed, grads, 0, wide), (grad_attn, context, 0, width))
+        chunks, more = weight_grads((normed, grads, 0, wide))
         squares = jnp.pad(squares + more, ((0, 0), (0, model - 128)))
         return near, far, chunks, jnp.concatenate([gain_part1, gain_part2, squares], 0)
     near, far, chunks, total = vmem_call(
         functools.partial(attn_grads_kernel, depth, width),
-        [sds((tokens // 2, model), BF)] * 2 + [sds((model, 4 * width), BF), sds((3, model), F32)],
+        [sds((tokens // 2, model), BF)] * 2 + [sds((model, wide), BF), sds((3, model), F32)],
         *got,
         attn_w,
         normed,
-        grad_attn,
-        context,
         gain[None],
         gain_part2,
         squares,
         index=me,
         scratch=[pltpu.VMEM((depth, rows, wide), BF), pltpu.VMEM((tokens, wide), BF)],
-        flops=14 * tokens * width * model,
+        flops=12 * tokens * width * model,
         vmem=56,
     )
-    return near, far, chunks.reshape(axis_total(OWNERS), -1, 4 * width), total
+    return near, far, chunks.reshape(axis_total(OWNERS), -1, wide), total
 
 
 OWNERS = ("pz", "rs")
@@ -775,6 +787,9 @@
     for number, piece in enumerate(pieces):
         lane = 0
         for k, first, count in piece:
+            if k is None:
+                lane += 128 * count
+                continue
             for t in range(first, first + count):
                 for part in range(parts):
                     for p in range(depth):
@@ -1020,9 +1035,9 @@
     normed1_pieces = gather_pieces(normed1_rows)
     grad_ffn = stack_rows(gather_pieces(masked))
 
-    normed1, qkv = project(normed1_pieces, attn_w, width, after(me.reshape(1), ffn_low), depth)
+    normed1, qkv = project(normed1_pieces, attn_w, width, me, depth)
     qkv = swap_parts(qkv, positions)
-    context = swap_parts(attend_pieces(qkv, me), positions)
+    context = swap_parts(attend_pieces(qkv, after(me.reshape(1), ffn_low)), positions)
     ffn_w = to_planes(after(ffn_low, *context))
     context, near, far = attn_out_terms(context, attn_w, me)
     hidden_in, normed2_rows = join_rows(scatter_pieces(near, far), rows_in, mask, gain_ffn)
@@ -1031,28 +1046,25 @@
     acts, gate_up_grads, near, far = ffn_block(normed2, grad_ffn, ffn_w)
     terms = scatter_pieces(near, far)
     hidden = acts.shape[1]
-    pieces = [[(0, 0, per), (1, 0, per)], [(2, 0, per)]]
+    pieces = [[(0, 0, per), (1, 0, per)], [(2, 0, per), (None, 0, width // 128)]]
     chunks_a, squares_a = weight_grads((normed2, gate_up_grads, 0, 2 * hidden))
     owned_a = to_owners(chunks_a)
-    chunks_b, squares_b = weight_grads((grad_ffn, acts, 0, hidden))
-
     ffn_terms = mm_nt(acts, ffn_w[:, 2 * hidden :]).astype(BF)
 
     grad_hidden, masked, gain_part2 = norm_back(
-        terms, hidden_in, rows_grad, mask, gain_ffn, after(me.reshape(1), chunks_b, ffn_terms)
+        terms, hidden_in, rows_grad, mask, gain_ffn, after(me.reshape(1), ffn_terms)
     )
     grad_attn, grad_context = context_grads(gather_pieces(masked), attn_w, width, me, depth)
     grad_context = swap_parts(grad_context, positions)
     grad_qkv = swap_parts(attend_back_pieces(qkv, grad_context, me), positions)
     half = ffn_terms.shape[0] // 2
     ffn_terms = scatter_pieces(ffn_terms[:half], ffn_terms[half:])
+    chunks_b, squares_b = weight_grads((grad_ffn, acts, 0, hidden), (grad_attn, context, 0, width))
     owned_b = to_owners(after(chunks_b, *grad_qkv, *ffn_terms[1:]))
     near, far, attn_chunks, total = attn_grads(
         grad_qkv,
         attn_w,
         normed1,
-        grad_attn,
-        context,
         gain_attn,
         gain_part2,
         squares_a + squares_b,
@@ -1062,15 +1074,16 @@
 
     if lax.axis_size("rf") > 1:
         total = lax.psum(total, "rf")
-    total = all_sum(all_sum(total, mp_axes), ("rs",))
-    total = all_sum(after(total, *terms[1:]), positions)
+    total = all_sum(total, mp_axes)
+    totals = [total] + [hop(total, ("rs",), t) for t in range(1, lax.axis_size("rs"))]
+    if len(totals) != 2:
+        totals = [tree_sum(totals), jnp.zeros_like(total)]
     back = finish_rows(
-        terms, ffn_terms, rows_in, grad_hidden, hidden_in, mask, gain_attn, me, depth
-    )
-    back = swap_parts(back, positions)
-    attn_owned = to_owners(after(attn_chunks, total, owned_b, *back[1:]))
-
-    back = by_position(back, me)
+        terms, ffn_terms, totals, rows_in, grad_hidden, hidden_in, mask, gain_attn, me, depth
+    )
+
+    back, total = by_position(swap_parts(back, positions), me, total.shape[0])
+    attn_owned = to_owners(after(attn_chunks, total, owned_b))
     back = swap_parts([back] * axis_total(mp_axes), mp_axes)
     output, input_grad = whole_frames(back, linear_index(mp_axes))
 
@@ -1082,14 +1095,21 @@
     attn_state = [lanes_view(v) for v in (attn_weight, attn_first, attn_second)]
     ffn_new, _ = adamw_owned(ffn_state, [owned_a, owned_b], total, ffn_weight.shape, pieces)
     if width % 128:
-        grads = attn_owned.reshape(depth, lax.axis_size("rs"), -1, 4, width)
+        grads = jnp.concatenate([attn_owned, owned_b[:, :, hidden:]], -1)
+        grads = grads.reshape(depth, lax.axis_size("rs"), -1, 4, width)
         grads = grads.transpose(2, 3, 0, 1, 4).reshape(attn_weight.shape).astype(F32)
         attn_new = adamw_update(
             attn_weight, attn_first, attn_second, grads, clip_factor, WEIGHT_DECAY, LEARN_RATE
         )
     else:
+        tiles = width // 128
+        attn_pieces = [[(k, 0, tiles) for k in range(3)], [(None, 0, per), (3, 0, tiles)]]
         attn_new, _ = adamw_owned(
-            attn_state, [attn_owned], after(total, ffn_new[0], output), attn_weight.shape
+            attn_state,
+            [attn_owned, owned_b],
+            after(total, ffn_new[0], output),
+            attn_weight.shape,
+            attn_pieces,
         )
         attn_new = tuple(lanes_back(v, attn_weight.shape) for v in attn_new)
     ffn_new = tuple(lanes_back(v, ffn_weight.shape) for v in ffn_new)

time: 315 us -> 301 us (0.956)
  starting transfers between devices: 96.8 us -> 88.6 us
    ppermute x60 -> x57, waiting for transfers between devices: 109 us -> 102 us  [hop(): return lax.ppermute(value, axes, [(i, i ^ step) for i in range(n)])]
    all_to_all x2, waiting for transfers between devices: 14.5 us -> 21.5 us  [to_planes(): full = lax.all_to_all(low, OWNERS, 0, 0, tiled=True)]
    ppermute x60 -> x57, starting transfers between devices: 70 us -> 65.5 us  [hop(): return lax.ppermute(value, axes, [(i, i ^ step) for i in range(n)])]
    all_to_all x3, starting transfers between devices: 16.7 us -> 12.7 us  [to_owners(): return lax.all_to_all(chunks, OWNERS, 0, 0, tiled=True)]
    unnamed x132 -> x134, local copies, waits for them, and re-layouts: 21.5 us -> 20.3 us
  transfers between devices with their start and end apart: 65 -> 62, of which waited for: 24 -> 25; matrix products, arithmetic and copies ran while one was open for 3% -> 3% of each run, Pallas kernels for 12% -> 13%
where the time goes in v2:
time: 301 us; the launch traced here: 300 us
  waiting for transfers between devices  123 us (41%)
  starting transfers between devices  88.6 us (29%)
  Pallas kernels  55.2 us (18%)
  local copies, waits for them, and re-layouts  24.2 us (8%)
  between operations  3.44 us (1%)
    ppermute x57, waiting for transfers between devices, hop(): return lax.ppermute(value, axes, [(i, i ^ step) for i in range(n)])  102 us
    ppermute x57, starting transfers between devices, hop(): return lax.ppermute(value, axes, [(i, i ^ step) for i in range(n)])  65.5 us
    pallas_call x2, Pallas kernels, adamw_owned(): pl.pallas_call(functools.partial(adamw_kernel, (kinds, cols // 128, depth...  22 us
    all_to_all x2, waiting for transfers between devices, to_planes(): full = lax.all_to_all(low, OWNERS, 0, 0, tiled=True)  21.5 us
    pallas_call x23, Pallas kernels, vmem_call(): pl.pallas_call(kernel, out_shape=list(outs), in_specs=[pl.BlockSpec(memor...  21.1 us
    unnamed x134, local copies, waits for them, and re-layouts  20.3 us
    all_to_all x3, starting transfers between devices, to_owners(): return lax.all_to_all(chunks, OWNERS, 0, 0, tiled=True)  12.7 us
    all_to_all x2, starting transfers between devices, to_planes(): full = lax.all_to_all(low, OWNERS, 0, 0, tiled=True)  10.3 us
  transfers between devices with their start and end apart: 62, of which 25 were waited for; matrix products, arithmetic and copies ran while one was open for 3% of the time, Pallas kernels for 13%

profile of v2, /device:TPU:0, one launch (start us, length us, event | category | flops | bytes accessed | tf_op | source)
XLA Modules:
  0.0 300.0 jit_solution(14742550584562699718)
XLA Ops:
  2.5 5.1 %collective-permute-start.2 = (bf16[2,16,1152]{2,1,0:T(8,128)(2,1)S(1)}, bf16[2,16,1152]{2,1,0:T(8,128)(2,1)S(1)}, u32[]{:S(2)}, u32[]{:S(2)}) collective-permute-start(bf16[2,16,1152]{2,1,0:T(8,128)(2,1)S(1)} %get-tuple-element.163), channel_id=1, source_target_pairs={{0,24},{8,16},{16,8},{24,0},{1,25},{9,17},{17,9},{25,1},{2,26},{10... | collective-permute-start | bytes 221192 | tf_op jit(solution)/shard_map/ppermute | solution.py:41
  15.4 5.5 %all-to-all-start = ((bf16[8,128,512]{2,1,0:T(8,128)(2,1)}), bf16[8,128,512]{2,1,0:T(8,128)(2,1)S(1)}, u32[]{:S(2)}, u32[]{:S(2)}) async-start(bf16[8,128,512]{2,1,0:T(8,128)(2,1)} %after.9), calls=%async_computation | async-start | bytes 2097152 | tf_op jit(solution)/shard_map/all_to_all | solution.py:869
  24.5 4.1 %collective-permute-done.5.refs_3_.refs_4_ = bf16[64,1024]{1,0:T(8,128)(2,1)S(1)} collective-permute-done((bf16[64,1024]{1,0:T(8,128)(2,1)S(1)}, bf16[64,1024]{1,0:T(8,128)(2,1)S(1)}, u32[]{:S(2)}, u32[]{:S(2)}) %collective-permute-start.5) | collective-permute-done | bytes 131104 | tf_op jit(solution)/shard_map/ppermute | solution.py:41
  28.7 9.3 %collective-permute-done.4.refs_2_.refs_3_ = bf16[64,1024]{1,0:T(8,128)(2,1)S(1)} collective-permute-done((bf16[64,1024]{1,0:T(8,128)(2,1)S(1)}, bf16[64,1024]{1,0:T(8,128)(2,1)S(1)}, u32[]{:S(2)}, u32[]{:S(2)}) %collective-permute-start.4) | collective-permute-done | bytes 131104 | tf_op jit(solution)/shard_map/ppermute | solution.py:41
  39.9 6.2 %all-to-all-done = bf16[8,128,512]{2,1,0:T(8,128)(2,1)S(1)} async-done(((bf16[8,128,512]{2,1,0:T(8,128)(2,1)}), bf16[8,128,512]{2,1,0:T(8,128)(2,1)S(1)}, u32[]{:S(2)}, u32[]{:S(2)}) %all-to-all-start) | async-done | bytes 1048608 | tf_op jit(solution)/shard_map/all_to_all | solution.py:869
  52.2 6.0 %split_weights.2.refs_1_.refs_0_ = bf16[8,128,1536]{2,1,0:T(8,128)(2,1)S(1)} custom-call(f32[12288,128]{1,0:T(8,128)} %bitcast.89), custom_call_target="tpu_custom_call" | custom-call | flops 1572864 | bytes 9437184 | tf_op jit(solution)/shard_map/split_weights/pallas_call | solution.py:831
  70.2 4.8 %all-to-all-start.1 = ((bf16[8,128,1536]{2,1,0:T(8,128)(2,1)}), bf16[8,128,1536]{2,1,0:T(8,128)(2,1)}, u32[]{:S(2)}, u32[]{:S(2)}) async-start(bf16[8,128,1536]{2,1,0:T(8,128)(2,1)} %after.10), calls=%async_computation.1 | async-start | bytes 6291456 | tf_op jit(solution)/shard_map/all_to_all | solution.py:869
  85.5 24.5 %collective-permute-done.15.refs_2_ = bf16[64,1024]{1,0:T(8,128)(2,1)S(1)} collective-permute-done((bf16[64,1024]{1,0:T(8,128)(2,1)S(1)}, bf16[64,1024]{1,0:T(8,128)(2,1)S(1)}, u32[]{:S(2)}, u32[]{:S(2)}) %collective-permute-start.15) | collective-permute-done | bytes 131104 | tf_op jit(solution)/shard_map/ppermute | solution.py:41
  111.0 3.5 %collective-permute-start.19 = (bf16[64,1024]{1,0:T(8,128)(2,1)S(1)}, bf16[64,1024]{1,0:T(8,128)(2,1)S(1)}, u32[]{:S(2)}, u32[]{:S(2)}) collective-permute-start(bf16[64,1024]{1,0:T(8,128)(2,1)S(1)} %get-tuple-element.102.refs_0_), channel_id=1, source_target_pairs={{0,6},{2,4},{4,2},{6,0},{1,7},{3,5},{5,3},{7,1},{8,14},{10,12},{12... | collective-permute-start | bytes 393224 | tf_op jit(solution)/shard_map/ppermute | solution.py:41
  115.0 8.6 %collective-permute-done.22.refs_2_ = bf16[64,1024]{1,0:T(8,128)(2,1)S(1)} collective-permute-done((bf16[64,1024]{1,0:T(8,128)(2,1)S(1)}, bf16[64,1024]{1,0:T(8,128)(2,1)S(1)}, u32[]{:S(2)}, u32[]{:S(2)}) %collective-permute-start.22) | collective-permute-done | bytes 131104 | tf_op jit(solution)/shard_map/ppermute | solution.py:41
  127.5 15.3 %all-to-all-done.1 = bf16[8,128,1536]{2,1,0:T(8,128)(2,1)} async-done(((bf16[8,128,1536]{2,1,0:T(8,128)(2,1)}), bf16[8,128,1536]{2,1,0:T(8,128)(2,1)}, u32[]{:S(2)}, u32[]{:S(2)}) %all-to-all-start.1) | async-done | bytes 3145760 | tf_op jit(solution)/shard_map/all_to_all | solution.py:869
  142.8 5.2 %ffn_kernel.1 = (bf16[512,512]{1,0:T(8,128)(2,1)S(1)}, bf16[512,1024]{1,0:T(8,128)(2,1)S(1)}, bf16[256,1024]{1,0:T(8,128)(2,1)S(1)}, bf16[256,1024]{1,0:T(8,128)(2,1)S(1)}) custom-call(bf16[512,1024]{1,0:T(8,128)(2,1)S(1)} %stack_kernel.8.x_ref.refs_0_, bf16[512,1024]{1,0:T(8,128)(2,1)S(1)} %stack_kernel.10.g_ref.refs_0_, bf16[1024,1536]{1,0:T(8,128)(2,1)} %bitcast.15.w_ref), custom_call_target="tpu_custom_call" | custom-call | flops 2684354560 | bytes 7864320 | tf_op jit(solution)/shard_map/ffn_kernel/pallas_call | solution.py:177
  151.8 4.7 %all-to-all-start.2 = ((bf16[8,128,1024]{2,1,0:T(8,128)(2,1)}), bf16[8,128,1024]{2,1,0:T(8,128)(2,1)}, u32[]{:S(2)}, u32[]{:S(2)}) async-start(bf16[8,128,1024]{2,1,0:T(8,128)(2,1)} %bitcast.88), calls=%async_computation.2 | async-start | bytes 4194304 | tf_op jit(solution)/shard_map/all_to_all | solution.py:877
  167.7 12.2 %collective-permute-done.27.refs_2_ = bf16[64,1024]{1,0:T(8,128)(2,1)} collective-permute-done((bf16[64,1024]{1,0:T(8,128)(2,1)}, bf16[64,1024]{1,0:T(8,128)(2,1)}, u32[]{:S(2)}, u32[]{:S(2)}) %collective-permute-start.27) | collective-permute-done | bytes 131104 | tf_op jit(solution)/shard_map/ppermute | solution.py:41
  182.7 3.6 %collective-permute-start.31 = (bf16[64,1024]{1,0:T(8,128)(2,1)S(1)}, bf16[64,1024]{1,0:T(8,128)(2,1)S(1)}, u32[]{:S(2)}, u32[]{:S(2)}) collective-permute-start(bf16[64,1024]{1,0:T(8,128)(2,1)S(1)} %get-tuple-element.115.refs_0_.refs_1_), channel_id=1, source_target_pairs={{0,6},{2,4},{4,2},{6,0},{1,7},{3,5},{5,3},{7,1},{8,14},{10,12},{12... | collective-permute-start | bytes 393224 | tf_op jit(solution)/shard_map/ppermute | solution.py:41
  188.4 3.4 %collective-permute-done.31.refs_3_.refs_4_ = bf16[64,1024]{1,0:T(8,128)(2,1)S(1)} collective-permute-done((bf16[64,1024]{1,0:T(8,128)(2,1)S(1)}, bf16[64,1024]{1,0:T(8,128)(2,1)S(1)}, u32[]{:S(2)}, u32[]{:S(2)}) %collective-permute-start.31) | collective-permute-done | bytes 131104 | tf_op jit(solution)/shard_map/ppermute | solution.py:41
  214.5 4.2 %collective-permute-done.37.refs_2_.refs_3_ = bf16[128,384]{1,0:T(8,128)(2,1)S(1)} collective-permute-done((bf16[128,384]{1,0:T(8,128)(2,1)S(1)}, bf16[128,384]{1,0:T(8,128)(2,1)S(1)}, u32[]{:S(2)}, u32[]{:S(2)}) %collective-permute-start.37) | collective-permute-done | bytes 98336 | tf_op jit(solution)/shard_map/ppermute | solution.py:41
  219.4 4.4 %all-to-all-start.3 = ((bf16[8,128,640]{2,1,0:T(8,128)(2,1)}), bf16[8,128,640]{2,1,0:T(8,128)(2,1)S(1)}, u32[]{:S(2)}, u32[]{:S(2)}) async-start(bf16[8,128,640]{2,1,0:T(8,128)(2,1)} %after.13), calls=%async_computation.3 | async-start | bytes 2621440 | tf_op jit(solution)/shard_map/all_to_all | solution.py:877
  224.8 4.9 %attn_grads_kernel.1 = (bf16[256,1024]{1,0:T(8,128)(2,1)}, bf16[256,1024]{1,0:T(8,128)(2,1)}, bf16[1024,384]{1,0:T(8,128)(2,1)}, f32[3,1024]{1,0:T(4,128)}) custom-call(s32[1]{0:T(128)} %after.11.me_ref, bf16[128,384]{1,0:T(8,128)(2,1)} %copy-done.48, bf16[128,384]{1,0:T(8,128)(2,1)} %copy-done.59, bf16[128,384]{1,0:T(8,128)(2,1)} %copy-done.60, ...), custom_call_target="tpu_custom_call" | custom-call | flops 805306368 | bytes 4346368 | tf_op jit(solution)/shard_map/attn_grads_kernel/pallas_call | solution.py:177
  240.2 8.8 %collective-permute-done.50.refs_9_ = f32[3,1024]{1,0:T(4,128)S(1)} collective-permute-done((f32[3,1024]{1,0:T(4,128)S(1)}, f32[3,1024]{1,0:T(4,128)S(1)}, u32[]{:S(2)}, u32[]{:S(2)}) %collective-permute-start.50) | collective-permute-done | bytes 12320 | tf_op jit(solution)/shard_map/ppermute | solution.py:41
  258.9 5.5 %collective-permute-done.52.refs_2_ = bf16[3,16,1024]{2,1,0:T(8,128)(2,1)S(1)} collective-permute-done((bf16[3,16,1024]{2,1,0:T(8,128)(2,1)}, bf16[3,16,1024]{2,1,0:T(8,128)(2,1)S(1)}, u32[]{:S(2)}, u32[]{:S(2)}) %collective-permute-start.52) | collective-permute-done | bytes 98336 | tf_op jit(solution)/shard_map/ppermute | solution.py:41
  267.0 3.7 %all-to-all-start.4 = ((bf16[8,128,384]{2,1,0:T(8,128)(2,1)}), bf16[8,128,384]{2,1,0:T(8,128)(2,1)S(1)}, u32[]{:S(2)}, u32[]{:S(2)}) async-start(bf16[8,128,384]{2,1,0:T(8,128)(2,1)} %after.15), calls=%async_computation.4 | async-start | bytes 1572864 | tf_op jit(solution)/shard_map/all_to_all | solution.py:877
  274.5 15.1 %adamw.2 = (f32[12288,128]{1,0:T(8,128)}, f32[12288,128]{1,0:T(8,128)}, f32[12288,128]{1,0:T(8,128)}) custom-call(f32[3,1024]{1,0:T(4,128)S(1)} %copy-done.19, bf16[8,128,1024]{2,1,0:T(8,128)(2,1)} %all-to-all-done.2.refs_1_.refs_0_, bf16[8,128,640]{2,1,0:T(8,128)(2,1)S(1)} %copy-done.2, f32[12288,128]{1,0:T(8,128)} %bitcast.90, f32[12288,128]{1,0:T(8,128)} %bitcast.92, ...), custom_call_target="tpu_custom_call" | custom-call | flops 31457280 | bytes 40894464 | tf_op jit(solution)/shard_map/adamw/pallas_call | solution.py:981
  292.0 6.9 %adamw.3 = (f32[4096,128]{1,0:T(8,128)}, f32[4096,128]{1,0:T(8,128)}, f32[4096,128]{1,0:T(8,128)}) custom-call(f32[3,1024]{1,0:T(4,128)S(1)} %copy-done.20, bf16[8,128,384]{2,1,0:T(8,128)(2,1)S(1)} %all-to-all-done.4.refs_0_, bf16[8,128,640]{2,1,0:T(8,128)(2,1)} %copy-done.1, f32[4096,128]{1,0:T(8,128)} %bitcast.85, f32[4096,128]{1,0:T(8,128)} %bitcast.95, ...), custom_call_target="tpu_custom_call" | custom-call | flops 10485760 | bytes 13631488 | tf_op jit(solution)/shard_map/adamw/pallas_call | solution.py:981
  (285 shorter events, 121.2 us)
Async XLA Ops:
  15.4 30.7 %all-to-all-start = ((bf16[8,128,512]{2,1,0:T(8,128)(2,1)}), bf16[8,128,512]{2,1,0:T(8,128)(2,1)S(1)}, u32[]{:S(2)}, u32[]{:S(2)}) async-start(bf16[8,128,512]{2,1,0:T(8,128)(2,1)} %after.9), calls=%async_computation | async-start | bytes 2097152 | tf_op jit(solution)/shard_map/all_to_all | solution.py:869
  23.9 14.0 %collective-permute-start.4 = (bf16[64,1024]{1,0:T(8,128)(2,1)S(1)}, bf16[64,1024]{1,0:T(8,128)(2,1)S(1)}, u32[]{:S(2)}, u32[]{:S(2)}) collective-permute-start(bf16[64,1024]{1,0:T(8,128)(2,1)S(1)} %copy-done.9), channel_id=1, source_target_pairs={{0,4},{2,6},{4,0},{6,2},{1,5},{3,7},{5,1},{7,3},{8,12},{10,14},{12... | collective-permute-start | bytes 393224 | tf_op jit(solution)/shard_map/ppermute | solution.py:41
  24.0 13.9 %collective-permute-start.3 = (bf16[64,1024]{1,0:T(8,128)(2,1)S(1)}, bf16[64,1024]{1,0:T(8,128)(2,1)S(1)}, u32[]{:S(2)}, u32[]{:S(2)}) collective-permute-start(bf16[64,1024]{1,0:T(8,128)(2,1)S(1)} %copy-done.9), channel_id=1, source_target_pairs={{0,2},{2,0},{4,6},{6,4},{1,3},{3,1},{5,7},{7,5},{8,10},{10,8},{12,... | collective-permute-start | bytes 393224 | tf_op jit(solution)/shard_map/ppermute | solution.py:41
  47.8 12.6 %collective-permute-start.7 = (bf16[128,384]{1,0:T(8,128)(2,1)S(1)}, bf16[128,384]{1,0:T(8,128)(2,1)S(1)}, u32[]{:S(2)}, u32[]{:S(2)}) collective-permute-start(bf16[128,384]{1,0:T(8,128)(2,1)S(1)} %get-tuple-element.87), channel_id=1, source_target_pairs={{0,8},{8,0},{16,24},{24,16},{1,9},{9,1},{17,25},{25,17},{2,10},{10... | collective-permute-start | bytes 294920 | tf_op jit(solution)/shard_map/ppermute | solution.py:41
  47.8 12.6 %collective-permute-start.8 = (bf16[128,384]{1,0:T(8,128)(2,1)S(1)}, bf16[128,384]{1,0:T(8,128)(2,1)S(1)}, u32[]{:S(2)}, u32[]{:S(2)}) collective-permute-start(bf16[128,384]{1,0:T(8,128)(2,1)S(1)} %get-tuple-element.88), channel_id=1, source_target_pairs={{0,16},{8,24},{16,0},{24,8},{1,17},{9,25},{17,1},{25,9},{2,18},{10... | collective-permute-start | bytes 294920 | tf_op jit(solution)/shard_map/ppermute | solution.py:41
  70.2 72.6 %all-to-all-start.1 = ((bf16[8,128,1536]{2,1,0:T(8,128)(2,1)}), bf16[8,128,1536]{2,1,0:T(8,128)(2,1)}, u32[]{:S(2)}, u32[]{:S(2)}) async-start(bf16[8,128,1536]{2,1,0:T(8,128)(2,1)} %after.10), calls=%async_computation.1 | async-start | bytes 6291456 | tf_op jit(solution)/shard_map/all_to_all | solution.py:869
  79.2 30.8 %collective-permute-start.15 = (bf16[64,1024]{1,0:T(8,128)(2,1)S(1)}, bf16[64,1024]{1,0:T(8,128)(2,1)S(1)}, u32[]{:S(2)}, u32[]{:S(2)}) collective-permute-start(bf16[64,1024]{1,0:T(8,128)(2,1)S(1)} %get-tuple-element.98), channel_id=1, source_target_pairs={{0,4},{2,6},{4,0},{6,2},{1,5},{3,7},{5,1},{7,3},{8,12},{10,14},{12... | collective-permute-start | bytes 393224 | tf_op jit(solution)/shard_map/ppermute | solution.py:41
  81.2 28.8 %collective-permute-start.16 = (bf16[64,1024]{1,0:T(8,128)(2,1)S(1)}, bf16[64,1024]{1,0:T(8,128)(2,1)S(1)}, u32[]{:S(2)}, u32[]{:S(2)}) collective-permute-start(bf16[64,1024]{1,0:T(8,128)(2,1)S(1)} %get-tuple-element.99), channel_id=1, source_target_pairs={{0,6},{2,4},{4,2},{6,0},{1,7},{3,5},{5,3},{7,1},{8,14},{10,12},{12... | collective-permute-start | bytes 393224 | tf_op jit(solution)/shard_map/ppermute | solution.py:41
  81.2 33.2 %collective-permute-start.23 = (bf16[64,1024]{1,0:T(8,128)(2,1)S(1)}, bf16[64,1024]{1,0:T(8,128)(2,1)S(1)}, u32[]{:S(2)}, u32[]{:S(2)}) collective-permute-start(bf16[64,1024]{1,0:T(8,128)(2,1)S(1)} %get-tuple-element.103.refs_0_), channel_id=1, source_target_pairs={{0,6},{2,4},{4,2},{6,0},{1,7},{3,5},{5,3},{7,1},{8,14},{10,12},{12... | collective-permute-start | bytes 393224 | tf_op jit(solution)/shard_map/ppermute | solution.py:41
  84.1 39.5 %collective-permute-start.22 = (bf16[64,1024]{1,0:T(8,128)(2,1)S(1)}, bf16[64,1024]{1,0:T(8,128)(2,1)S(1)}, u32[]{:S(2)}, u32[]{:S(2)}) collective-permute-start(bf16[64,1024]{1,0:T(8,128)(2,1)S(1)} %get-tuple-element.103.refs_0_), channel_id=1, source_target_pairs={{0,4},{2,6},{4,0},{6,2},{1,5},{3,7},{5,1},{7,3},{8,12},{10,14},{12... | collective-permute-start | bytes 393224 | tf_op jit(solution)/shard_map/ppermute | solution.py:41
  84.2 39.4 %collective-permute-start.21 = (bf16[64,1024]{1,0:T(8,128)(2,1)S(1)}, bf16[64,1024]{1,0:T(8,128)(2,1)S(1)}, u32[]{:S(2)}, u32[]{:S(2)}) collective-permute-start(bf16[64,1024]{1,0:T(8,128)(2,1)S(1)} %get-tuple-element.103.refs_0_), channel_id=1, source_target_pairs={{0,2},{2,0},{4,6},{6,4},{1,3},{3,1},{5,7},{7,5},{8,10},{10,8},{12,... | collective-permute-start | bytes 393224 | tf_op jit(solution)/shard_map/ppermute | solution.py:41
  111.0 12.8 %collective-permute-start.19 = (bf16[64,1024]{1,0:T(8,128)(2,1)S(1)}, bf16[64,1024]{1,0:T(8,128)(2,1)S(1)}, u32[]{:S(2)}, u32[]{:S(2)}) collective-permute-start(bf16[64,1024]{1,0:T(8,128)(2,1)S(1)} %get-tuple-element.102.refs_0_), channel_id=1, source_target_pairs={{0,6},{2,4},{4,2},{6,0},{1,7},{3,5},{5,3},{7,1},{8,14},{10,12},{12... | collective-permute-start | bytes 393224 | tf_op jit(solution)/shard_map/ppermute | solution.py:41
  151.8 67.6 %all-to-all-start.2 = ((bf16[8,128,1024]{2,1,0:T(8,128)(2,1)}), bf16[8,128,1024]{2,1,0:T(8,128)(2,1)}, u32[]{:S(2)}, u32[]{:S(2)}) async-start(bf16[8,128,1024]{2,1,0:T(8,128)(2,1)} %bitcast.88), calls=%async_computation.2 | async-start | bytes 4194304 | tf_op jit(solution)/shard_map/all_to_all | solution.py:877
  161.6 18.3 %collective-permute-start.27 = (bf16[64,1024]{1,0:T(8,128)(2,1)}, bf16[64,1024]{1,0:T(8,128)(2,1)}, u32[]{:S(2)}, u32[]{:S(2)}) collective-permute-start(bf16[64,1024]{1,0:T(8,128)(2,1)} %get-tuple-element.111), channel_id=1, source_target_pairs={{0,4},{2,6},{4,0},{6,2},{1,5},{3,7},{5,1},{7,3},{8,12},{10,14},{12... | collective-permute-start | bytes 393224 | tf_op jit(solution)/shard_map/ppermute | solution.py:41
  163.2 16.7 %collective-permute-start.28 = (bf16[64,1024]{1,0:T(8,128)(2,1)}, bf16[64,1024]{1,0:T(8,128)(2,1)}, u32[]{:S(2)}, u32[]{:S(2)}) collective-permute-start(bf16[64,1024]{1,0:T(8,128)(2,1)} %get-tuple-element.112), channel_id=1, source_target_pairs={{0,6},{2,4},{4,2},{6,0},{1,7},{3,5},{5,3},{7,1},{8,14},{10,12},{12... | collective-permute-start | bytes 393224 | tf_op jit(solution)/shard_map/ppermute | solution.py:41
  194.9 14.9 %collective-permute-start.44 = (bf16[64,1024]{1,0:T(8,128)(2,1)S(1)}, bf16[64,1024]{1,0:T(8,128)(2,1)S(1)}, u32[]{:S(2)}, u32[]{:S(2)}) collective-permute-start(bf16[64,1024]{1,0:T(8,128)(2,1)S(1)} %get-tuple-element.137), channel_id=1, source_target_pairs={{0,2},{2,0},{4,6},{6,4},{1,3},{3,1},{5,7},{7,5},{8,10},{10,8},{12,... | collective-permute-start | bytes 393224 | tf_op jit(solution)/shard_map/ppermute | solution.py:41
  201.6 12.9 %collective-permute-start.45 = (bf16[64,1024]{1,0:T(8,128)(2,1)S(1)}, bf16[64,1024]{1,0:T(8,128)(2,1)S(1)}, u32[]{:S(2)}, u32[]{:S(2)}) collective-permute-start(bf16[64,1024]{1,0:T(8,128)(2,1)S(1)} %get-tuple-element.138), channel_id=1, source_target_pairs={{0,4},{2,6},{4,0},{6,2},{1,5},{3,7},{5,1},{7,3},{8,12},{10,14},{12... | collective-permute-start | bytes 393224 | tf_op jit(solution)/shard_map/ppermute | solution.py:41
  219.4 46.5 %all-to-all-start.3 = ((bf16[8,128,640]{2,1,0:T(8,128)(2,1)}), bf16[8,128,640]{2,1,0:T(8,128)(2,1)S(1)}, u32[]{:S(2)}, u32[]{:S(2)}) async-start(bf16[8,128,640]{2,1,0:T(8,128)(2,1)} %after.13), calls=%async_computation.3 | async-start | bytes 2621440 | tf_op jit(solution)/shard_map/all_to_all | solution.py:877
  233.9 15.1 %collective-permute-start.40 = (bf16[64,1024]{1,0:T(8,128)(2,1)S(1)}, bf16[64,1024]{1,0:T(8,128)(2,1)S(1)}, u32[]{:S(2)}, u32[]{:S(2)}) collective-permute-start(bf16[64,1024]{1,0:T(8,128)(2,1)S(1)} %get-tuple-element.133), channel_id=1, source_target_pairs={{0,2},{2,0},{4,6},{6,4},{1,3},{3,1},{5,7},{7,5},{8,10},{10,8},{12,... | collective-permute-start | bytes 393224 | tf_op jit(solution)/shard_map/ppermute | solution.py:41
  235.7 13.3 %collective-permute-start.41 = (bf16[64,1024]{1,0:T(8,128)(2,1)S(1)}, bf16[64,1024]{1,0:T(8,128)(2,1)S(1)}, u32[]{:S(2)}, u32[]{:S(2)}) collective-permute-start(bf16[64,1024]{1,0:T(8,128)(2,1)S(1)} %get-tuple-element.134), channel_id=1, source_target_pairs={{0,4},{2,6},{4,0},{6,2},{1,5},{3,7},{5,1},{7,3},{8,12},{10,14},{12... | collective-permute-start | bytes 393224 | tf_op jit(solution)/shard_map/ppermute | solution.py:41
  267.0 24.2 %all-to-all-start.4 = ((bf16[8,128,384]{2,1,0:T(8,128)(2,1)}), bf16[8,128,384]{2,1,0:T(8,128)(2,1)S(1)}, u32[]{:S(2)}, u32[]{:S(2)}) async-start(bf16[8,128,384]{2,1,0:T(8,128)(2,1)} %after.15), calls=%async_computation.4 | async-start | bytes 1572864 | tf_op jit(solution)/shard_map/all_to_all | solution.py:877
  270.7 19.5 %collective-permute-start.56 = (bf16[4,2,16,1024]{3,2,1,0:T(8,128)(2,1)S(1)}, bf16[4,2,16,1024]{3,2,1,0:T(8,128)(2,1)S(1)}, u32[]{:S(2)}, u32[]{:S(2)}) collective-permute-start(bf16[4,2,16,1024]{3,2,1,0:T(8,128)(2,1)S(1)} %get-tuple-element.146.refs_0_), channel_id=1, source_target_pairs={{0,3},{1,2},{2,1},{3,0},{4,7},{5,6},{6,5},{7,4},{8,11},{9,10},{10,... | collective-permute-start | bytes 786440 | tf_op jit(solution)/shard_map/ppermute | solution.py:41
  271.5 18.7 %collective-permute-start.55 = (bf16[4,2,16,1024]{3,2,1,0:T(8,128)(2,1)S(1)}, bf16[4,2,16,1024]{3,2,1,0:T(8,128)(2,1)S(1)}, u32[]{:S(2)}, u32[]{:S(2)}) collective-permute-start(bf16[4,2,16,1024]{3,2,1,0:T(8,128)(2,1)S(1)} %get-tuple-element.146.refs_0_), channel_id=1, source_target_pairs={{0,2},{1,3},{2,0},{3,1},{4,6},{5,7},{6,4},{7,5},{8,10},{9,11},{10,... | collective-permute-start | bytes 786440 | tf_op jit(solution)/shard_map/ppermute | solution.py:41
  273.0 17.2 %collective-permute-start.54 = (bf16[4,2,16,1024]{3,2,1,0:T(8,128)(2,1)S(1)}, bf16[4,2,16,1024]{3,2,1,0:T(8,128)(2,1)S(1)}, u32[]{:S(2)}, u32[]{:S(2)}) collective-permute-start(bf16[4,2,16,1024]{3,2,1,0:T(8,128)(2,1)S(1)} %get-tuple-element.146.refs_0_), channel_id=1, source_target_pairs={{0,1},{1,0},{2,3},{3,2},{4,5},{5,4},{6,7},{7,6},{8,9},{9,8},{10,11... | collective-permute-start | bytes 786440 | tf_op jit(solution)/shard_map/ppermute | solution.py:41
  (105 other events, 1041.1 us)

commit v3 on v2

--- a/solution.py
+++ b/solution.py
@@ -269,11 +269,11 @@
         rows_ref[at, :] = got[t][0, :, :model].astype(F32)
         grad_ref[at, :] = got[t][1, :, :model].astype(F32)
         mask_ref[at, :] = got[t][0, :, model:].astype(F32)
-    normed_ref[...] = rms_forward(rows_ref[...], gain_ref[...])[2]
+    normed_ref[...] = rms_forward(rows_ref[...], gain_ref[0:1, :])[2]
     masked_ref[...] = (mask_ref[:, :1] * grad_ref[...]).astype(BF)
 
 
-def unpack_rows(got, gain, me):
+def unpack_rows(got, gains, me):
     depth = len(got)
     share, wide = got[0].shape[1:]
     shape = (depth * share, wide - 128)
@@ -281,7 +281,7 @@
         functools.partial(unpack_kernel, depth),
         [sds(shape, F32), sds(shape, F32), sds((shape[0], 128), F32), sds(shape, BF), sds(shape, BF)],
         *got,
-        gain[None],
+        gains,
         index=me,
     )
 
@@ -416,10 +416,10 @@
     hidden_ref, normed_ref = refs[chips + 3 :]
     hidden = rows_ref[...] + mask_ref[:, :1] * sum_refs(terms)
     hidden_ref[...] = hidden
-    normed_ref[...] = rms_forward(hidden, gain_ref[...])[2]
-
-
-def join_rows(terms, rows_in, mask, gain):
+    normed_ref[...] = rms_forward(hidden, gain_ref[1:2, :])[2]
+
+
+def join_rows(terms, rows_in, mask, gains):
     shape = rows_in.shape
     return vmem_call(
         functools.partial(join_kernel, len(terms)),
@@ -427,7 +427,7 @@
         *terms,
         rows_in,
         mask,
-        gain[None],
+        gains,
     )
 
 
@@ -436,14 +436,15 @@
     rows_ref, grad_ref, mask_ref, gain_ref = refs[chips : chips + 4]
     out_ref, masked_ref, gain_out_ref = refs[chips + 4 :]
     grad_normed = sum_refs(terms)
-    unit_rows, inv_rms, _ = rms_forward(rows_ref[...], gain_ref[...])
-    grad = grad_ref[...] + rms_backward(grad_normed, unit_rows, inv_rms, gain_ref[...])
+    gain = gain_ref[1:2, :]
+    unit_rows, inv_rms, _ = rms_forward(rows_ref[...], gain)
+    grad = grad_ref[...] + rms_backward(grad_normed, unit_rows, inv_rms, gain)
     out_ref[...] = grad
     masked_ref[...] = (mask_ref[:, :1] * grad).astype(BF)
     gain_out_ref[...] = jnp.sum(grad_normed * unit_rows, axis=0, keepdims=True)
 
 
-def norm_back(terms, rows, grad_rows, mask, gain, index):
+def norm_back(terms, rows, grad_rows, mask, gains, index):
     shape = rows.shape
     return vmem_call(
         functools.partial(norm_back_kernel, len(terms)),
@@ -452,7 +453,7 @@
         rows,
         grad_rows,
         mask,
-        gain[None],
+        gains,
         index=index,
     )
 
@@ -462,8 +463,9 @@
     totals, refs = refs[2 * chips : 2 * chips + 2], refs[2 * chips + 2 :]
     rows_ref, grad_ref, hidden_ref, mask_ref, gain_ref = refs[:5]
     outs, (output, input_grad) = refs[5:-2], refs[-2:]
-    unit_rows, inv_rms, _ = rms_forward(rows_ref[...], gain_ref[...])
-    grad = rms_backward(sum_refs(terms), unit_rows, inv_rms, gain_ref[...])
+    gain = gain_ref[0:1, :]
+    unit_rows, inv_rms, _ = rms_forward(rows_ref[...], gain)
+    grad = rms_backward(sum_refs(terms), unit_rows, inv_rms, gain)
     output[...] = (hidden_ref[...] + mask_ref[:, :1] * sum_refs(ffn_terms)).astype(BF)
     input_grad[...] = (grad_ref[...] + grad).astype(BF)
     total = totals[0][...] + totals[1][...]
@@ -480,7 +482,7 @@
         ref[2, 8 : 8 + count, :] = low
 
 
-def finish_rows(terms, ffn_terms, totals, rows, grad_rows, hidden, mask, gain, me, depth):
+def finish_rows(terms, ffn_terms, totals, rows, grad_rows, hidden, mask, gains, me, depth):
     tokens, model = rows.shape
     return vmem_call(
         functools.partial(finish_kernel, depth, len(terms)),
@@ -492,7 +494,7 @@
         grad_rows,
         hidden,
         mask,
-        gain[None],
+        gains,
         index=me,
         scratch=[pltpu.VMEM((tokens, model), BF)] * 2,
         vmem=56,
@@ -686,10 +688,10 @@
         terms = mm_nt(by_chunk[c], w_ref[:, : 3 * width])
         out[at : at + rows, :] = terms.astype(BF)
         total = total + jnp.sum(terms * normed_ref[here, :].astype(F32), axis=0, keepdims=True)
-    gain_out_ref[...] = total / gain_ref[...]
-
-
-def qkv_back(got, attn_w, normed, gain, width, me):
+    gain_out_ref[...] = total / gain_ref[0:1, :]
+
+
+def qkv_back(got, attn_w, normed, gains, width, me):
     depth = len(got)
     rows = got[0].shape[0]
     tokens = depth * rows
@@ -702,7 +704,7 @@
         *got,
         attn_w,
         normed,
-        gain[None],
+        gains,
         index=me,
         scratch=[pltpu.VMEM((depth, rows, 3 * width), BF)],
         flops=6 * tokens * width * model,
@@ -717,7 +719,7 @@
         by_chunk[me_ref[0] ^ t] = got[t][...]
     rows = by_chunk.shape[1]
     half = depth // 2
-    total = jnp.zeros(gain_ref.shape, F32)
+    total = jnp.zeros(gain2_ref.shape, F32)
     for c in range(depth):
         here = slice(c * rows, (c + 1) * rows)
         grads[here, :] = by_chunk[c]
@@ -726,7 +728,7 @@
         terms = mm_nt(by_chunk[c], w_ref[:, : 3 * width])
         out[at : at + rows, :] = terms.astype(BF)
         total = total + jnp.sum(terms * normed_ref[here, :].astype(F32), axis=0, keepdims=True)
-    total_ref[0:1, :] = total / gain_ref[...]
+    total_ref[0:1, :] = total / gain_ref[0:1, :]
     total_ref[1:2, :] = gain2_ref[...]
     chunk = mm_tn(normed_ref[...], grads[...])
     chunk_ref[...] = chunk.astype(BF)
@@ -734,18 +736,18 @@
     squares = square_ref[...]
     for j in range(0, 3 * width, 128):
         squares = squares + column[:, j : j + 128]
-    total_ref[2:3, :] = jnp.zeros(gain_ref.shape, F32)
+    total_ref[2:3, :] = jnp.zeros(gain2_ref.shape, F32)
     total_ref[2:3, :128] = squares
 
 
-def attn_grads(got, attn_w, normed, gain, gain_part2, squares, me):
+def attn_grads(got, attn_w, normed, gains, gain_part2, squares, me):
     depth = len(got)
     rows, wide = got[0].shape
     width = wide // 3
     tokens = depth * rows
     model = attn_w.shape[0]
     if lax.axis_size("rf") > 1 or width % 128:
-        grads, near, far, gain_part1 = qkv_back(got, attn_w, normed, gain, width, me)
+        grads, near, far, gain_part1 = qkv_back(got, attn_w, normed, gains, width, me)
         chunks, more = weight_grads((normed, grads, 0, wide))
         squares = jnp.pad(squares + more, ((0, 0), (0, model - 128)))
         return near, far, chunks, jnp.concatenate([gain_part1, gain_part2, squares], 0)
@@ -755,7 +757,7 @@
         *got,
         attn_w,
         normed,
-        gain[None],
+        gains,
         gain_part2,
         squares,
         index=me,
@@ -894,16 +896,16 @@
     return jnp.sqrt(jnp.sum(sums, axis=1, keepdims=True))
 
 
-def adamw_kernel(dims, pieces, steps, stages, total_ref, *refs):
+def adamw_kernel(dims, pieces, steps, stages, total_from, *refs):
     kinds, tiles, depth, _ = dims
     n = len(pieces)
     g_refs, state, refs = refs[:n], refs[n : n + 3], refs[n + 3 :]
     stage_refs, new_refs, staged_refs = refs[:stages], refs[stages : stages + 3], refs[stages + 3 :]
     staged_refs, refs = staged_refs[:stages], staged_refs[stages:]
     g_held, refs = refs[:n], refs[n:]
-    here = len(refs) == 6
+    here = len(refs) == 7
     state_held, refs = (state, refs) if here else (refs[:3], refs[3:])
-    new_held, grads, in_sems, out_sems = refs[:3], refs[3], refs[4], refs[5]
+    new_held, grads, total_ref, in_sems, out_sems = refs[:3], *refs[3:]
     rows, units, _ = grads.shape
     count = rows * units
     places = {at: (number, chunk, lane) for at, chunk, number, lane in tiles_of(dims, pieces)}
@@ -926,6 +928,9 @@
         for j, (source, to) in enumerate(zip(stage_refs, staged_refs))
     ]
 
+    summed = pltpu.make_async_copy(total_from, total_ref, out_sems.at[steps, stages])
+    summed.start()
+
     @pl.loop(0, steps)
     def _(i):
         for copy in fetches(i):
@@ -933,6 +938,7 @@
 
     for copy in staging:
         copy.start()
+    summed.wait()
     clip = CLIP_NORM / jnp.maximum(norm_of(total_ref[...]), CLIP_NORM)
 
     @pl.loop(0, steps)
@@ -983,16 +989,15 @@
             adamw_kernel, (kinds, cols // 128, depth, parts), pieces, steps, len(stage)
         ),
         out_shape=[sds(view, F32)] * 3 + [sds(v.shape, F32) for v in stage],
-        in_specs=[inside]
-        + [anywhere] * len(chunks)
+        in_specs=[anywhere] * (1 + len(chunks))
         + [inside if here else anywhere] * 3
         + [anywhere] * len(stage),
         out_specs=[anywhere] * 3 + [inside] * len(stage),
         scratch_shapes=[pltpu.VMEM(v.shape, BF) for v in chunks]
         + [pltpu.VMEM(view, F32)] * (3 if here else 6)
-        + [pltpu.VMEM((step, units, 128), F32)]
+        + [pltpu.VMEM((step, units, 128), F32), pltpu.VMEM(total.shape, F32)]
         + [pltpu.SemaphoreType.DMA((steps, len(chunks) + 3))]
-        + [pltpu.SemaphoreType.DMA((steps + 1, 3))],
+        + [pltpu.SemaphoreType.DMA((steps + 1, 4))],
         compiler_params=pltpu.CompilerParams(vmem_limit_bytes=(20 if here else 52) << 20),
         cost_estimate=pl.CostEstimate(
             flops=20 * math.prod(shape), bytes_accessed=26 * math.prod(shape), transcendentals=0
@@ -1000,6 +1005,23 @@
         name="adamw",
     )(total, *chunks, *state, *stage)
     return out[:3], out[3:]
+
+
+def gains_kernel(total_ref, w_ref, m_ref, v_ref, norm_ref, *new_refs):
+    norm = norm_of(total_ref[...])
+    norm_ref[...] = norm
+    clip = CLIP_NORM / jnp.maximum(norm, CLIP_NORM)
+    new = adamw_update(
+        w_ref[...], m_ref[...], v_ref[...], total_ref[0:2, :], clip, 0.0, GAIN_RATE
+    )
+    for ref, values in zip(new_refs, new):
+        ref[...] = values
+
+
+def update_gains(total, state):
+    return vmem_call(
+        gains_kernel, [sds((1, 1), F32)] + [sds(v.shape, F32) for v in state], total, *state
+    )
 
 
 def body(
@@ -1019,8 +1041,6 @@
     depth, frames, model = inputs.shape
     mp_axes = ("mx", "mc")
     share = frames // axis_total(mp_axes)
-    gain_attn = norm_gains[0]
-    gain_ffn = norm_gains[1]
 
     me = lax.axis_index("pz")
     positions = ("pz",)
@@ -1028,8 +1048,8 @@
     packed = pack_rows(inputs, out_grad, depth_counts, me, linear_index(mp_axes), share)
     packed = swap_parts(packed, positions)
     attn_low = split_weights(attn_weight, 48)[0]
-    rows_in, rows_grad, mask, normed1_rows, masked = unpack_rows(packed, gain_attn, me)
-    attn_w = to_planes(after(attn_low, normed1_rows))
+    rows_in, rows_grad, mask, normed1_rows, masked = unpack_rows(packed, norm_gains, me)
+    attn_w = to_planes(after(attn_low, mask))
     ffn_low = split_weights(ffn_weight, 48)[0]
     width = attn_w.shape[1] // 4
     normed1_pieces = gather_pieces(normed1_rows)
@@ -1038,9 +1058,9 @@
     normed1, qkv = project(normed1_pieces, attn_w, width, me, depth)
     qkv = swap_parts(qkv, positions)
     context = swap_parts(attend_pieces(qkv, after(me.reshape(1), ffn_low)), positions)
-    ffn_w = to_planes(after(ffn_low, *context))
+    ffn_w = to_planes(after(ffn_low, *context[1:]))
     context, near, far = attn_out_terms(context, attn_w, me)
-    hidden_in, normed2_rows = join_rows(scatter_pieces(near, far), rows_in, mask, gain_ffn)
+    hidden_in, normed2_rows = join_rows(scatter_pieces(near, far), rows_in, mask, norm_gains)
     normed2 = stack_rows(gather_pieces(normed2_rows))
 
     acts, gate_up_grads, near, far = ffn_block(normed2, grad_ffn, ffn_w)
@@ -1052,7 +1072,7 @@
     ffn_terms = mm_nt(acts, ffn_w[:, 2 * hidden :]).astype(BF)
 
     grad_hidden, masked, gain_part2 = norm_back(
-        terms, hidden_in, rows_grad, mask, gain_ffn, after(me.reshape(1), ffn_terms)
+        terms, hidden_in, rows_grad, mask, norm_gains, after(me.reshape(1), ffn_terms)
     )
     grad_attn, grad_context = context_grads(gather_pieces(masked), attn_w, width, me, depth)
     grad_context = swap_parts(grad_context, positions)
@@ -1060,12 +1080,12 @@
     half = ffn_terms.shape[0] // 2
     ffn_terms = scatter_pieces(ffn_terms[:half], ffn_terms[half:])
     chunks_b, squares_b = weight_grads((grad_ffn, acts, 0, hidden), (grad_attn, context, 0, width))
-    owned_b = to_owners(after(chunks_b, *grad_qkv, *ffn_terms[1:]))
+    owned_b = to_owners(after(chunks_b, *grad_qkv[1:], *ffn_terms[1:]))
     near, far, attn_chunks, total = attn_grads(
         grad_qkv,
         attn_w,
         normed1,
-        gain_attn,
+        norm_gains,
         gain_part2,
         squares_a + squares_b,
         after(me.reshape(1), owned_a),
@@ -1079,25 +1099,23 @@
     if len(totals) != 2:
         totals = [tree_sum(totals), jnp.zeros_like(total)]
     back = finish_rows(
-        terms, ffn_terms, totals, rows_in, grad_hidden, hidden_in, mask, gain_attn, me, depth
+        terms, ffn_terms, totals, rows_in, grad_hidden, hidden_in, mask, norm_gains, me, depth
     )
 
     back, total = by_position(swap_parts(back, positions), me, total.shape[0])
-    attn_owned = to_owners(after(attn_chunks, total, owned_b))
+    attn_owned = to_owners(after(attn_chunks, total))
     back = swap_parts([back] * axis_total(mp_axes), mp_axes)
     output, input_grad = whole_frames(back, linear_index(mp_axes))
-
-    gain_grad = total[:2]
-    grad_norm = norm_of(total)[0, 0]
-    clip_factor = CLIP_NORM / jnp.maximum(grad_norm, CLIP_NORM)
 
     ffn_state = [lanes_view(v) for v in (ffn_weight, ffn_first, ffn_second)]
     attn_state = [lanes_view(v) for v in (attn_weight, attn_first, attn_second)]
     ffn_new, _ = adamw_owned(ffn_state, [owned_a, owned_b], total, ffn_weight.shape, pieces)
+    grad_norm, *gain_new = update_gains(total, [norm_gains, gain_first, gain_second])
     if width % 128:
         grads = jnp.concatenate([attn_owned, owned_b[:, :, hidden:]], -1)
         grads = grads.reshape(depth, lax.axis_size("rs"), -1, 4, width)
         grads = grads.transpose(2, 3, 0, 1, 4).reshape(attn_weight.shape).astype(F32)
+        clip_factor = CLIP_NORM / jnp.maximum(grad_norm[0, 0], CLIP_NORM)
         attn_new = adamw_update(
             attn_weight, attn_first, attn_second, grads, clip_factor, WEIGHT_DECAY, LEARN_RATE
         )
@@ -1114,10 +1132,7 @@
         attn_new = tuple(lanes_back(v, attn_weight.shape) for v in attn_new)
     ffn_new = tuple(lanes_back(v, ffn_weight.shape) for v in ffn_new)
 
-    gain_new = adamw_update(
-        norm_gains, gain_first, gain_second, gain_grad, clip_factor, 0.0, GAIN_RATE
-    )
-    return (output, input_grad, grad_norm) + attn_new + ffn_new + gain_new
+    return (output, input_grad, grad_norm[0, 0]) + attn_new + ffn_new + tuple(gain_new)
 
 
 def solution(mesh):

time: 301 us -> 294 us (0.977)
    ppermute x57, waiting for transfers between devices: 102 us -> 98.2 us  [hop(): return lax.ppermute(value, axes, [(i, i ^ step) for i in range(n)])]
    unnamed x134 -> x130, local copies, waits for them, and re-layouts: 20.3 us -> 19.5 us
    pallas_call x23 -> x24, Pallas kernels: 21.1 us -> 21.8 us  [vmem_call(): pl.pallas_call(kernel, out_shape=list(outs), in_specs=[pl.BlockSpec(memor...]
  transfers between devices with their start and end apart: 62 -> 62, of which waited for: 25 -> 26; matrix products, arithmetic and copies ran while one was open for 3% -> 2% of each run, Pallas kernels for 13% -> 14%
where the time goes in v3:
time: 294 us; the launch traced here: 293 us
  waiting for transfers between devices  120 us (41%)
  starting transfers between devices  89 us (30%)
  Pallas kernels  56.1 us (19%)
  local copies, waits for them, and re-layouts  22.6 us (8%)
    ppermute x57, waiting for transfers between devices, hop(): return lax.ppermute(value, axes, [(i, i ^ step) for i in range(n)])  98.2 us
    ppermute x57, starting transfers between devices, hop(): return lax.ppermute(value, axes, [(i, i ^ step) for i in range(n)])  66.9 us
    pallas_call x2, Pallas kernels, adamw_owned(): pl.pallas_call(functools.partial(adamw_kernel, (kinds, cols // 128, depth...  22.1 us
    pallas_call x24, Pallas kernels, vmem_call(): pl.pallas_call(kernel, out_shape=list(outs), in_specs=[pl.BlockSpec(memor...  21.8 us
    all_to_all x2, waiting for transfers between devices, to_planes(): full = lax.all_to_all(low, OWNERS, 0, 0, tiled=True)  21.4 us
    unnamed x130, local copies, waits for them, and re-layouts  19.5 us
    all_to_all x3, starting transfers between devices, to_owners(): return lax.all_to_all(chunks, OWNERS, 0, 0, tiled=True)  12.3 us
    all_to_all x2, starting transfers between devices, to_planes(): full = lax.all_to_all(low, OWNERS, 0, 0, tiled=True)  9.76 us
  transfers between devices with their start and end apart: 62, of which 26 were waited for; matrix products, arithmetic and copies ran while one was open for 2% of the time, Pallas kernels for 14%

profile of v3, /device:TPU:0, one launch (start us, length us, event | category | flops | bytes accessed | tf_op | source)
XLA Modules:
  0.0 293.3 jit_solution(6732233494227208370)
XLA Ops:
  2.5 5.1 %collective-permute-start.2 = (bf16[2,16,1152]{2,1,0:T(8,128)(2,1)S(1)}, bf16[2,16,1152]{2,1,0:T(8,128)(2,1)S(1)}, u32[]{:S(2)}, u32[]{:S(2)}) collective-permute-start(bf16[2,16,1152]{2,1,0:T(8,128)(2,1)S(1)} %get-tuple-element.168), channel_id=1, source_target_pairs={{0,24},{8,16},{16,8},{24,0},{1,25},{9,17},{17,9},{25,1},{2,26},{10... | collective-permute-start | bytes 221192 | tf_op jit(solution)/shard_map/ppermute | solution.py:41
  15.4 5.0 %all-to-all-start = ((bf16[8,128,512]{2,1,0:T(8,128)(2,1)}), bf16[8,128,512]{2,1,0:T(8,128)(2,1)S(1)}, u32[]{:S(2)}, u32[]{:S(2)}) async-start(bf16[8,128,512]{2,1,0:T(8,128)(2,1)} %after.9), calls=%async_computation | async-start | bytes 2097152 | tf_op jit(solution)/shard_map/all_to_all | solution.py:871
  23.9 4.3 %collective-permute-done.5.refs_3_.refs_4_ = bf16[64,1024]{1,0:T(8,128)(2,1)S(1)} collective-permute-done((bf16[64,1024]{1,0:T(8,128)(2,1)S(1)}, bf16[64,1024]{1,0:T(8,128)(2,1)S(1)}, u32[]{:S(2)}, u32[]{:S(2)}) %collective-permute-start.5) | collective-permute-done | bytes 131104 | tf_op jit(solution)/shard_map/ppermute | solution.py:41
  28.2 8.8 %collective-permute-done.4.refs_2_.refs_3_ = bf16[64,1024]{1,0:T(8,128)(2,1)S(1)} collective-permute-done((bf16[64,1024]{1,0:T(8,128)(2,1)S(1)}, bf16[64,1024]{1,0:T(8,128)(2,1)S(1)}, u32[]{:S(2)}, u32[]{:S(2)}) %collective-permute-start.4) | collective-permute-done | bytes 131104 | tf_op jit(solution)/shard_map/ppermute | solution.py:41
  39.0 6.2 %all-to-all-done = bf16[8,128,512]{2,1,0:T(8,128)(2,1)S(1)} async-done(((bf16[8,128,512]{2,1,0:T(8,128)(2,1)}), bf16[8,128,512]{2,1,0:T(8,128)(2,1)S(1)}, u32[]{:S(2)}, u32[]{:S(2)}) %all-to-all-start) | async-done | bytes 1048608 | tf_op jit(solution)/shard_map/all_to_all | solution.py:871
  51.3 6.0 %split_weights.2.refs_1_.refs_0_ = bf16[8,128,1536]{2,1,0:T(8,128)(2,1)S(1)} custom-call(f32[12288,128]{1,0:T(8,128)} %bitcast.89), custom_call_target="tpu_custom_call" | custom-call | flops 1572864 | bytes 9437184 | tf_op jit(solution)/shard_map/split_weights/pallas_call | solution.py:833
  68.7 4.8 %all-to-all-start.1 = ((bf16[8,128,1536]{2,1,0:T(8,128)(2,1)}), bf16[8,128,1536]{2,1,0:T(8,128)(2,1)}, u32[]{:S(2)}, u32[]{:S(2)}) async-start(bf16[8,128,1536]{2,1,0:T(8,128)(2,1)} %after.10), calls=%async_computation.1 | async-start | bytes 6291456 | tf_op jit(solution)/shard_map/all_to_all | solution.py:871
  84.0 31.1 %collective-permute-done.15.refs_2_ = bf16[64,1024]{1,0:T(8,128)(2,1)S(1)} collective-permute-done((bf16[64,1024]{1,0:T(8,128)(2,1)S(1)}, bf16[64,1024]{1,0:T(8,128)(2,1)S(1)}, u32[]{:S(2)}, u32[]{:S(2)}) %collective-permute-start.15) | collective-permute-done | bytes 131104 | tf_op jit(solution)/shard_map/ppermute | solution.py:41
  116.2 3.0 %collective-permute-start.18 = (bf16[64,1024]{1,0:T(8,128)(2,1)S(1)}, bf16[64,1024]{1,0:T(8,128)(2,1)S(1)}, u32[]{:S(2)}, u32[]{:S(2)}) collective-permute-start(bf16[64,1024]{1,0:T(8,128)(2,1)S(1)} %get-tuple-element.106.refs_0_), channel_id=1, source_target_pairs={{0,4},{2,6},{4,0},{6,2},{1,5},{3,7},{5,1},{7,3},{8,12},{10,14},{12... | collective-permute-start | bytes 393224 | tf_op jit(solution)/shard_map/ppermute | solution.py:41
  126.3 15.2 %all-to-all-done.1 = bf16[8,128,1536]{2,1,0:T(8,128)(2,1)} async-done(((bf16[8,128,1536]{2,1,0:T(8,128)(2,1)}), bf16[8,128,1536]{2,1,0:T(8,128)(2,1)}, u32[]{:S(2)}, u32[]{:S(2)}) %all-to-all-start.1) | async-done | bytes 3145760 | tf_op jit(solution)/shard_map/all_to_all | solution.py:871
  141.5 5.1 %ffn_kernel.1 = (bf16[512,512]{1,0:T(8,128)(2,1)S(1)}, bf16[512,1024]{1,0:T(8,128)(2,1)S(1)}, bf16[256,1024]{1,0:T(8,128)(2,1)S(1)}, bf16[256,1024]{1,0:T(8,128)(2,1)S(1)}) custom-call(bf16[512,1024]{1,0:T(8,128)(2,1)S(1)} %stack_kernel.8.x_ref.refs_0_, bf16[512,1024]{1,0:T(8,128)(2,1)S(1)} %stack_kernel.10.g_ref.refs_0_, bf16[1024,1536]{1,0:T(8,128)(2,1)} %bitcast.15.w_ref), custom_call_target="tpu_custom_call" | custom-call | flops 2684354560 | bytes 7864320 | tf_op jit(solution)/shard_map/ffn_kernel/pallas_call | solution.py:177
  150.4 4.7 %all-to-all-start.2 = ((bf16[8,128,1024]{2,1,0:T(8,128)(2,1)}), bf16[8,128,1024]{2,1,0:T(8,128)(2,1)}, u32[]{:S(2)}, u32[]{:S(2)}) async-start(bf16[8,128,1024]{2,1,0:T(8,128)(2,1)} %bitcast.88), calls=%async_computation.2 | async-start | bytes 4194304 | tf_op jit(solution)/shard_map/all_to_all | solution.py:879
  166.4 11.4 %collective-permute-done.27.refs_2_ = bf16[64,1024]{1,0:T(8,128)(2,1)} collective-permute-done((bf16[64,1024]{1,0:T(8,128)(2,1)}, bf16[64,1024]{1,0:T(8,128)(2,1)}, u32[]{:S(2)}, u32[]{:S(2)}) %collective-permute-start.27) | collective-permute-done | bytes 131104 | tf_op jit(solution)/shard_map/ppermute | solution.py:41
  180.6 3.1 %collective-permute-start.31 = (bf16[64,1024]{1,0:T(8,128)(2,1)S(1)}, bf16[64,1024]{1,0:T(8,128)(2,1)S(1)}, u32[]{:S(2)}, u32[]{:S(2)}) collective-permute-start(bf16[64,1024]{1,0:T(8,128)(2,1)S(1)} %get-tuple-element.119.refs_0_.refs_1_), channel_id=1, source_target_pairs={{0,6},{2,4},{4,2},{6,0},{1,7},{3,5},{5,3},{7,1},{8,14},{10,12},{12... | collective-permute-start | bytes 393224 | tf_op jit(solution)/shard_map/ppermute | solution.py:41
  187.8 3.8 %collective-permute-done.30.refs_2_.refs_3_ = bf16[64,1024]{1,0:T(8,128)(2,1)S(1)} collective-permute-done((bf16[64,1024]{1,0:T(8,128)(2,1)S(1)}, bf16[64,1024]{1,0:T(8,128)(2,1)S(1)}, u32[]{:S(2)}, u32[]{:S(2)}) %collective-permute-start.30) | collective-permute-done | bytes 131104 | tf_op jit(solution)/shard_map/ppermute | solution.py:41
  194.3 6.5 %collective-permute-start.34 = (bf16[128,128]{1,0:T(8,128)(2,1)S(1)}, bf16[128,128]{1,0:T(8,128)(2,1)S(1)}, u32[]{:S(2)}, u32[]{:S(2)}) collective-permute-start(bf16[128,128]{1,0:T(8,128)(2,1)S(1)} %get-tuple-element.122), channel_id=1, source_target_pairs={{0,16},{8,24},{16,0},{24,8},{1,17},{9,25},{17,1},{25,9},{2,18},{10... | collective-permute-start | bytes 98312 | tf_op jit(solution)/shard_map/ppermute | solution.py:41
  217.9 3.6 %all-to-all-start.3 = ((bf16[8,128,640]{2,1,0:T(8,128)(2,1)}), bf16[8,128,640]{2,1,0:T(8,128)(2,1)S(1)}, u32[]{:S(2)}, u32[]{:S(2)}) async-start(bf16[8,128,640]{2,1,0:T(8,128)(2,1)} %after.13), calls=%async_computation.3 | async-start | bytes 2621440 | tf_op jit(solution)/shard_map/all_to_all | solution.py:879
  222.5 5.0 %attn_grads_kernel.1 = (bf16[256,1024]{1,0:T(8,128)(2,1)}, bf16[256,1024]{1,0:T(8,128)(2,1)}, bf16[1024,384]{1,0:T(8,128)(2,1)}, f32[3,1024]{1,0:T(4,128)}) custom-call(s32[1]{0:T(128)} %after.11.me_ref, bf16[128,384]{1,0:T(8,128)(2,1)} %copy-done.52, bf16[128,384]{1,0:T(8,128)(2,1)} %copy-done.60, bf16[128,384]{1,0:T(8,128)(2,1)} %copy-done.61, ...), custom_call_target="tpu_custom_call" | custom-call | flops 805306368 | bytes 4350464 | tf_op jit(solution)/shard_map/attn_grads_kernel/pallas_call | solution.py:177
  237.8 7.7 %collective-permute-done.50.refs_9_ = f32[3,1024]{1,0:T(4,128)S(1)} collective-permute-done((f32[3,1024]{1,0:T(4,128)S(1)}, f32[3,1024]{1,0:T(4,128)S(1)}, u32[]{:S(2)}, u32[]{:S(2)}) %collective-permute-start.50) | collective-permute-done | bytes 12320 | tf_op jit(solution)/shard_map/ppermute | solution.py:41
  250.0 3.5 %collective-permute-start.52 = (bf16[3,16,1024]{2,1,0:T(8,128)(2,1)}, bf16[3,16,1024]{2,1,0:T(8,128)(2,1)S(1)}, u32[]{:S(2)}, u32[]{:S(2)}) collective-permute-start(bf16[3,16,1024]{2,1,0:T(8,128)(2,1)} %get-tuple-element.148), channel_id=1, source_target_pairs={{0,16},{8,24},{16,0},{24,8},{1,17},{9,25},{17,1},{25,9},{2,18},{10... | collective-permute-start | bytes 294920 | tf_op jit(solution)/shard_map/ppermute | solution.py:41
  254.9 3.6 %collective-permute-done.52.refs_2_ = bf16[3,16,1024]{2,1,0:T(8,128)(2,1)S(1)} collective-permute-done((bf16[3,16,1024]{2,1,0:T(8,128)(2,1)}, bf16[3,16,1024]{2,1,0:T(8,128)(2,1)S(1)}, u32[]{:S(2)}, u32[]{:S(2)}) %collective-permute-start.52) | collective-permute-done | bytes 98336 | tf_op jit(solution)/shard_map/ppermute | solution.py:41
  262.5 4.0 %all-to-all-start.4 = ((bf16[8,128,384]{2,1,0:T(8,128)(2,1)}), bf16[8,128,384]{2,1,0:T(8,128)(2,1)S(1)}, u32[]{:S(2)}, u32[]{:S(2)}) async-start(bf16[8,128,384]{2,1,0:T(8,128)(2,1)} %after.15), calls=%async_computation.4 | async-start | bytes 1572864 | tf_op jit(solution)/shard_map/all_to_all | solution.py:879
  269.1 15.1 %adamw.2 = (f32[12288,128]{1,0:T(8,128)}, f32[12288,128]{1,0:T(8,128)}, f32[12288,128]{1,0:T(8,128)}) custom-call(f32[3,1024]{1,0:T(4,128)S(1)} %copy-done.20, bf16[8,128,1024]{2,1,0:T(8,128)(2,1)} %all-to-all-done.2.refs_1_.refs_0_, bf16[8,128,640]{2,1,0:T(8,128)(2,1)S(1)} %all-to-all-done.3.refs_1_, f32[12288,128]{1,0:T(8,128)} %bitcast.90, ...), custom_call_target="tpu_custom_call" | custom-call | flops 31457280 | bytes 40894464 | tf_op jit(solution)/shard_map/adamw/pallas_call | solution.py:987
  286.1 7.0 %adamw.3 = (f32[4096,128]{1,0:T(8,128)}, f32[4096,128]{1,0:T(8,128)}, f32[4096,128]{1,0:T(8,128)}) custom-call(f32[3,1024]{1,0:T(4,128)S(1)} %copy-done.21, bf16[8,128,384]{2,1,0:T(8,128)(2,1)S(1)} %all-to-all-done.4.refs_0_, bf16[8,128,640]{2,1,0:T(8,128)(2,1)} %copy-done.2, f32[4096,128]{1,0:T(8,128)} %bitcast.85, f32[4096,128]{1,0:T(8,128)} %bitcast.95, ...), custom_call_target="tpu_custom_call" | custom-call | flops 10485760 | bytes 13631488 | tf_op jit(solution)/shard_map/adamw/pallas_call | solution.py:987
  (278 shorter events, 118.0 us)
Async XLA Ops:
  15.4 29.8 %all-to-all-start = ((bf16[8,128,512]{2,1,0:T(8,128)(2,1)}), bf16[8,128,512]{2,1,0:T(8,128)(2,1)S(1)}, u32[]{:S(2)}, u32[]{:S(2)}) async-start(bf16[8,128,512]{2,1,0:T(8,128)(2,1)} %after.9), calls=%async_computation | async-start | bytes 2097152 | tf_op jit(solution)/shard_map/all_to_all | solution.py:871
  23.3 13.7 %collective-permute-start.4 = (bf16[64,1024]{1,0:T(8,128)(2,1)S(1)}, bf16[64,1024]{1,0:T(8,128)(2,1)S(1)}, u32[]{:S(2)}, u32[]{:S(2)}) collective-permute-start(bf16[64,1024]{1,0:T(8,128)(2,1)S(1)} %get-tuple-element.89.refs_0_.refs_1_), channel_id=1, source_target_pairs={{0,4},{2,6},{4,0},{6,2},{1,5},{3,7},{5,1},{7,3},{8,12},{10,14},{12... | collective-permute-start | bytes 393224 | tf_op jit(solution)/shard_map/ppermute | solution.py:41
  23.3 13.7 %collective-permute-start.3 = (bf16[64,1024]{1,0:T(8,128)(2,1)S(1)}, bf16[64,1024]{1,0:T(8,128)(2,1)S(1)}, u32[]{:S(2)}, u32[]{:S(2)}) collective-permute-start(bf16[64,1024]{1,0:T(8,128)(2,1)S(1)} %get-tuple-element.89.refs_0_.refs_1_), channel_id=1, source_target_pairs={{0,2},{2,0},{4,6},{6,4},{1,3},{3,1},{5,7},{7,5},{8,10},{10,8},{12,... | collective-permute-start | bytes 393224 | tf_op jit(solution)/shard_map/ppermute | solution.py:41
  46.9 12.6 %collective-permute-start.7 = (bf16[128,384]{1,0:T(8,128)(2,1)S(1)}, bf16[128,384]{1,0:T(8,128)(2,1)S(1)}, u32[]{:S(2)}, u32[]{:S(2)}) collective-permute-start(bf16[128,384]{1,0:T(8,128)(2,1)S(1)} %get-tuple-element.92), channel_id=1, source_target_pairs={{0,8},{8,0},{16,24},{24,16},{1,9},{9,1},{17,25},{25,17},{2,10},{10... | collective-permute-start | bytes 294920 | tf_op jit(solution)/shard_map/ppermute | solution.py:41
  46.9 12.6 %collective-permute-start.8 = (bf16[128,384]{1,0:T(8,128)(2,1)S(1)}, bf16[128,384]{1,0:T(8,128)(2,1)S(1)}, u32[]{:S(2)}, u32[]{:S(2)}) collective-permute-start(bf16[128,384]{1,0:T(8,128)(2,1)S(1)} %get-tuple-element.93), channel_id=1, source_target_pairs={{0,16},{8,24},{16,0},{24,8},{1,17},{9,25},{17,1},{25,9},{2,18},{10... | collective-permute-start | bytes 294920 | tf_op jit(solution)/shard_map/ppermute | solution.py:41
  48.5 11.0 %collective-permute-start.9 = (bf16[128,384]{1,0:T(8,128)(2,1)S(1)}, bf16[128,384]{1,0:T(8,128)(2,1)S(1)}, u32[]{:S(2)}, u32[]{:S(2)}) collective-permute-start(bf16[128,384]{1,0:T(8,128)(2,1)S(1)} %get-tuple-element.94), channel_id=1, source_target_pairs={{0,24},{8,16},{16,8},{24,0},{1,25},{9,17},{17,9},{25,1},{2,26},{10... | collective-permute-start | bytes 294920 | tf_op jit(solution)/shard_map/ppermute | solution.py:41
  68.7 72.8 %all-to-all-start.1 = ((bf16[8,128,1536]{2,1,0:T(8,128)(2,1)}), bf16[8,128,1536]{2,1,0:T(8,128)(2,1)}, u32[]{:S(2)}, u32[]{:S(2)}) async-start(bf16[8,128,1536]{2,1,0:T(8,128)(2,1)} %after.10), calls=%async_computation.1 | async-start | bytes 6291456 | tf_op jit(solution)/shard_map/all_to_all | solution.py:871
  77.7 37.5 %collective-permute-start.15 = (bf16[64,1024]{1,0:T(8,128)(2,1)S(1)}, bf16[64,1024]{1,0:T(8,128)(2,1)S(1)}, u32[]{:S(2)}, u32[]{:S(2)}) collective-permute-start(bf16[64,1024]{1,0:T(8,128)(2,1)S(1)} %get-tuple-element.103), channel_id=1, source_target_pairs={{0,4},{2,6},{4,0},{6,2},{1,5},{3,7},{5,1},{7,3},{8,12},{10,14},{12... | collective-permute-start | bytes 393224 | tf_op jit(solution)/shard_map/ppermute | solution.py:41
  79.7 35.5 %collective-permute-start.16 = (bf16[64,1024]{1,0:T(8,128)(2,1)S(1)}, bf16[64,1024]{1,0:T(8,128)(2,1)S(1)}, u32[]{:S(2)}, u32[]{:S(2)}) collective-permute-start(bf16[64,1024]{1,0:T(8,128)(2,1)S(1)} %get-tuple-element.104), channel_id=1, source_target_pairs={{0,6},{2,4},{4,2},{6,0},{1,7},{3,5},{5,3},{7,1},{8,14},{10,12},{12... | collective-permute-start | bytes 393224 | tf_op jit(solution)/shard_map/ppermute | solution.py:41
  79.7 39.5 %collective-permute-start.23 = (bf16[64,1024]{1,0:T(8,128)(2,1)S(1)}, bf16[64,1024]{1,0:T(8,128)(2,1)S(1)}, u32[]{:S(2)}, u32[]{:S(2)}) collective-permute-start(bf16[64,1024]{1,0:T(8,128)(2,1)S(1)} %get-tuple-element.107.refs_0_), channel_id=1, source_target_pairs={{0,6},{2,4},{4,2},{6,0},{1,7},{3,5},{5,3},{7,1},{8,14},{10,12},{12... | collective-permute-start | bytes 393224 | tf_op jit(solution)/shard_map/ppermute | solution.py:41
  82.6 37.4 %collective-permute-start.22 = (bf16[64,1024]{1,0:T(8,128)(2,1)S(1)}, bf16[64,1024]{1,0:T(8,128)(2,1)S(1)}, u32[]{:S(2)}, u32[]{:S(2)}) collective-permute-start(bf16[64,1024]{1,0:T(8,128)(2,1)S(1)} %get-tuple-element.107.refs_0_), channel_id=1, source_target_pairs={{0,4},{2,6},{4,0},{6,2},{1,5},{3,7},{5,1},{7,3},{8,12},{10,14},{12... | collective-permute-start | bytes 393224 | tf_op jit(solution)/shard_map/ppermute | solution.py:41
  82.6 37.4 %collective-permute-start.21 = (bf16[64,1024]{1,0:T(8,128)(2,1)S(1)}, bf16[64,1024]{1,0:T(8,128)(2,1)S(1)}, u32[]{:S(2)}, u32[]{:S(2)}) collective-permute-start(bf16[64,1024]{1,0:T(8,128)(2,1)S(1)} %get-tuple-element.107.refs_0_), channel_id=1, source_target_pairs={{0,2},{2,0},{4,6},{6,4},{1,3},{3,1},{5,7},{7,5},{8,10},{10,8},{12,... | collective-permute-start | bytes 393224 | tf_op jit(solution)/shard_map/ppermute | solution.py:41
  150.4 67.4 %all-to-all-start.2 = ((bf16[8,128,1024]{2,1,0:T(8,128)(2,1)}), bf16[8,128,1024]{2,1,0:T(8,128)(2,1)}, u32[]{:S(2)}, u32[]{:S(2)}) async-start(bf16[8,128,1024]{2,1,0:T(8,128)(2,1)} %bitcast.88), calls=%async_computation.2 | async-start | bytes 4194304 | tf_op jit(solution)/shard_map/all_to_all | solution.py:879
  160.2 17.5 %collective-permute-start.27 = (bf16[64,1024]{1,0:T(8,128)(2,1)}, bf16[64,1024]{1,0:T(8,128)(2,1)}, u32[]{:S(2)}, u32[]{:S(2)}) collective-permute-start(bf16[64,1024]{1,0:T(8,128)(2,1)} %get-tuple-element.115), channel_id=1, source_target_pairs={{0,4},{2,6},{4,0},{6,2},{1,5},{3,7},{5,1},{7,3},{8,12},{10,14},{12... | collective-permute-start | bytes 393224 | tf_op jit(solution)/shard_map/ppermute | solution.py:41
  161.9 15.9 %collective-permute-start.28 = (bf16[64,1024]{1,0:T(8,128)(2,1)}, bf16[64,1024]{1,0:T(8,128)(2,1)}, u32[]{:S(2)}, u32[]{:S(2)}) collective-permute-start(bf16[64,1024]{1,0:T(8,128)(2,1)} %get-tuple-element.116), channel_id=1, source_target_pairs={{0,6},{2,4},{4,2},{6,0},{1,7},{3,5},{5,3},{7,1},{8,14},{10,12},{12... | collective-permute-start | bytes 393224 | tf_op jit(solution)/shard_map/ppermute | solution.py:41
  192.0 17.6 %collective-permute-start.44 = (bf16[64,1024]{1,0:T(8,128)(2,1)S(1)}, bf16[64,1024]{1,0:T(8,128)(2,1)S(1)}, u32[]{:S(2)}, u32[]{:S(2)}) collective-permute-start(bf16[64,1024]{1,0:T(8,128)(2,1)S(1)} %get-tuple-element.141), channel_id=1, source_target_pairs={{0,2},{2,0},{4,6},{6,4},{1,3},{3,1},{5,7},{7,5},{8,10},{10,8},{12,... | collective-permute-start | bytes 393224 | tf_op jit(solution)/shard_map/ppermute | solution.py:41
  202.2 12.2 %collective-permute-start.45 = (bf16[64,1024]{1,0:T(8,128)(2,1)S(1)}, bf16[64,1024]{1,0:T(8,128)(2,1)S(1)}, u32[]{:S(2)}, u32[]{:S(2)}) collective-permute-start(bf16[64,1024]{1,0:T(8,128)(2,1)S(1)} %get-tuple-element.142), channel_id=1, source_target_pairs={{0,4},{2,6},{4,0},{6,2},{1,5},{3,7},{5,1},{7,3},{8,12},{10,14},{12... | collective-permute-start | bytes 393224 | tf_op jit(solution)/shard_map/ppermute | solution.py:41
  217.9 44.6 %all-to-all-start.3 = ((bf16[8,128,640]{2,1,0:T(8,128)(2,1)}), bf16[8,128,640]{2,1,0:T(8,128)(2,1)S(1)}, u32[]{:S(2)}, u32[]{:S(2)}) async-start(bf16[8,128,640]{2,1,0:T(8,128)(2,1)} %after.13), calls=%async_computation.3 | async-start | bytes 2621440 | tf_op jit(solution)/shard_map/all_to_all | solution.py:879
  231.5 14.1 %collective-permute-start.40 = (bf16[64,1024]{1,0:T(8,128)(2,1)S(1)}, bf16[64,1024]{1,0:T(8,128)(2,1)S(1)}, u32[]{:S(2)}, u32[]{:S(2)}) collective-permute-start(bf16[64,1024]{1,0:T(8,128)(2,1)S(1)} %get-tuple-element.137), channel_id=1, source_target_pairs={{0,2},{2,0},{4,6},{6,4},{1,3},{3,1},{5,7},{7,5},{8,10},{10,8},{12,... | collective-permute-start | bytes 393224 | tf_op jit(solution)/shard_map/ppermute | solution.py:41
  233.0 12.6 %collective-permute-start.41 = (bf16[64,1024]{1,0:T(8,128)(2,1)S(1)}, bf16[64,1024]{1,0:T(8,128)(2,1)S(1)}, u32[]{:S(2)}, u32[]{:S(2)}) collective-permute-start(bf16[64,1024]{1,0:T(8,128)(2,1)S(1)} %get-tuple-element.138), channel_id=1, source_target_pairs={{0,4},{2,6},{4,0},{6,2},{1,5},{3,7},{5,1},{7,3},{8,12},{10,14},{12... | collective-permute-start | bytes 393224 | tf_op jit(solution)/shard_map/ppermute | solution.py:41
  262.5 23.0 %all-to-all-start.4 = ((bf16[8,128,384]{2,1,0:T(8,128)(2,1)}), bf16[8,128,384]{2,1,0:T(8,128)(2,1)S(1)}, u32[]{:S(2)}, u32[]{:S(2)}) async-start(bf16[8,128,384]{2,1,0:T(8,128)(2,1)} %after.15), calls=%async_computation.4 | async-start | bytes 1572864 | tf_op jit(solution)/shard_map/all_to_all | solution.py:879
  266.4 17.8 %collective-permute-start.56 = (bf16[4,2,16,1024]{3,2,1,0:T(8,128)(2,1)S(1)}, bf16[4,2,16,1024]{3,2,1,0:T(8,128)(2,1)S(1)}, u32[]{:S(2)}, u32[]{:S(2)}) collective-permute-start(bf16[4,2,16,1024]{3,2,1,0:T(8,128)(2,1)S(1)} %get-tuple-element.150.refs_0_), channel_id=1, source_target_pairs={{0,3},{1,2},{2,1},{3,0},{4,7},{5,6},{6,5},{7,4},{8,11},{9,10},{10,... | collective-permute-start | bytes 786440 | tf_op jit(solution)/shard_map/ppermute | solution.py:41
  266.5 17.8 %collective-permute-start.55 = (bf16[4,2,16,1024]{3,2,1,0:T(8,128)(2,1)S(1)}, bf16[4,2,16,1024]{3,2,1,0:T(8,128)(2,1)S(1)}, u32[]{:S(2)}, u32[]{:S(2)}) collective-permute-start(bf16[4,2,16,1024]{3,2,1,0:T(8,128)(2,1)S(1)} %get-tuple-element.150.refs_0_), channel_id=1, source_target_pairs={{0,2},{1,3},{2,0},{3,1},{4,6},{5,7},{6,4},{7,5},{8,10},{9,11},{10,... | collective-permute-start | bytes 786440 | tf_op jit(solution)/shard_map/ppermute | solution.py:41
  267.6 16.6 %collective-permute-start.54 = (bf16[4,2,16,1024]{3,2,1,0:T(8,128)(2,1)S(1)}, bf16[4,2,16,1024]{3,2,1,0:T(8,128)(2,1)S(1)}, u32[]{:S(2)}, u32[]{:S(2)}) collective-permute-start(bf16[4,2,16,1024]{3,2,1,0:T(8,128)(2,1)S(1)} %get-tuple-element.150.refs_0_), channel_id=1, source_target_pairs={{0,1},{1,0},{2,3},{3,2},{4,5},{5,4},{6,7},{7,6},{8,9},{9,8},{10,11... | collective-permute-start | bytes 786440 | tf_op jit(solution)/shard_map/ppermute | solution.py:41
  (103 other events, 1071.4 us)

commit v4 on v3

--- a/solution.py
+++ b/solution.py
@@ -19,7 +19,7 @@
 ADAM_EPS = 1e-08
 CLIP_NORM = 1.0
 
-VMEM_LIMIT = 16 << 20
+VMEM_LIMIT = 28 << 20
 
 BF = jnp.bfloat16
 F32 = jnp.float32

time: 294 us -> 294 us (level)
  no operation moved by 1% of the time
where the time goes in v4:
time: 294 us; the launch traced here: 293 us
  waiting for transfers between devices  120 us (41%)
  starting transfers between devices  89 us (30%)
  Pallas kernels  56.1 us (19%)
  local copies, waits for them, and re-layouts  22.6 us (8%)
    ppermute x57, waiting for transfers between devices, hop(): return lax.ppermute(value, axes, [(i, i ^ step) for i in range(n)])  98.2 us
    ppermute x57, starting transfers between devices, hop(): return lax.ppermute(value, axes, [(i, i ^ step) for i in range(n)])  66.9 us
    pallas_call x2, Pallas kernels, adamw_owned(): pl.pallas_call(functools.partial(adamw_kernel, (kinds, cols // 128, depth...  22.1 us
    pallas_call x24, Pallas kernels, vmem_call(): pl.pallas_call(kernel, out_shape=list(outs), in_specs=[pl.BlockSpec(memor...  21.8 us
    all_to_all x2, waiting for transfers between devices, to_planes(): full = lax.all_to_all(low, OWNERS, 0, 0, tiled=True)  21.4 us
    unnamed x130, local copies, waits for them, and re-layouts  19.5 us
    all_to_all x3, starting transfers between devices, to_owners(): return lax.all_to_all(chunks, OWNERS, 0, 0, tiled=True)  12.3 us
    all_to_all x2, starting transfers between devices, to_planes(): full = lax.all_to_all(low, OWNERS, 0, 0, tiled=True)  9.76 us
  transfers between devices with their start and end apart: 62, of which 26 were waited for; matrix products, arithmetic and copies ran while one was open for 2% of the time, Pallas kernels for 14%

profile of v4, /device:TPU:0, one launch (start us, length us, event | category | flops | bytes accessed | tf_op | source)
XLA Modules:
  0.0 293.3 jit_solution(6698473688851980038)
XLA Ops:
  2.5 5.1 %collective-permute-start.2 = (bf16[2,16,1152]{2,1,0:T(8,128)(2,1)S(1)}, bf16[2,16,1152]{2,1,0:T(8,128)(2,1)S(1)}, u32[]{:S(2)}, u32[]{:S(2)}) collective-permute-start(bf16[2,16,1152]{2,1,0:T(8,128)(2,1)S(1)} %get-tuple-element.168), channel_id=1, source_target_pairs={{0,24},{8,16},{16,8},{24,0},{1,25},{9,17},{17,9},{25,1},{2,26},{10... | collective-permute-start | bytes 221192 | tf_op jit(solution)/shard_map/ppermute | solution.py:41
  15.4 5.0 %all-to-all-start = ((bf16[8,128,512]{2,1,0:T(8,128)(2,1)}), bf16[8,128,512]{2,1,0:T(8,128)(2,1)S(1)}, u32[]{:S(2)}, u32[]{:S(2)}) async-start(bf16[8,128,512]{2,1,0:T(8,128)(2,1)} %after.9), calls=%async_computation | async-start | bytes 2097152 | tf_op jit(solution)/shard_map/all_to_all | solution.py:871
  23.9 4.3 %collective-permute-done.5.refs_3_.refs_4_ = bf16[64,1024]{1,0:T(8,128)(2,1)S(1)} collective-permute-done((bf16[64,1024]{1,0:T(8,128)(2,1)S(1)}, bf16[64,1024]{1,0:T(8,128)(2,1)S(1)}, u32[]{:S(2)}, u32[]{:S(2)}) %collective-permute-start.5) | collective-permute-done | bytes 131104 | tf_op jit(solution)/shard_map/ppermute | solution.py:41
  28.2 8.8 %collective-permute-done.4.refs_2_.refs_3_ = bf16[64,1024]{1,0:T(8,128)(2,1)S(1)} collective-permute-done((bf16[64,1024]{1,0:T(8,128)(2,1)S(1)}, bf16[64,1024]{1,0:T(8,128)(2,1)S(1)}, u32[]{:S(2)}, u32[]{:S(2)}) %collective-permute-start.4) | collective-permute-done | bytes 131104 | tf_op jit(solution)/shard_map/ppermute | solution.py:41
  39.0 6.2 %all-to-all-done = bf16[8,128,512]{2,1,0:T(8,128)(2,1)S(1)} async-done(((bf16[8,128,512]{2,1,0:T(8,128)(2,1)}), bf16[8,128,512]{2,1,0:T(8,128)(2,1)S(1)}, u32[]{:S(2)}, u32[]{:S(2)}) %all-to-all-start) | async-done | bytes 1048608 | tf_op jit(solution)/shard_map/all_to_all | solution.py:871
  51.3 6.0 %split_weights.2.refs_1_.refs_0_ = bf16[8,128,1536]{2,1,0:T(8,128)(2,1)S(1)} custom-call(f32[12288,128]{1,0:T(8,128)} %bitcast.89), custom_call_target="tpu_custom_call" | custom-call | flops 1572864 | bytes 9437184 | tf_op jit(solution)/shard_map/split_weights/pallas_call | solution.py:833
  68.7 4.8 %all-to-all-start.1 = ((bf16[8,128,1536]{2,1,0:T(8,128)(2,1)}), bf16[8,128,1536]{2,1,0:T(8,128)(2,1)}, u32[]{:S(2)}, u32[]{:S(2)}) async-start(bf16[8,128,1536]{2,1,0:T(8,128)(2,1)} %after.10), calls=%async_computation.1 | async-start | bytes 6291456 | tf_op jit(solution)/shard_map/all_to_all | solution.py:871
  84.0 31.1 %collective-permute-done.15.refs_2_ = bf16[64,1024]{1,0:T(8,128)(2,1)S(1)} collective-permute-done((bf16[64,1024]{1,0:T(8,128)(2,1)S(1)}, bf16[64,1024]{1,0:T(8,128)(2,1)S(1)}, u32[]{:S(2)}, u32[]{:S(2)}) %collective-permute-start.15) | collective-permute-done | bytes 131104 | tf_op jit(solution)/shard_map/ppermute | solution.py:41
  116.2 3.0 %collective-permute-start.18 = (bf16[64,1024]{1,0:T(8,128)(2,1)S(1)}, bf16[64,1024]{1,0:T(8,128)(2,1)S(1)}, u32[]{:S(2)}, u32[]{:S(2)}) collective-permute-start(bf16[64,1024]{1,0:T(8,128)(2,1)S(1)} %get-tuple-element.106.refs_0_), channel_id=1, source_target_pairs={{0,4},{2,6},{4,0},{6,2},{1,5},{3,7},{5,1},{7,3},{8,12},{10,14},{12... | collective-permute-start | bytes 393224 | tf_op jit(solution)/shard_map/ppermute | solution.py:41
  126.3 15.2 %all-to-all-done.1 = bf16[8,128,1536]{2,1,0:T(8,128)(2,1)} async-done(((bf16[8,128,1536]{2,1,0:T(8,128)(2,1)}), bf16[8,128,1536]{2,1,0:T(8,128)(2,1)}, u32[]{:S(2)}, u32[]{:S(2)}) %all-to-all-start.1) | async-done | bytes 3145760 | tf_op jit(solution)/shard_map/all_to_all | solution.py:871
  141.5 5.1 %ffn_kernel.1 = (bf16[512,512]{1,0:T(8,128)(2,1)S(1)}, bf16[512,1024]{1,0:T(8,128)(2,1)S(1)}, bf16[256,1024]{1,0:T(8,128)(2,1)S(1)}, bf16[256,1024]{1,0:T(8,128)(2,1)S(1)}) custom-call(bf16[512,1024]{1,0:T(8,128)(2,1)S(1)} %stack_kernel.8.x_ref.refs_0_, bf16[512,1024]{1,0:T(8,128)(2,1)S(1)} %stack_kernel.10.g_ref.refs_0_, bf16[1024,1536]{1,0:T(8,128)(2,1)} %bitcast.15.w_ref), custom_call_target="tpu_custom_call" | custom-call | flops 2684354560 | bytes 7864320 | tf_op jit(solution)/shard_map/ffn_kernel/pallas_call | solution.py:177
  150.4 4.7 %all-to-all-start.2 = ((bf16[8,128,1024]{2,1,0:T(8,128)(2,1)}), bf16[8,128,1024]{2,1,0:T(8,128)(2,1)}, u32[]{:S(2)}, u32[]{:S(2)}) async-start(bf16[8,128,1024]{2,1,0:T(8,128)(2,1)} %bitcast.88), calls=%async_computation.2 | async-start | bytes 4194304 | tf_op jit(solution)/shard_map/all_to_all | solution.py:879
  166.4 11.4 %collective-permute-done.27.refs_2_ = bf16[64,1024]{1,0:T(8,128)(2,1)} collective-permute-done((bf16[64,1024]{1,0:T(8,128)(2,1)}, bf16[64,1024]{1,0:T(8,128)(2,1)}, u32[]{:S(2)}, u32[]{:S(2)}) %collective-permute-start.27) | collective-permute-done | bytes 131104 | tf_op jit(solution)/shard_map/ppermute | solution.py:41
  180.6 3.1 %collective-permute-start.31 = (bf16[64,1024]{1,0:T(8,128)(2,1)S(1)}, bf16[64,1024]{1,0:T(8,128)(2,1)S(1)}, u32[]{:S(2)}, u32[]{:S(2)}) collective-permute-start(bf16[64,1024]{1,0:T(8,128)(2,1)S(1)} %get-tuple-element.119.refs_0_.refs_1_), channel_id=1, source_target_pairs={{0,6},{2,4},{4,2},{6,0},{1,7},{3,5},{5,3},{7,1},{8,14},{10,12},{12... | collective-permute-start | bytes 393224 | tf_op jit(solution)/shard_map/ppermute | solution.py:41
  187.8 3.8 %collective-permute-done.30.refs_2_.refs_3_ = bf16[64,1024]{1,0:T(8,128)(2,1)S(1)} collective-permute-done((bf16[64,1024]{1,0:T(8,128)(2,1)S(1)}, bf16[64,1024]{1,0:T(8,128)(2,1)S(1)}, u32[]{:S(2)}, u32[]{:S(2)}) %collective-permute-start.30) | collective-permute-done | bytes 131104 | tf_op jit(solution)/shard_map/ppermute | solution.py:41
  194.3 6.5 %collective-permute-start.34 = (bf16[128,128]{1,0:T(8,128)(2,1)S(1)}, bf16[128,128]{1,0:T(8,128)(2,1)S(1)}, u32[]{:S(2)}, u32[]{:S(2)}) collective-permute-start(bf16[128,128]{1,0:T(8,128)(2,1)S(1)} %get-tuple-element.122), channel_id=1, source_target_pairs={{0,16},{8,24},{16,0},{24,8},{1,17},{9,25},{17,1},{25,9},{2,18},{10... | collective-permute-start | bytes 98312 | tf_op jit(solution)/shard_map/ppermute | solution.py:41
  217.9 3.6 %all-to-all-start.3 = ((bf16[8,128,640]{2,1,0:T(8,128)(2,1)}), bf16[8,128,640]{2,1,0:T(8,128)(2,1)S(1)}, u32[]{:S(2)}, u32[]{:S(2)}) async-start(bf16[8,128,640]{2,1,0:T(8,128)(2,1)} %after.13), calls=%async_computation.3 | async-start | bytes 2621440 | tf_op jit(solution)/shard_map/all_to_all | solution.py:879
  222.5 5.0 %attn_grads_kernel.1 = (bf16[256,1024]{1,0:T(8,128)(2,1)}, bf16[256,1024]{1,0:T(8,128)(2,1)}, bf16[1024,384]{1,0:T(8,128)(2,1)}, f32[3,1024]{1,0:T(4,128)}) custom-call(s32[1]{0:T(128)} %after.11.me_ref, bf16[128,384]{1,0:T(8,128)(2,1)} %copy-done.52, bf16[128,384]{1,0:T(8,128)(2,1)} %copy-done.60, bf16[128,384]{1,0:T(8,128)(2,1)} %copy-done.61, ...), custom_call_target="tpu_custom_call" | custom-call | flops 805306368 | bytes 4350464 | tf_op jit(solution)/shard_map/attn_grads_kernel/pallas_call | solution.py:177
  237.8 7.7 %collective-permute-done.50.refs_9_ = f32[3,1024]{1,0:T(4,128)S(1)} collective-permute-done((f32[3,1024]{1,0:T(4,128)S(1)}, f32[3,1024]{1,0:T(4,128)S(1)}, u32[]{:S(2)}, u32[]{:S(2)}) %collective-permute-start.50) | collective-permute-done | bytes 12320 | tf_op jit(solution)/shard_map/ppermute | solution.py:41
  250.0 3.5 %collective-permute-start.52 = (bf16[3,16,1024]{2,1,0:T(8,128)(2,1)}, bf16[3,16,1024]{2,1,0:T(8,128)(2,1)S(1)}, u32[]{:S(2)}, u32[]{:S(2)}) collective-permute-start(bf16[3,16,1024]{2,1,0:T(8,128)(2,1)} %get-tuple-element.148), channel_id=1, source_target_pairs={{0,16},{8,24},{16,0},{24,8},{1,17},{9,25},{17,1},{25,9},{2,18},{10... | collective-permute-start | bytes 294920 | tf_op jit(solution)/shard_map/ppermute | solution.py:41
  254.9 3.6 %collective-permute-done.52.refs_2_ = bf16[3,16,1024]{2,1,0:T(8,128)(2,1)S(1)} collective-permute-done((bf16[3,16,1024]{2,1,0:T(8,128)(2,1)}, bf16[3,16,1024]{2,1,0:T(8,128)(2,1)S(1)}, u32[]{:S(2)}, u32[]{:S(2)}) %collective-permute-start.52) | collective-permute-done | bytes 98336 | tf_op jit(solution)/shard_map/ppermute | solution.py:41
  262.5 4.0 %all-to-all-start.4 = ((bf16[8,128,384]{2,1,0:T(8,128)(2,1)}), bf16[8,128,384]{2,1,0:T(8,128)(2,1)S(1)}, u32[]{:S(2)}, u32[]{:S(2)}) async-start(bf16[8,128,384]{2,1,0:T(8,128)(2,1)} %after.15), calls=%async_computation.4 | async-start | bytes 1572864 | tf_op jit(solution)/shard_map/all_to_all | solution.py:879
  269.1 15.1 %adamw.2 = (f32[12288,128]{1,0:T(8,128)}, f32[12288,128]{1,0:T(8,128)}, f32[12288,128]{1,0:T(8,128)}) custom-call(f32[3,1024]{1,0:T(4,128)S(1)} %copy-done.20, bf16[8,128,1024]{2,1,0:T(8,128)(2,1)} %all-to-all-done.2.refs_1_.refs_0_, bf16[8,128,640]{2,1,0:T(8,128)(2,1)S(1)} %all-to-all-done.3.refs_1_, f32[12288,128]{1,0:T(8,128)} %bitcast.90, ...), custom_call_target="tpu_custom_call" | custom-call | flops 31457280 | bytes 40894464 | tf_op jit(solution)/shard_map/adamw/pallas_call | solution.py:987
  286.1 7.0 %adamw.3 = (f32[4096,128]{1,0:T(8,128)}, f32[4096,128]{1,0:T(8,128)}, f32[4096,128]{1,0:T(8,128)}) custom-call(f32[3,1024]{1,0:T(4,128)S(1)} %copy-done.21, bf16[8,128,384]{2,1,0:T(8,128)(2,1)S(1)} %all-to-all-done.4.refs_0_, bf16[8,128,640]{2,1,0:T(8,128)(2,1)} %copy-done.2, f32[4096,128]{1,0:T(8,128)} %bitcast.85, f32[4096,128]{1,0:T(8,128)} %bitcast.95, ...), custom_call_target="tpu_custom_call" | custom-call | flops 10485760 | bytes 13631488 | tf_op jit(solution)/shard_map/adamw/pallas_call | solution.py:987
  (278 shorter events, 118.0 us)
Async XLA Ops:
  15.4 29.8 %all-to-all-start = ((bf16[8,128,512]{2,1,0:T(8,128)(2,1)}), bf16[8,128,512]{2,1,0:T(8,128)(2,1)S(1)}, u32[]{:S(2)}, u32[]{:S(2)}) async-start(bf16[8,128,512]{2,1,0:T(8,128)(2,1)} %after.9), calls=%async_computation | async-start | bytes 2097152 | tf_op jit(solution)/shard_map/all_to_all | solution.py:871
  23.3 13.7 %collective-permute-start.4 = (bf16[64,1024]{1,0:T(8,128)(2,1)S(1)}, bf16[64,1024]{1,0:T(8,128)(2,1)S(1)}, u32[]{:S(2)}, u32[]{:S(2)}) collective-permute-start(bf16[64,1024]{1,0:T(8,128)(2,1)S(1)} %get-tuple-element.89.refs_0_.refs_1_), channel_id=1, source_target_pairs={{0,4},{2,6},{4,0},{6,2},{1,5},{3,7},{5,1},{7,3},{8,12},{10,14},{12... | collective-permute-start | bytes 393224 | tf_op jit(solution)/shard_map/ppermute | solution.py:41
  23.3 13.7 %collective-permute-start.3 = (bf16[64,1024]{1,0:T(8,128)(2,1)S(1)}, bf16[64,1024]{1,0:T(8,128)(2,1)S(1)}, u32[]{:S(2)}, u32[]{:S(2)}) collective-permute-start(bf16[64,1024]{1,0:T(8,128)(2,1)S(1)} %get-tuple-element.89.refs_0_.refs_1_), channel_id=1, source_target_pairs={{0,2},{2,0},{4,6},{6,4},{1,3},{3,1},{5,7},{7,5},{8,10},{10,8},{12,... | collective-permute-start | bytes 393224 | tf_op jit(solution)/shard_map/ppermute | solution.py:41
  46.9 12.6 %collective-permute-start.7 = (bf16[128,384]{1,0:T(8,128)(2,1)S(1)}, bf16[128,384]{1,0:T(8,128)(2,1)S(1)}, u32[]{:S(2)}, u32[]{:S(2)}) collective-permute-start(bf16[128,384]{1,0:T(8,128)(2,1)S(1)} %get-tuple-element.92), channel_id=1, source_target_pairs={{0,8},{8,0},{16,24},{24,16},{1,9},{9,1},{17,25},{25,17},{2,10},{10... | collective-permute-start | bytes 294920 | tf_op jit(solution)/shard_map/ppermute | solution.py:41
  46.9 12.6 %collective-permute-start.8 = (bf16[128,384]{1,0:T(8,128)(2,1)S(1)}, bf16[128,384]{1,0:T(8,128)(2,1)S(1)}, u32[]{:S(2)}, u32[]{:S(2)}) collective-permute-start(bf16[128,384]{1,0:T(8,128)(2,1)S(1)} %get-tuple-element.93), channel_id=1, source_target_pairs={{0,16},{8,24},{16,0},{24,8},{1,17},{9,25},{17,1},{25,9},{2,18},{10... | collective-permute-start | bytes 294920 | tf_op jit(solution)/shard_map/ppermute | solution.py:41
  48.5 11.0 %collective-permute-start.9 = (bf16[128,384]{1,0:T(8,128)(2,1)S(1)}, bf16[128,384]{1,0:T(8,128)(2,1)S(1)}, u32[]{:S(2)}, u32[]{:S(2)}) collective-permute-start(bf16[128,384]{1,0:T(8,128)(2,1)S(1)} %get-tuple-element.94), channel_id=1, source_target_pairs={{0,24},{8,16},{16,8},{24,0},{1,25},{9,17},{17,9},{25,1},{2,26},{10... | collective-permute-start | bytes 294920 | tf_op jit(solution)/shard_map/ppermute | solution.py:41
  68.7 72.8 %all-to-all-start.1 = ((bf16[8,128,1536]{2,1,0:T(8,128)(2,1)}), bf16[8,128,1536]{2,1,0:T(8,128)(2,1)}, u32[]{:S(2)}, u32[]{:S(2)}) async-start(bf16[8,128,1536]{2,1,0:T(8,128)(2,1)} %after.10), calls=%async_computation.1 | async-start | bytes 6291456 | tf_op jit(solution)/shard_map/all_to_all | solution.py:871
  77.7 37.5 %collective-permute-start.15 = (bf16[64,1024]{1,0:T(8,128)(2,1)S(1)}, bf16[64,1024]{1,0:T(8,128)(2,1)S(1)}, u32[]{:S(2)}, u32[]{:S(2)}) collective-permute-start(bf16[64,1024]{1,0:T(8,128)(2,1)S(1)} %get-tuple-element.103), channel_id=1, source_target_pairs={{0,4},{2,6},{4,0},{6,2},{1,5},{3,7},{5,1},{7,3},{8,12},{10,14},{12... | collective-permute-start | bytes 393224 | tf_op jit(solution)/shard_map/ppermute | solution.py:41
  79.7 35.5 %collective-permute-start.16 = (bf16[64,1024]{1,0:T(8,128)(2,1)S(1)}, bf16[64,1024]{1,0:T(8,128)(2,1)S(1)}, u32[]{:S(2)}, u32[]{:S(2)}) collective-permute-start(bf16[64,1024]{1,0:T(8,128)(2,1)S(1)} %get-tuple-element.104), channel_id=1, source_target_pairs={{0,6},{2,4},{4,2},{6,0},{1,7},{3,5},{5,3},{7,1},{8,14},{10,12},{12... | collective-permute-start | bytes 393224 | tf_op jit(solution)/shard_map/ppermute | solution.py:41
  79.7 39.5 %collective-permute-start.23 = (bf16[64,1024]{1,0:T(8,128)(2,1)S(1)}, bf16[64,1024]{1,0:T(8,128)(2,1)S(1)}, u32[]{:S(2)}, u32[]{:S(2)}) collective-permute-start(bf16[64,1024]{1,0:T(8,128)(2,1)S(1)} %get-tuple-element.107.refs_0_), channel_id=1, source_target_pairs={{0,6},{2,4},{4,2},{6,0},{1,7},{3,5},{5,3},{7,1},{8,14},{10,12},{12... | collective-permute-start | bytes 393224 | tf_op jit(solution)/shard_map/ppermute | solution.py:41
  82.6 37.4 %collective-permute-start.22 = (bf16[64,1024]{1,0:T(8,128)(2,1)S(1)}, bf16[64,1024]{1,0:T(8,128)(2,1)S(1)}, u32[]{:S(2)}, u32[]{:S(2)}) collective-permute-start(bf16[64,1024]{1,0:T(8,128)(2,1)S(1)} %get-tuple-element.107.refs_0_), channel_id=1, source_target_pairs={{0,4},{2,6},{4,0},{6,2},{1,5},{3,7},{5,1},{7,3},{8,12},{10,14},{12... | collective-permute-start | bytes 393224 | tf_op jit(solution)/shard_map/ppermute | solution.py:41
  82.6 37.4 %collective-permute-start.21 = (bf16[64,1024]{1,0:T(8,128)(2,1)S(1)}, bf16[64,1024]{1,0:T(8,128)(2,1)S(1)}, u32[]{:S(2)}, u32[]{:S(2)}) collective-permute-start(bf16[64,1024]{1,0:T(8,128)(2,1)S(1)} %get-tuple-element.107.refs_0_), channel_id=1, source_target_pairs={{0,2},{2,0},{4,6},{6,4},{1,3},{3,1},{5,7},{7,5},{8,10},{10,8},{12,... | collective-permute-start | bytes 393224 | tf_op jit(solution)/shard_map/ppermute | solution.py:41
  150.4 67.4 %all-to-all-start.2 = ((bf16[8,128,1024]{2,1,0:T(8,128)(2,1)}), bf16[8,128,1024]{2,1,0:T(8,128)(2,1)}, u32[]{:S(2)}, u32[]{:S(2)}) async-start(bf16[8,128,1024]{2,1,0:T(8,128)(2,1)} %bitcast.88), calls=%async_computation.2 | async-start | bytes 4194304 | tf_op jit(solution)/shard_map/all_to_all | solution.py:879
  160.2 17.5 %collective-permute-start.27 = (bf16[64,1024]{1,0:T(8,128)(2,1)}, bf16[64,1024]{1,0:T(8,128)(2,1)}, u32[]{:S(2)}, u32[]{:S(2)}) collective-permute-start(bf16[64,1024]{1,0:T(8,128)(2,1)} %get-tuple-element.115), channel_id=1, source_target_pairs={{0,4},{2,6},{4,0},{6,2},{1,5},{3,7},{5,1},{7,3},{8,12},{10,14},{12... | collective-permute-start | bytes 393224 | tf_op jit(solution)/shard_map/ppermute | solution.py:41
  161.9 15.9 %collective-permute-start.28 = (bf16[64,1024]{1,0:T(8,128)(2,1)}, bf16[64,1024]{1,0:T(8,128)(2,1)}, u32[]{:S(2)}, u32[]{:S(2)}) collective-permute-start(bf16[64,1024]{1,0:T(8,128)(2,1)} %get-tuple-element.116), channel_id=1, source_target_pairs={{0,6},{2,4},{4,2},{6,0},{1,7},{3,5},{5,3},{7,1},{8,14},{10,12},{12... | collective-permute-start | bytes 393224 | tf_op jit(solution)/shard_map/ppermute | solution.py:41
  192.0 17.6 %collective-permute-start.44 = (bf16[64,1024]{1,0:T(8,128)(2,1)S(1)}, bf16[64,1024]{1,0:T(8,128)(2,1)S(1)}, u32[]{:S(2)}, u32[]{:S(2)}) collective-permute-start(bf16[64,1024]{1,0:T(8,128)(2,1)S(1)} %get-tuple-element.141), channel_id=1, source_target_pairs={{0,2},{2,0},{4,6},{6,4},{1,3},{3,1},{5,7},{7,5},{8,10},{10,8},{12,... | collective-permute-start | bytes 393224 | tf_op jit(solution)/shard_map/ppermute | solution.py:41
  202.2 12.2 %collective-permute-start.45 = (bf16[64,1024]{1,0:T(8,128)(2,1)S(1)}, bf16[64,1024]{1,0:T(8,128)(2,1)S(1)}, u32[]{:S(2)}, u32[]{:S(2)}) collective-permute-start(bf16[64,1024]{1,0:T(8,128)(2,1)S(1)} %get-tuple-element.142), channel_id=1, source_target_pairs={{0,4},{2,6},{4,0},{6,2},{1,5},{3,7},{5,1},{7,3},{8,12},{10,14},{12... | collective-permute-start | bytes 393224 | tf_op jit(solution)/shard_map/ppermute | solution.py:41
  217.9 44.6 %all-to-all-start.3 = ((bf16[8,128,640]{2,1,0:T(8,128)(2,1)}), bf16[8,128,640]{2,1,0:T(8,128)(2,1)S(1)}, u32[]{:S(2)}, u32[]{:S(2)}) async-start(bf16[8,128,640]{2,1,0:T(8,128)(2,1)} %after.13), calls=%async_computation.3 | async-start | bytes 2621440 | tf_op jit(solution)/shard_map/all_to_all | solution.py:879
  231.5 14.1 %collective-permute-start.40 = (bf16[64,1024]{1,0:T(8,128)(2,1)S(1)}, bf16[64,1024]{1,0:T(8,128)(2,1)S(1)}, u32[]{:S(2)}, u32[]{:S(2)}) collective-permute-start(bf16[64,1024]{1,0:T(8,128)(2,1)S(1)} %get-tuple-element.137), channel_id=1, source_target_pairs={{0,2},{2,0},{4,6},{6,4},{1,3},{3,1},{5,7},{7,5},{8,10},{10,8},{12,... | collective-permute-start | bytes 393224 | tf_op jit(solution)/shard_map/ppermute | solution.py:41
  233.0 12.6 %collective-permute-start.41 = (bf16[64,1024]{1,0:T(8,128)(2,1)S(1)}, bf16[64,1024]{1,0:T(8,128)(2,1)S(1)}, u32[]{:S(2)}, u32[]{:S(2)}) collective-permute-start(bf16[64,1024]{1,0:T(8,128)(2,1)S(1)} %get-tuple-element.138), channel_id=1, source_target_pairs={{0,4},{2,6},{4,0},{6,2},{1,5},{3,7},{5,1},{7,3},{8,12},{10,14},{12... | collective-permute-start | bytes 393224 | tf_op jit(solution)/shard_map/ppermute | solution.py:41
  262.5 23.0 %all-to-all-start.4 = ((bf16[8,128,384]{2,1,0:T(8,128)(2,1)}), bf16[8,128,384]{2,1,0:T(8,128)(2,1)S(1)}, u32[]{:S(2)}, u32[]{:S(2)}) async-start(bf16[8,128,384]{2,1,0:T(8,128)(2,1)} %after.15), calls=%async_computation.4 | async-start | bytes 1572864 | tf_op jit(solution)/shard_map/all_to_all | solution.py:879
  266.4 17.8 %collective-permute-start.56 = (bf16[4,2,16,1024]{3,2,1,0:T(8,128)(2,1)S(1)}, bf16[4,2,16,1024]{3,2,1,0:T(8,128)(2,1)S(1)}, u32[]{:S(2)}, u32[]{:S(2)}) collective-permute-start(bf16[4,2,16,1024]{3,2,1,0:T(8,128)(2,1)S(1)} %get-tuple-element.150.refs_0_), channel_id=1, source_target_pairs={{0,3},{1,2},{2,1},{3,0},{4,7},{5,6},{6,5},{7,4},{8,11},{9,10},{10,... | collective-permute-start | bytes 786440 | tf_op jit(solution)/shard_map/ppermute | solution.py:41
  266.5 17.8 %collective-permute-start.55 = (bf16[4,2,16,1024]{3,2,1,0:T(8,128)(2,1)S(1)}, bf16[4,2,16,1024]{3,2,1,0:T(8,128)(2,1)S(1)}, u32[]{:S(2)}, u32[]{:S(2)}) collective-permute-start(bf16[4,2,16,1024]{3,2,1,0:T(8,128)(2,1)S(1)} %get-tuple-element.150.refs_0_), channel_id=1, source_target_pairs={{0,2},{1,3},{2,0},{3,1},{4,6},{5,7},{6,4},{7,5},{8,10},{9,11},{10,... | collective-permute-start | bytes 786440 | tf_op jit(solution)/shard_map/ppermute | solution.py:41
  267.6 16.6 %collective-permute-start.54 = (bf16[4,2,16,1024]{3,2,1,0:T(8,128)(2,1)S(1)}, bf16[4,2,16,1024]{3,2,1,0:T(8,128)(2,1)S(1)}, u32[]{:S(2)}, u32[]{:S(2)}) collective-permute-start(bf16[4,2,16,1024]{3,2,1,0:T(8,128)(2,1)S(1)} %get-tuple-element.150.refs_0_), channel_id=1, source_target_pairs={{0,1},{1,0},{2,3},{3,2},{4,5},{5,4},{6,7},{7,6},{8,9},{9,8},{10,11... | collective-permute-start | bytes 786440 | tf_op jit(solution)/shard_map/ppermute | solution.py:41
  (103 other events, 1071.4 us)
